TPU v7x, 512 devices: a whole 4x4x16 slice. The times are simulated.
512 devices in a mesh: tm: 8 (over z_hi, y), space: 64 (over x, z_lo, core).
Axes of the slice: x: 4, y: 4, z: 16 (z_hi: 2, z_lo: 8; z = z_hi * 8 + z_lo), core: 2. Of those that a mesh axis runs over, the one named last changes fastest.
Arguments:
- noisy_state: float32 [32, 2, 1024, 256], P('tm', None, 'space'), may hold values from -6 to 6
- fresh_noise: float32 [32, 2, 1024, 256], P('tm', None, 'space'), may hold values from -6 to 6
- level_index: int32 [1], replicated, may hold values from 1 to 31
- station_obs: float32 [32, 2, 8192], P('tm', None, 'space'), may hold values from -6 to 6
- obs_variance: float32 [8192], P('space'), may hold values from 0.05 to 0.5
- station_owner: int32 [8192, 1], P('space'), may hold values from 0 to 63; in each aligned block of 128 rows (0 to 127, 128 to 255, ...) at most 8 rows name the same one
- station_cell: int32 [8192], P('space'), may hold values from 0 to 4095
- conv_in: bfloat16 [3, 64, 48], replicated, may hold values from -0.5 to 0.5
- conv_mid: bfloat16 [3, 64, 192], replicated, may hold values from -0.25 to 0.25
- conv_res: bfloat16 [3, 64, 192], replicated, may hold values from -0.25 to 0.25
- conv_out: bfloat16 [3, 16, 192], replicated, may hold values from -0.25 to 0.25
- in_bias: float32 [64], replicated, may hold values from -3 to 3
- noise_embed: float32 [64], replicated, may hold values from -3 to 3
- norm_gain: float32 [64], replicated, may hold values from 0.5 to 2
Outputs:
- next_state: float32 [32, 2, 1024, 256], P('tm', None, 'space')
Inputs may be any that keep to these rules, and one draw needn't show every extreme that they name: `station_owner`: among the stations of one device (each aligned block of 128 stations) at most 8 have the same owner strip; every strip owns some station.
All inputs are finite; a program needn't handle non-finite values.
Results may differ from a plain program's by a relative error of at most 0.0023.
Values may be sent and summed in bfloat16 or wider, within the bound.
No kernel may reach another device: no remote copies, remote signals or barrier semaphores. Data moves between devices by JAX's collectives and lax.ppermute only.
A program may use at most 64 MiB of HBM per device.

v0:
```python
import jax
import jax.numpy as jnp
from jax import lax
from jax.sharding import PartitionSpec as P

WIN = 8
LEVELS = 32
STRIDE = 4
CHAN = 16


def extended_2(cells, sides, width):
    for axis, dim in sides:
        count = lax.axis_size(axis)
        head = lax.slice_in_dim(cells, 0, width, axis=dim)
        tail = lax.slice_in_dim(cells, cells.shape[dim] - width, cells.shape[dim], axis=dim)
        cells = jnp.concatenate(
            [
                lax.ppermute(tail, axis, [(i, (i + 1) % count) for i in range(count)]),
                cells,
                lax.ppermute(head, axis, [((i + 1) % count, i) for i in range(count)]),
            ],
            axis=dim,
        )
    return cells


def shifted(value, axis, steps):
    count = lax.axis_size(axis)
    first, last = (max(0, -steps), min(count, count - steps))
    return lax.ppermute(value, axis, [(source, source + steps) for source in range(first, last)])


def sent_together(arrays, axis, split_dim, concat_dim, along):
    both = jnp.concatenate(arrays, axis=along)
    result, at, done = (
        lax.all_to_all(both, axis, split_axis=split_dim, concat_axis=concat_dim, tiled=True),
        0,
        [],
    )
    for a in arrays:
        done.append(lax.slice_in_dim(result, at, at + a.shape[along], axis=along))
        at += a.shape[along]
    return tuple(done)


def scale_at(level):
    return 0.3 * jnp.exp(jnp.log(5.0) * level.astype(jnp.float32) / (LEVELS - 1))


def conv_rows(weight, padded):
    out_rows = padded.shape[2] - 2
    stacked = jnp.concatenate(
        [jnp.roll(padded, 1 - col_tap, axis=3) for col_tap in range(3)], axis=1
    )
    total = None
    for row_tap in range(3):
        product = jnp.einsum(
            "oc,ncyx->noyx",
            weight[row_tap],
            stacked[:, :, row_tap : row_tap + out_rows, :],
            preferred_element_type=jnp.float32,
        )
        total = product if total is None else total + product
    return total


def score_net(windows, conv_in, conv_mid, conv_res, conv_out, bias, norm_gain):
    source = extended_2(windows, (("space", 2),), 4)
    first = jax.nn.silu(conv_rows(conv_in, source) + bias[None, :, None, None]).astype(jnp.bfloat16)
    middle = conv_rows(conv_mid, first)
    normed = (
        middle
        * lax.rsqrt(jnp.mean(middle * middle, axis=1, keepdims=True) + 1e-05)
        * norm_gain[None, :, None, None]
    )
    second = jax.nn.silu(normed).astype(jnp.bfloat16)
    branch = jax.nn.silu(conv_rows(conv_res, second))
    margin = (first.shape[2] - branch.shape[2]) // 2
    third = (first[:, :, margin : margin + branch.shape[2]].astype(jnp.float32) + branch).astype(
        jnp.bfloat16
    )
    return conv_rows(conv_out, third)


def local(
    noisy_state,
    fresh_noise,
    level_index,
    station_obs,
    obs_variance,
    station_owner,
    station_cell,
    conv_in,
    conv_mid,
    conv_res,
    conv_out,
    in_bias,
    noise_embed,
    norm_gain,
):
    step_count, layer_count, row_count, col_count = noisy_state.shape
    noise_scale = scale_at(level_index[0])
    next_scale = scale_at(level_index[0] - 1)
    bias = in_bias + noise_embed * jnp.log(10.0 * noise_scale)
    scaled = (noisy_state / jnp.sqrt(1.0 + noise_scale * noise_scale)).astype(jnp.bfloat16)
    time_rank = lax.axis_index("tm")
    total_steps = step_count * lax.axis_size("tm")
    ahead = shifted(scaled, "tm", -1)
    behind = shifted(scaled, "tm", 1)
    extended = jnp.concatenate([behind, scaled, ahead], axis=0)
    offset = STRIDE
    window_count = (extended.shape[0] - WIN) // STRIDE + 1
    windows = jnp.stack(
        [extended[window * STRIDE : window * STRIDE + WIN] for window in range(window_count)]
    )
    windows = windows.reshape(window_count, CHAN, row_count, col_count)
    outputs = score_net(windows, conv_in, conv_mid, conv_res, conv_out, bias, norm_gain)
    starts = time_rank * step_count - offset + STRIDE * jnp.arange(window_count, dtype=jnp.int32)
    usable = ((starts >= 0) & (starts + WIN <= total_steps)).astype(jnp.float32)
    halves = (
        outputs.reshape(window_count, 2, STRIDE, layer_count, row_count, col_count)
        * usable[:, None, None, None, None, None]
    )
    blank = jnp.zeros((1, STRIDE, layer_count, row_count, col_count), jnp.float32)
    summed = jnp.concatenate([halves[:, 0], blank], axis=0) + jnp.concatenate(
        [blank, halves[:, 1]], axis=0
    )
    summed = summed.reshape(extended.shape[0], layer_count, row_count, col_count)
    own = summed[STRIDE : STRIDE + step_count]
    moment = time_rank * step_count + jnp.arange(step_count, dtype=jnp.int32)
    cover = jnp.where((moment < STRIDE) | (moment >= total_steps - STRIDE), 1.0, 2.0).astype(
        jnp.float32
    )
    estimate = noisy_state - noise_scale * (own / cover[:, None, None, None])
    space_size = lax.axis_size("space")
    station_count = station_cell.shape[0]
    capacity = 4 * station_count // space_size
    values = station_obs.reshape(step_count * layer_count, station_count)
    target = station_owner[:, 0]
    earlier = lax.broadcasted_iota(
        jnp.int32, (station_count, station_count), 0
    ) < lax.broadcasted_iota(jnp.int32, (station_count, station_count), 1)
    ranked = jnp.sum(
        jnp.where((target[:, None] == target[None, :]) & earlier, 1, 0), axis=0
    ).astype(jnp.int32)
    slot = target * capacity + ranked
    slot_count = space_size * capacity
    value_slots = jnp.zeros((values.shape[0], slot_count), jnp.float32).at[:, slot].set(values)
    spread_slots = jnp.zeros((1, slot_count), jnp.float32).at[0, slot].set(obs_variance)
    cell_slots = jnp.full((1, slot_count), -1, jnp.int32).at[0, slot].set(station_cell)
    got_values, got_spread, got_cells = (
        *sent_together((value_slots, spread_slots), "space", 1, 1, 0),
        lax.all_to_all(cell_slots, "space", split_axis=1, concat_axis=1, tiled=True),
    )
    present = got_cells[0] >= 0
    spot = jnp.maximum(got_cells[0], 0)
    flat = estimate.reshape(step_count * layer_count, row_count * col_count)
    seen = jnp.take(flat, spot, axis=1)
    misfit = jnp.where(
        present[None, :], (got_values - seen) / (got_spread + noise_scale * noise_scale), 0.0
    )
    pull = jnp.zeros_like(flat).at[:, spot].add(misfit)
    return (
        estimate
        + noise_scale * noise_scale * pull.reshape(estimate.shape)
        + next_scale * fresh_noise
    )


def solution(mesh):
    placed = (
        P("tm", None, "space", None),
        P("tm", None, "space", None),
        P(),
        P("tm", None, "space"),
        P("space"),
        P("space", None),
        P("space"),
        P(),
        P(),
        P(),
        P(),
        P(),
        P(),
        P(),
    )
    return jax.shard_map(
        local, mesh=mesh, in_specs=placed, out_specs=P("tm", None, "space", None), check_vma=False
    )
```

profile of v0, /device:TPU:24, one launch (start us, length us, event | category | flops | bytes accessed | tf_op | source)
XLA Modules:
  0.0 101.6 jit_solution(9081661608196632827)
XLA Ops:
  0.7 0.9 divide_convert_fusion
  1.7 15.4 %collective-permute-start = (bf16[4,2,16,256]{3,2,1,0:T(8,128)(2,1)S(1)}, bf16[4,2,16,256]{3,2,1,0:T(8,128)(2,1)S(1)}, u32[]{:S(2)}, u32[]{:S(2)}) collective-permute-start(bf16[4,2,16,256]{3,2,1,0:T(8,128)(2,1)S(1)} %divide_convert_fusion), channel_id=1, source_target_pairs={{0,64},{64,128},{128,192},{192,256},{256,320},{320,384},{384,448},... | collective-permute-start | bytes 196616 | tf_op jit(solution)/shard_map/ppermute | solution.py:31
  17.1 1.9 %collective-permute-start.1 = (bf16[4,2,16,256]{3,2,1,0:T(8,128)(2,1)S(1)}, bf16[4,2,16,256]{3,2,1,0:T(8,128)(2,1)S(1)}, u32[]{:S(2)}, u32[]{:S(2)}) collective-permute-start(bf16[4,2,16,256]{3,2,1,0:T(8,128)(2,1)S(1)} %divide_convert_fusion), channel_id=1, source_target_pairs={{64,0},{128,64},{192,128},{256,192},{320,256},{384,320},{448,384},... | collective-permute-start | bytes 196616 | tf_op jit(solution)/shard_map/ppermute | solution.py:31
  19.0 0.8 select_reduce_fusion
  19.8 0.7 fusion.97
  20.5 1.1 %scatter_custom_fusion = s32[512]{0:T(512)S(1)} fusion(s32[128]{0:T(128)S(1)} %fusion.97, s32[128]{0:T(128)} %param.20, s32[]{:T(128)} %constant.84.clone.1), kind=kCustom, calls=%fused_computation.126 | custom fusion | bytes 2560 | tf_op jit(solution)/shard_map/scatter | solution.py:151
  21.6 0.7 all_to_all.12
  22.3 8.5 %all-to-all-start = ((s32[1,64,8]{2,0,1:T(1,128)}), s32[1,64,8]{2,0,1:T(1,128)S(1)}, u32[]{:S(2)}, u32[]{:S(2)}) async-start(s32[1,64,8]{2,0,1:T(1,128)} %bitcast.51), calls=%async_computation | async-start | bytes 65536 | tf_op jit(solution)/shard_map/all_to_all | solution.py:154
  30.9 0.8 copy.51
  31.6 0.9 scatter_custom_fusion.1
  32.6 1.1 %scatter_custom_fusion.2 = f32[512]{0:T(512)S(1)} fusion(s32[128]{0:T(128)S(1)} %fusion.97, f32[128]{0:T(128)} %param.18, f32[]{:T(128)} %constant.33.clone.1), kind=kCustom, calls=%fused_computation.124 | custom fusion | bytes 2560 | tf_op jit(solution)/shard_map/scatter | solution.py:150
  33.9 0.8 maximum_bitcast_fusion
  34.7 0.7 multiply_add_fusion.1
  35.4 7.7 %all-to-all-done = s32[1,64,8]{2,0,1:T(1,128)S(1)} async-done(((s32[1,64,8]{2,0,1:T(1,128)}), s32[1,64,8]{2,0,1:T(1,128)S(1)}, u32[]{:S(2)}, u32[]{:S(2)}) %all-to-all-start) | async-done | bytes 2080 | tf_op jit(solution)/shard_map/all_to_all | solution.py:154
  43.2 5.4 %all-to-all-start.1 = ((f32[9,64,8]{0,2,1:T(8,128)}), f32[9,64,8]{0,2,1:T(8,128)S(1)}, u32[]{:S(2)}, u32[]{:S(2)}) async-start(f32[9,64,8]{0,2,1:T(8,128)} %maximum_bitcast_fusion), calls=%async_computation.1 | async-start | bytes 524288 | tf_op jit(solution)/shard_map/all_to_all | solution.py:37
  49.3 2.0 %collective-permute-start.2 = (bf16[2,16,4,256]{3,1,2,0:T(8,128)(2,1)S(1)}, bf16[2,16,4,256]{3,1,2,0:T(8,128)(2,1)S(1)}, u32[]{:S(2)}, u32[]{:S(2)}) collective-permute-start(bf16[2,16,4,256]{3,1,2,0:T(8,128)(2,1)S(1)} %get-tuple-element.25), channel_id=1, source_target_pairs={{0,1},{1,2},{2,3},{3,4},{4,5},{5,6},{6,7},{7,8},{8,9},{9,10},{10,1... | collective-permute-start | bytes 196616 | tf_op jit(solution)/shard_map/ppermute | solution.py:19
  51.3 12.3 %collective-permute-start.3 = (bf16[2,16,4,256]{3,1,2,0:T(8,128)(2,1)S(1)}, bf16[2,16,4,256]{3,1,2,0:T(8,128)(2,1)S(1)}, u32[]{:S(2)}, u32[]{:S(2)}) collective-permute-start(bf16[2,16,4,256]{3,1,2,0:T(8,128)(2,1)S(1)} %get-tuple-element.26), channel_id=1, source_target_pairs={{1,0},{2,1},{3,2},{4,3},{5,4},{6,5},{7,6},{8,7},{9,8},{10,9},{11,1... | collective-permute-start | bytes 196616 | tf_op jit(solution)/shard_map/ppermute | solution.py:21
  63.6 5.6 %all-to-all-done.1 = f32[9,64,8]{0,2,1:T(8,128)S(1)} async-done(((f32[9,64,8]{0,2,1:T(8,128)}), f32[9,64,8]{0,2,1:T(8,128)S(1)}, u32[]{:S(2)}, u32[]{:S(2)}) %all-to-all-start.1) | async-done | bytes 18464 | tf_op jit(solution)/shard_map/all_to_all | solution.py:37
  69.3 0.2 fusion.46
  70.0 0.6 fusion.80
  70.6 0.6 fusion.82
  71.2 1.8 %fusion.21 = bf16[2,64,22,256]{3,1,2,0:T(8,128)(2,1)S(1)} fusion(f32[2,22,256,64]{2,3,1,0:T(8,128)S(1)} %fusion.82, f32[2,22,256,64]{2,3,1,0:T(8,128)S(1)} %fusion.80, f32[64]{0:T(128)S(1)} %multiply_add_fusion.1, bf16[3,64,48]{1,2,0:T(8,128)(2,1)S(1)} %copy-done.6, bf16[2,16,24,1]{3,1,2,0:T(8,128)(2,1)S(1)} %get-tuple-element.22, ...), kind=kOutput, calls=%fused_computation.31 | convolution fusion | flops 83230720 | bytes 8794624 | tf_op jit(solution)/shard_map/oc,ncyx->noyx/dot_general | solution.py:58
  73.0 0.8 fusion.100
  73.9 0.4 fusion.99
  74.3 2.2 %maximum_maximum_fusion = bf16[2,192,22,256]{3,1,2,0:T(8,128)(2,1)S(1)} fusion(bf16[2,64,22,1]{3,1,2,0:T(8,128)(2,1)S(1)} %get-tuple-element.8, bf16[2,64,22,255]{3,1,2,0:T(8,128)(2,1)S(1)} %get-tuple-element.10, bf16[2,64,22,256]{3,1,2,0:T(8,128)(2,1)S(1)} %fusion.21, bf16[2,64,22,255]{3,1,2,0:T(8,128)(2,1)S(1)} %get-tuple-element.9, ...), kind=kLoop, calls=%fused_computation.5 | loop fusion | flops 21626880 | bytes 8650752 | tf_op jit(solution)/shard_map/concatenate | solution.py:53
  76.4 0.9 fusion
  77.3 0.8 fusion.2
  78.2 1.2 %multiply_reduce_fusion = (f32[2,20,256]{2,1,0:T(8,128)S(1)}, f32[2,20,256,64]{2,3,1,0:T(8,128)S(1)}) fusion(f32[2,20,256,64]{2,3,1,0:T(8,128)S(1)} %fusion, f32[2,20,256,64]{2,3,1,0:T(8,128)S(1)} %fusion.2, bf16[2,192,22,256]{3,1,2,0:T(8,128)(2,1)S(1)} %maximum_maximum_fusion, bf16[3,64,192]{2,1,0:T(8,128)(2,1)S(1)} %copy-done.2), kind=kOutput, calls=%fused_computation.37 | convolution fusion | flops 254269440 | bytes 11870208 | tf_op jit(solution)/shard_map/oc,ncyx->noyx/dot_general | solution.py:58
  79.4 1.1 %fusion.25 = bf16[2,64,20,256]{3,1,2,0:T(8,128)(2,1)S(1)} fusion(f32[2,20,256,64]{2,3,1,0:T(8,128)S(1)} %get-tuple-element.30, f32[64]{0:T(128)S(1)} %copy-done.5, f32[2,20,256]{2,1,0:T(8,128)S(1)} %add_rsqrt_fusion), kind=kLoop, calls=%fused_computation.39 | loop fusion | flops 4587520 | bytes 3973376 | tf_op jit(solution)/shard_map/convert_element_type | solution.py:77
  80.5 0.7 fusion.102
  81.2 0.3 fusion.101
  81.5 2.1 %maximum_maximum_fusion.1 = bf16[2,192,20,256]{3,1,2,0:T(8,128)(2,1)S(1)} fusion(bf16[2,64,20,1]{3,1,2,0:T(8,128)(2,1)S(1)} %get-tuple-element.12, bf16[2,64,20,255]{3,1,2,0:T(8,128)(2,1)S(1)} %get-tuple-element.14, bf16[2,64,20,256]{3,1,2,0:T(8,128)(2,1)S(1)} %fusion.25, bf16[2,64,20,255]{3,1,2,0:T(8,128)(2,1)S(1)} %get-tuple-element.13, ...), kind=kLoop, calls=%fused_computation.12 | loop fusion | flops 19660800 | bytes 7864320 | tf_op jit(solution)/shard_map/concatenate | solution.py:53
  83.6 0.8 fusion.6
  84.4 0.8 fusion.8
  85.2 1.3 %fusion.30 = bf16[2,64,18,256]{3,1,2,0:T(8,128)(2,1)S(1)} fusion(f32[2,18,256,64]{2,3,1,0:T(8,128)S(1)} %fusion.6, f32[2,18,256,64]{2,3,1,0:T(8,128)S(1)} %fusion.8, bf16[2,192,20,256]{3,1,2,0:T(8,128)(2,1)S(1)} %maximum_maximum_fusion.1, bf16[2,64,22,256]{3,1,2,0:T(8,128)(2,1)S(1)} %fusion.21, bf16[3,64,192]{2,1,0:T(8,128)(2,1)S(1)} %copy-done.3), kind=kOutput, calls=%fused_computation.46 | convolution fusion | flops 231800832 | bytes 10649600 | tf_op jit(solution)/shard_map/oc,ncyx->noyx/dot_general | solution.py:58
  86.5 0.6 fusion.104
  87.1 0.3 fusion.103
  87.4 2.0 %maximum_maximum_fusion.2 = bf16[2,192,18,256]{3,1,2,0:T(8,128)(2,1)S(1)} fusion(bf16[2,64,18,1]{3,1,2,0:T(8,128)(2,1)S(1)} %get-tuple-element.16, bf16[2,64,18,255]{3,1,2,0:T(8,128)(2,1)S(1)} %get-tuple-element.18, bf16[2,64,18,256]{3,1,2,0:T(8,128)(2,1)S(1)} %fusion.30, bf16[2,64,18,255]{3,1,2,0:T(8,128)(2,1)S(1)} %get-tuple-element.17, ...), kind=kLoop, calls=%fused_computation.19 | loop fusion | flops 17694720 | bytes 7077888 | tf_op jit(solution)/shard_map/concatenate | solution.py:53
  89.5 0.5 fusion.12
  90.0 0.5 fusion.14
  90.5 0.5 fusion.41
  91.1 0.3 reshape.106
  91.4 0.3 copy_multiply_fusion
  91.8 0.2 copy-done
  92.2 0.6 copy.53
  92.8 5.8 %scatter_custom_fusion.3 = f32[8,4096]{0,1:T(8,128)} fusion(s32[512]{0:T(512)S(1)} %reshape.152, f32[]{:T(128)} %constant.33.clone.1, f32[9,64,8]{0,2,1:T(8,128)S(1)} %all-to-all-done.1, f32[]{:T(128)} %constant.88.clone.1, f32[512]{0:T(512)S(1)} %add.185, pred[512]{0:T(512)(128)(4,1)S(1)} %le.24, pred[512]{0:T(512)(128)(4,1)S(1)} %ge.34, ...), kind=kCustom, calls=%fused_computation.51 | custom fusion | flops 20480 | bytes 2499072 | tf_op jit(solution)/shard_map/scatter-add | solution.py:163
  98.6 2.2 %copy.54 = f32[8,4096]{1,0:T(8,128)S(1)} copy(f32[8,4096]{0,1:T(8,128)} %scatter_custom_fusion.3) | data formatting | bytes 262144 | tf_op jit(solution)/shard_map/scatter-add | solution.py:163
  100.9 0.7 multiply_add_fusion
  (40 shorter events, 1.7 us)
Async XLA Ops:
  1.7 47.5 %collective-permute-start = (bf16[4,2,16,256]{3,2,1,0:T(8,128)(2,1)S(1)}, bf16[4,2,16,256]{3,2,1,0:T(8,128)(2,1)S(1)}, u32[]{:S(2)}, u32[]{:S(2)}) collective-permute-start(bf16[4,2,16,256]{3,2,1,0:T(8,128)(2,1)S(1)} %divide_convert_fusion), channel_id=1, source_target_pairs={{0,64},{64,128},{128,192},{192,256},{256,320},{320,384},{384,448},... | collective-permute-start | bytes 196616 | tf_op jit(solution)/shard_map/ppermute | solution.py:31
  17.1 32.1 %collective-permute-start.1 = (bf16[4,2,16,256]{3,2,1,0:T(8,128)(2,1)S(1)}, bf16[4,2,16,256]{3,2,1,0:T(8,128)(2,1)S(1)}, u32[]{:S(2)}, u32[]{:S(2)}) collective-permute-start(bf16[4,2,16,256]{3,2,1,0:T(8,128)(2,1)S(1)} %divide_convert_fusion), channel_id=1, source_target_pairs={{64,0},{128,64},{192,128},{256,192},{320,256},{384,320},{448,384},... | collective-permute-start | bytes 196616 | tf_op jit(solution)/shard_map/ppermute | solution.py:31
  22.3 20.9 %all-to-all-start = ((s32[1,64,8]{2,0,1:T(1,128)}), s32[1,64,8]{2,0,1:T(1,128)S(1)}, u32[]{:S(2)}, u32[]{:S(2)}) async-start(s32[1,64,8]{2,0,1:T(1,128)} %bitcast.51), calls=%async_computation | async-start | bytes 65536 | tf_op jit(solution)/shard_map/all_to_all | solution.py:154
  43.2 26.1 %all-to-all-start.1 = ((f32[9,64,8]{0,2,1:T(8,128)}), f32[9,64,8]{0,2,1:T(8,128)S(1)}, u32[]{:S(2)}, u32[]{:S(2)}) async-start(f32[9,64,8]{0,2,1:T(8,128)} %maximum_bitcast_fusion), calls=%async_computation.1 | async-start | bytes 524288 | tf_op jit(solution)/shard_map/all_to_all | solution.py:37
  49.1 20.8 %copy-start.6 = (bf16[3,64,48]{1,2,0:T(8,128)(2,1)S(1)}, bf16[3,64,48]{1,2,0:T(8,128)(2,1)}, u32[]{:S(2)}) copy-start(bf16[3,64,48]{1,2,0:T(8,128)(2,1)} %param.21) | copy-start | bytes 55300
  49.3 20.3 %collective-permute-start.2 = (bf16[2,16,4,256]{3,1,2,0:T(8,128)(2,1)S(1)}, bf16[2,16,4,256]{3,1,2,0:T(8,128)(2,1)S(1)}, u32[]{:S(2)}, u32[]{:S(2)}) collective-permute-start(bf16[2,16,4,256]{3,1,2,0:T(8,128)(2,1)S(1)} %get-tuple-element.25), channel_id=1, source_target_pairs={{0,1},{1,2},{2,3},{3,4},{4,5},{5,6},{6,7},{7,8},{8,9},{9,10},{10,1... | collective-permute-start | bytes 196616 | tf_op jit(solution)/shard_map/ppermute | solution.py:19
  51.3 18.3 %collective-permute-start.3 = (bf16[2,16,4,256]{3,1,2,0:T(8,128)(2,1)S(1)}, bf16[2,16,4,256]{3,1,2,0:T(8,128)(2,1)S(1)}, u32[]{:S(2)}, u32[]{:S(2)}) collective-permute-start(bf16[2,16,4,256]{3,1,2,0:T(8,128)(2,1)S(1)} %get-tuple-element.26), channel_id=1, source_target_pairs={{1,0},{2,1},{3,2},{4,3},{5,4},{6,5},{7,6},{8,7},{9,8},{10,9},{11,1... | collective-permute-start | bytes 196616 | tf_op jit(solution)/shard_map/ppermute | solution.py:21
  74.2 2.2 %copy-start.2 = (bf16[3,64,192]{2,1,0:T(8,128)(2,1)S(1)}, bf16[3,64,192]{2,1,0:T(8,128)(2,1)}, u32[]{:S(2)}) copy-start(bf16[3,64,192]{2,1,0:T(8,128)(2,1)} %param.22) | copy-start | bytes 221188
  78.1 1.2 %copy-start.5 = (f32[64]{0:T(128)S(1)}, f32[64]{0:T(128)}, u32[]{:S(2)}) copy-start(f32[64]{0:T(128)} %param.27) | copy-start | bytes 772
  81.5 2.1 %copy-start.3 = (bf16[3,64,192]{2,1,0:T(8,128)(2,1)S(1)}, bf16[3,64,192]{2,1,0:T(8,128)(2,1)}, u32[]{:S(2)}) copy-start(bf16[3,64,192]{2,1,0:T(8,128)(2,1)} %param.23) | copy-start | bytes 221188
  87.4 2.1 %copy-start.4 = (bf16[3,16,192]{2,1,0:T(8,128)(2,1)S(1)}, bf16[3,16,192]{2,1,0:T(8,128)(2,1)}, u32[]{:S(2)}) copy-start(bf16[3,16,192]{2,1,0:T(8,128)(2,1)} %param.24) | copy-start | bytes 55300
  91.1 0.9 copy-start
  98.6 2.3 %copy-start.1 = (f32[4,2,16,256]{3,2,1,0:T(8,128)S(1)}, f32[4,2,16,256]{3,2,1,0:T(8,128)}, u32[]{:S(2)}) copy-start(f32[4,2,16,256]{3,2,1,0:T(8,128)} %param.15) | copy-start | bytes 393220
where the time goes:
time: 103 us; the launch traced here: 102 us
  starting transfers between devices  45.4 us (44%)
  other arithmetic  18.9 us (18%)
  waiting for transfers between devices  13.4 us (13%)
  local copies, waits for them, and re-layouts  12.2 us (12%)
  matrix products  10.3 us (10%)
  between operations  1.32 us (1%)
    ppermute x2, starting transfers between devices, shifted(): lax.ppermute(value, axis, [(source, source + steps) for source in range(f...  17.3 us
    ppermute x1, starting transfers between devices, extended_2(): lax.ppermute(head, axis, [((i + 1) % count, i) for i in range(count)])  12.3 us
    dot_general x12, matrix products, conv_rows(): jnp.einsum('oc,ncyx->noyx', weight[row_tap], stacked[:, :, row_tap:row_ta...  10.3 us
    all_to_all x1, starting transfers between devices, local(): lax.all_to_all(cell_slots, 'space', split_axis=1, concat_axis=1, tiled=True)  8.49 us
    all_to_all x1, waiting for transfers between devices, local(): lax.all_to_all(cell_slots, 'space', split_axis=1, concat_axis=1, tiled=True)  7.73 us
    concatenate x3, other arithmetic, conv_rows(): jnp.concatenate([jnp.roll(padded, 1 - col_tap, axis=3) for col_tap in ran...  6.28 us
    scatter-add x1, other arithmetic, local(): pull = jnp.zeros_like(flat).at[:, spot].add(misfit)  5.81 us
    all_to_all x1, waiting for transfers between devices, sent_together(): lax.all_to_all(both, axis, split_axis=split_dim, concat_axis=concat_dim,...  5.65 us
  transfers between devices with their start and end apart: 6, of which 2 were waited for; matrix products, arithmetic and copies ran while one was open for 8% of the time, Pallas kernels for 0%

commit v1 on v0

v1 whole, which is shorter than its diff:
```python
import jax
import jax.numpy as jnp
from jax import lax
from jax.experimental import pallas as pl
from jax.experimental.pallas import tpu as pltpu
from jax.sharding import PartitionSpec as P

LEVELS = 32
BF = jnp.bfloat16
F32 = jnp.float32
GROUP = 2
OUT_GROUP = 4
VM = pl.BlockSpec(memory_space=pltpu.VMEM)
SM = pl.BlockSpec(memory_space=pltpu.SMEM)


def scale_at(level):
    return 0.3 * jnp.exp(jnp.log(5.0) * level.astype(jnp.float32) / (LEVELS - 1))


def rolled(x, k):
    return pltpu.roll(x, k % x.shape[1], 1)


def parts_of(v):
    high = v.astype(BF)
    rest = v - high.astype(F32)
    middle = rest.astype(BF)
    low = (rest - middle.astype(F32)).astype(BF)
    return high, middle, low


def silu_half(h):
    return h + h * jnp.tanh(h)


def pack_body(scal, obs, var, owner, cell, out):
    count = obs.shape[2]
    slots = out.shape[0]
    own_col = owner[...]
    row = lax.broadcasted_iota(jnp.int32, (count, count), 0)
    col = lax.broadcasted_iota(jnp.int32, (count, count), 1)
    own_row = jnp.sum(jnp.where(row == col, own_col, 0).astype(F32), axis=0, keepdims=True)
    same = (own_col.astype(F32) == own_row) & (row < col)
    rank = jnp.sum(jnp.where(same, 1.0, 0.0), axis=0, keepdims=True)
    slot = (own_row * 8.0 + rank).astype(jnp.int32)
    weight = 1.0 / (var[...] + scal[0])
    values = jnp.concatenate([obs[k] for k in range(obs.shape[0])], axis=0) * weight
    spot = cell[...]
    extra = [weight, (spot // 256).astype(F32), (spot % 256).astype(F32)]
    spare = jnp.zeros((128 - values.shape[0] - len(extra), count), F32)
    table = jnp.concatenate([values] + extra + [spare], axis=0)
    hot = jnp.where(
        lax.broadcasted_iota(jnp.int32, (slots, count), 0) == slot, 1.0, 0.0
    ).astype(BF)
    total = None
    for part in parts_of(table):
        piece = lax.dot_general(
            hot, part, (((1,), (1,)), ((), ())), preferred_element_type=F32
        )
        total = piece if total is None else total + piece
    out[...] = total


def pack(scal, obs, var, owner, cell):
    return pl.pallas_call(
        pack_body,
        out_shape=jax.ShapeDtypeStruct((512, 128), F32),
        in_specs=[SM, VM, VM, VM, VM],
        out_specs=VM,
        cost_estimate=pl.CostEstimate(flops=50_000_000, bytes_accessed=400_000, transcendentals=0),
    )(scal, obs, var, owner, cell)


def finish_body(scal, noisy, fresh, den, got, out):
    slots = got.shape[0]
    table = got[...].T
    masks = (
        lax.broadcasted_iota(jnp.int32, (16, slots), 0) == table[9:10].astype(jnp.int32)
    )
    cols = jnp.where(
        lax.broadcasted_iota(jnp.int32, (256, slots), 0) == table[10:11].astype(jnp.int32),
        1.0,
        0.0,
    ).astype(BF)
    left = jnp.concatenate(
        [jnp.where(masks, table[v : v + 1], 0.0) for v in range(9)], axis=0
    )
    total = None
    for part in parts_of(left):
        piece = lax.dot_general(
            part, cols, (((1,), (1,)), ((), ())), preferred_element_type=F32
        )
        total = piece if total is None else total + piece
    square, after, scale = scal[0], scal[1], scal[2]
    weight = total[128:144]
    for v in range(8):
        estimate = noisy[v] - scale * den[v]
        pull = total[v * 16 : (v + 1) * 16] - estimate * weight
        out[v] = estimate + square * pull + after * fresh[v]


def finish(scal, noisy, fresh, den, got):
    return pl.pallas_call(
        finish_body,
        out_shape=jax.ShapeDtypeStruct((8, 16, 256), F32),
        in_specs=[SM, VM, VM, VM, VM],
        out_specs=VM,
        cost_estimate=pl.CostEstimate(flops=100_000_000, bytes_accessed=800_000, transcendentals=0),
    )(scal, noisy, fresh, den, got)


def conv_body(par, own, t1, t2, m1, m2, w1, wm, wr, wo, b1, gain, out, x1, x2, x3, x4):
    even_t = par[0] == 1
    even_s = par[1] == 1

    def shifts(v):
        b = v.astype(BF)
        left, right = b[:, :256], b[:, 256:]
        return (
            jnp.concatenate([rolled(left, 1), rolled(right, 1)], 1),
            b,
            jnp.concatenate([rolled(left, -1), rolled(right, -1)], 1),
        )

    def row_in(o, a, b, y):
        o, a, b = o.astype(F32), a.astype(F32), b.astype(F32)
        before = jnp.where(even_t, b, a)
        later = jnp.where(even_t, a, b)
        tap_b, tap_o, tap_l = [(rolled(z, 1), z, rolled(z, -1)) for z in (before, o, later)]
        left = jnp.concatenate([z for k in range(3) for z in (tap_b[k], tap_o[k])], 0)
        right = jnp.concatenate([z for k in range(3) for z in (tap_o[k], tap_l[k])], 0)
        x1[y * 48 : (y + 1) * 48, :256] = left.astype(BF)
        x1[y * 48 : (y + 1) * 48, 256:] = right.astype(BF)

    for y in range(16):
        row_in(own[y], t1[y], t2[y], 4 + y)
    for y in range(4):
        u, v = m1[y].astype(F32), m2[y].astype(F32)
        top = jnp.where(even_s, v, u)
        low = jnp.where(even_s, u, v)
        row_in(top[:8], top[8:16], top[16:], y)
        row_in(low[:8], low[8:16], low[16:], 20 + y)

    for g in range(8):
        y0 = min(3 * g, 19)
        acc = jnp.dot(w1[...], x1[y0 * 48 : y0 * 48 + 240, :], preferred_element_type=F32)
        for r in range(3 * g - y0, 3):
            taps = shifts(silu_half(acc[r * 64 : (r + 1) * 64] + b1[...]))
            for k in range(3):
                at = (y0 + r) * 192 + k * 64
                x2[at : at + 64, :] = taps[k]

    for g in range(20 // GROUP):
        y0 = g * GROUP
        acc = jnp.dot(
            wm[...], x2[y0 * 192 : (y0 + GROUP + 2) * 192, :], preferred_element_type=F32
        )
        for r in range(GROUP):
            m = acc[r * 64 : (r + 1) * 64]
            mean = jnp.sum(m * m, axis=0, keepdims=True) * (1 / 64)
            taps = shifts(silu_half(m * lax.rsqrt(mean + 1e-05) * gain[...]))
            for k in range(3):
                at = (y0 + r) * 192 + k * 64
                x3[at : at + 64, :] = taps[k]

    for g in range(18 // GROUP):
        y0 = g * GROUP
        acc = jnp.dot(
            wr[...], x3[y0 * 192 : (y0 + GROUP + 2) * 192, :], preferred_element_type=F32
        )
        for r in range(GROUP):
            y = y0 + r
            f = x2[(y + 2) * 192 + 64 : (y + 2) * 192 + 128, :].astype(F32)
            third = (f + silu_half(acc[r * 64 : (r + 1) * 64])).astype(BF)
            x4[y * 128 : y * 128 + 64, :] = third[:, :256]
            x4[y * 128 + 64 : y * 128 + 128, :] = third[:, 256:]

    size = OUT_GROUP * 8
    for g in range(16 // OUT_GROUP):
        y0 = g * OUT_GROUP
        acc = jnp.dot(
            wo[...], x4[y0 * 128 : (y0 + OUT_GROUP + 2) * 128, :], preferred_element_type=F32
        )
        res = rolled(acc[:size], 1) + acc[size : 2 * size] + rolled(acc[2 * size :], -1)
        for r in range(OUT_GROUP):
            out[:, y0 + r, :] = res[r * 8 : (r + 1) * 8]


def convs(par, own, t1, t2, m1, m2, w1, wm, wr, wo, b1, gain):
    return pl.pallas_call(
        conv_body,
        out_shape=jax.ShapeDtypeStruct((8, 16, 256), F32),
        in_specs=[SM] + [VM] * 11,
        out_specs=VM,
        scratch_shapes=[
            pltpu.VMEM((24 * 48, 512), BF),
            pltpu.VMEM((22 * 192, 512), BF),
            pltpu.VMEM((20 * 192, 512), BF),
            pltpu.VMEM((18 * 128, 256), BF),
        ],
        compiler_params=pltpu.CompilerParams(vmem_limit_bytes=40 * 2**20),
        cost_estimate=pl.CostEstimate(
            flops=8_000_000_000, bytes_accessed=1_000_000, transcendentals=2_000_000
        ),
    )(par, own, t1, t2, m1, m2, w1, wm, wr, wo, b1, gain)


def banded(weight, rows, factor):
    taps, outs, depth = weight.shape
    flat = (weight.astype(F32) * factor).astype(BF).transpose(1, 0, 2).reshape(outs, taps * depth)
    return jnp.concatenate(
        [jnp.pad(flat, ((0, 0), (r * depth, (rows - 1 - r) * depth))) for r in range(rows)], 0
    )


def banded_out(conv_out, coef):
    w = conv_out.reshape(3, 2, 8, 3, 64)
    w = jnp.stack([w[:, 1], w[:, 0]], 0).astype(F32) * coef[:, None, None, None, None]
    w = w.astype(BF).transpose(3, 2, 1, 0, 4).reshape(3, 8, 3 * 128)
    last = OUT_GROUP - 1
    return jnp.concatenate(
        [
            jnp.pad(w[b], ((0, 0), (r * 128, (last - r) * 128)))
            for b in range(3)
            for r in range(OUT_GROUP)
        ],
        0,
    )


def swapped(value, axis, first):
    count = lax.axis_size(axis)
    wrap = axis == "space"
    pairs = []
    for i in range(first, count if wrap else count - 1, 2):
        j = (i + 1) % count
        pairs += [(i, j), (j, i)]
    return lax.ppermute(value, axis, pairs)


def local(
    noisy_state,
    fresh_noise,
    level_index,
    station_obs,
    obs_variance,
    station_owner,
    station_cell,
    conv_in,
    conv_mid,
    conv_res,
    conv_out,
    in_bias,
    noise_embed,
    norm_gain,
):
    noise_scale = scale_at(level_index[0])
    next_scale = scale_at(level_index[0] - 1)
    bias = in_bias + noise_embed * jnp.log(10.0 * noise_scale)
    scal = jnp.stack([noise_scale * noise_scale, next_scale, noise_scale])
    time_rank = lax.axis_index("tm")
    times = lax.axis_size("tm")
    strip = lax.axis_index("space")
    even_t = time_rank % 2 == 0
    even_s = strip % 2 == 0
    par = jnp.stack([even_t, even_s]).astype(jnp.int32)

    noisy = noisy_state.reshape(8, 16, 256)
    own = (noisy / jnp.sqrt(1.0 + noise_scale * noise_scale)).astype(BF).transpose(1, 0, 2)
    t2 = swapped(own, "tm", 1)
    t1 = swapped(own, "tm", 0)

    slots = pack(
        scal,
        station_obs,
        obs_variance.reshape(1, 128),
        station_owner,
        station_cell.reshape(1, 128),
    )
    got = lax.all_to_all(slots.reshape(64, 8, 128), "space", 0, 0, tiled=True).reshape(512, 128)

    edge = jnp.where(even_s, 12, 0)
    both = jnp.concatenate([own, t1, t2], axis=1)
    m2 = swapped(lax.dynamic_slice_in_dim(both, 12 - edge, 4, 0), "space", 1)
    m1 = swapped(lax.dynamic_slice_in_dim(both, edge, 4, 0), "space", 0)

    coef = jnp.stack(
        [
            jnp.where(time_rank == 0, 0.0, jnp.where(time_rank == times - 1, 1.0, 0.5)),
            jnp.where(time_rank == 0, 1.0, jnp.where(time_rank == times - 1, 0.0, 0.5)),
        ]
    )
    den = convs(
        par,
        own,
        t1,
        t2,
        m1,
        m2,
        banded(conv_in, 3, 0.5),
        banded(conv_mid, GROUP, 1.0),
        banded(conv_res, GROUP, 0.5),
        banded_out(conv_out, coef),
        (0.5 * bias)[:, None],
        (0.5 * norm_gain)[:, None],
    )
    result = finish(scal, noisy, fresh_noise.reshape(8, 16, 256), den, got)
    return result.reshape(noisy_state.shape)


def solution(mesh):
    rest = (P(),) * 7
    placed = (
        P("tm", None, "space", None),
        P("tm", None, "space", None),
        P(),
        P("tm", None, "space"),
        P("space"),
        P("space", None),
        P("space"),
    ) + rest
    return jax.shard_map(
        local, mesh=mesh, in_specs=placed, out_specs=P("tm", None, "space", None), check_vma=False
    )
```

time: 103 us -> 64.7 us (0.63)
  other arithmetic: 18.9 us -> 2.02 us
  waiting for transfers between devices: 13.4 us -> 1.5 us
  matrix products: 10.3 us -> 0 us
  Pallas kernels: 0 us -> 9.46 us
  local copies, waits for them, and re-layouts: 12.2 us -> 8.11 us
  starting transfers between devices: 45.4 us -> 41.9 us
    all_to_all x2 -> x1, waiting for transfers between devices: 13.4 us -> 0.01 us  [local(): lax.all_to_all(slots.reshape(64, 8, 128), 'space', 0, 0, tiled=True)]
    dot_general x12 -> x0, matrix products: 10.3 us -> none  [conv_rows(): jnp.einsum('oc,ncyx->noyx', weight[row_tap], stacked[:, :, row_tap:row_ta...]
    pallas_call x0 -> x3, Pallas kernels: none -> 9.46 us  [the longest x1 5.15 us: convs(): pl.pallas_call(conv_body, out_shape=jax.ShapeDtypeStruct((8, 16, 256), F3...]
    concatenate x6 -> x3, other arithmetic: 7.02 us -> 0.23 us  [the longest x2 0.21 us: banded(): jnp.concatenate([jnp.pad(flat, ((0, 0), (r * depth, (rows - 1 - r) * dept...]
    unnamed x17 -> x32, local copies, waits for them, and re-layouts: 0.44 us -> 6.82 us
    scatter-add x1 -> x0, other arithmetic: 5.81 us -> none  [local(): pull = jnp.zeros_like(flat).at[:, spot].add(misfit)]
    all_to_all x2 -> x1, starting transfers between devices: 13.8 us -> 8.49 us  [local(): lax.all_to_all(slots.reshape(64, 8, 128), 'space', 0, 0, tiled=True)]
    slice x9 -> x5, local copies, waits for them, and re-layouts: 3.45 us -> 0.06 us  [the longest x4 0.04 us: banded_out(): w[b]]
  transfers between devices with their start and end apart: 6 -> 5, of which waited for: 2 -> 1; matrix products, arithmetic and copies ran while one was open for 8% -> 5% of each run, Pallas kernels for 0% -> 11%
where the time goes in v1:
time: 64.7 us; the launch traced here: 64.1 us
  starting transfers between devices  41.9 us (65%)
  Pallas kernels  9.46 us (15%)
  local copies, waits for them, and re-layouts  8.11 us (13%)
  other arithmetic  2.02 us (3%)
  waiting for transfers between devices  1.5 us (2%)
  between operations  1.18 us (2%)
    ppermute x4, starting transfers between devices, swapped(): return lax.ppermute(value, axis, pairs)  33.4 us
    all_to_all x1, starting transfers between devices, local(): lax.all_to_all(slots.reshape(64, 8, 128), 'space', 0, 0, tiled=True)  8.49 us
    unnamed x32, local copies, waits for them, and re-layouts  6.82 us
    pallas_call x1, Pallas kernels, convs(): pl.pallas_call(conv_body, out_shape=jax.ShapeDtypeStruct((8, 16, 256), F3...  5.15 us
    pallas_call x1, Pallas kernels, finish(): pl.pallas_call(finish_body, out_shape=jax.ShapeDtypeStruct((8, 16, 256),...  2.37 us
    pallas_call x1, Pallas kernels, pack(): pl.pallas_call(pack_body, out_shape=jax.ShapeDtypeStruct((512, 128), F32)...  1.95 us
    ppermute x4, waiting for transfers between devices, swapped(): return lax.ppermute(value, axis, pairs)  1.49 us
  transfers between devices with their start and end apart: 5, of which 1 were waited for; matrix products, arithmetic and copies ran while one was open for 5% of the time, Pallas kernels for 11%

profile of v1, /device:TPU:24, one launch (start us, length us, event | category | flops | bytes accessed | tf_op | source)
XLA Modules:
  0.0 64.1 jit_solution(3831899411183072685)
XLA Ops:
  0.7 0.9 %fusion.13 = bf16[16,8,256]{2,0,1:T(8,128)(2,1)S(1)} fusion(f32[]{:T(128)} %bitcast.4, f32[4,2,16,256]{3,2,1,0:T(8,128)} %param.14), kind=kLoop, calls=%fused_computation.24 | loop fusion | flops 65536 | bytes 196612 | tf_op jit(solution)/shard_map/transpose | solution.py:270
  1.7 2.7 %collective-permute-start = (bf16[16,8,256]{2,0,1:T(8,128)(2,1)S(1)}, bf16[16,8,256]{2,0,1:T(8,128)(2,1)S(1)}, u32[]{:S(2)}, u32[]{:S(2)}) collective-permute-start(bf16[16,8,256]{2,0,1:T(8,128)(2,1)S(1)} %fusion.13), channel_id=1, source_target_pairs={{0,64},{64,0},{128,192},{192,128},{256,320},{320,256},{384,448},{4... | collective-permute-start | bytes 196616 | tf_op jit(solution)/shard_map/ppermute | solution.py:239
  4.3 16.2 %collective-permute-start.1 = (bf16[16,8,256]{2,0,1:T(8,128)(2,1)S(1)}, bf16[16,8,256]{2,0,1:T(8,128)(2,1)S(1)}, u32[]{:S(2)}, u32[]{:S(2)}) collective-permute-start(bf16[16,8,256]{2,0,1:T(8,128)(2,1)S(1)} %fusion.13), channel_id=1, source_target_pairs={{64,128},{128,64},{192,256},{256,192},{320,384},{384,320},{65,129}... | collective-permute-start | bytes 196616 | tf_op jit(solution)/shard_map/ppermute | solution.py:239
  20.6 0.0 copy-start.6
  20.6 0.6 %copy-done.6 = s32[128,1]{0,1:T(1,128)S(1)} copy-done((s32[128,1]{0,1:T(1,128)S(1)}, s32[128,1]{0,1:T(1,128)}, u32[]{:S(2)}) %copy-start.6) | copy-done | bytes 536
  21.3 0.7 %copy.45.owner = s32[128,1]{1,0:T(8,128)} copy(s32[128,1]{0,1:T(1,128)S(1)} %copy-done.6) | data formatting | bytes 1024 | tf_op args[5]
  22.0 0.6 pad_maximum_fusion.1.scal
  22.6 1.9 %shard_map.137 = f32[512,128]{1,0:T(8,128)} custom-call(f32[3]{0:T(128)} %pad_maximum_fusion.1.scal, f32[4,2,128]{2,1,0:T(2,128)} %obs.1, f32[1,128]{1,0:T(1,128)} %bitcast.38, s32[128,1]{1,0:T(8,128)} %copy.45.owner, s32[1,128]{1,0:T(1,128)} %bitcast.39), custom_call_target="tpu_custom_call" | custom-call | flops 50000000 | bytes 400000 | tf_op jit(solution)/shard_map/pallas_call | solution.py:66
  24.5 8.5 %all-to-all-start = ((f32[64,8,128]{2,1,0:T(8,128)}), f32[64,8,128]{2,1,0:T(8,128)S(1)}, u32[]{:S(2)}, u32[]{:S(2)}) async-start(f32[64,8,128]{2,1,0:T(8,128)} %bitcast.32), calls=%async_computation | async-start | bytes 524288 | tf_op jit(solution)/shard_map/all_to_all | solution.py:281
  33.0 0.0 copy-start.4
  33.1 0.7 %copy-done.4 = bf16[3,64,48]{1,2,0:T(8,128)(2,1)S(1)} copy-done((bf16[3,64,48]{1,2,0:T(8,128)(2,1)S(1)}, bf16[3,64,48]{1,2,0:T(8,128)(2,1)}, u32[]{:S(2)}) %copy-start.4) | copy-done | bytes 18456
  33.8 0.0 copy-start.2
  33.8 0.1 copy.28
  33.9 0.1 fusion.11.w1
  34.0 0.7 %copy-done.2 = bf16[3,64,192]{2,1,0:T(8,128)(2,1)S(1)} copy-done((bf16[3,64,192]{2,1,0:T(8,128)(2,1)S(1)}, bf16[3,64,192]{2,1,0:T(8,128)(2,1)}, u32[]{:S(2)}) %copy-start.2) | copy-done | bytes 73752
  34.7 0.1 copy.31
  34.8 0.0 copy-start.3
  34.8 0.1 reshape.60
  35.0 0.8 %copy-done.3 = bf16[3,64,192]{2,1,0:T(8,128)(2,1)S(1)} copy-done((bf16[3,64,192]{2,1,0:T(8,128)(2,1)S(1)}, bf16[3,64,192]{2,1,0:T(8,128)(2,1)}, u32[]{:S(2)}) %copy-start.3) | copy-done | bytes 73752
  35.7 0.1 copy.32
  35.8 0.0 copy-start.5
  35.8 0.1 reshape.61
  36.0 0.6 copy-done.5
  36.6 0.1 reshape.62
  36.7 0.1 pad_maximum_fusion.2
  36.8 0.1 fusion.14
  36.9 0.1 squeeze.6
  37.0 0.1 squeeze.7
  37.2 0.1 squeeze.8
  37.3 0.0 copy-start.9
  37.3 0.6 copy-done.9
  37.9 0.1 fusion.4
  38.1 0.0 copy-start.7
  38.1 0.0 copy-start.8
  38.1 0.6 copy-done.7
  38.7 0.0 copy-done.8
  38.7 0.0 collective-permute-done
  38.8 0.1 constant_dynamic-slice_fusion
  38.9 2.0 %collective-permute-start.2 = (bf16[4,24,256]{2,0,1:T(4,128)(2,1)S(1)}, bf16[4,24,256]{2,0,1:T(4,128)(2,1)S(1)}, u32[]{:S(2)}, u32[]{:S(2)}) collective-permute-start(bf16[4,24,256]{2,0,1:T(4,128)(2,1)S(1)} %get-tuple-element.6), channel_id=1, source_target_pairs={{0,1},{1,0},{2,3},{3,2},{4,5},{5,4},{6,7},{7,6},{8,9},{9,8},{10,11... | collective-permute-start | bytes 147464 | tf_op jit(solution)/shard_map/ppermute | solution.py:239
  40.8 12.6 %collective-permute-start.3 = (bf16[4,24,256]{2,0,1:T(4,128)(2,1)S(1)}, bf16[4,24,256]{2,0,1:T(4,128)(2,1)S(1)}, u32[]{:S(2)}, u32[]{:S(2)}) collective-permute-start(bf16[4,24,256]{2,0,1:T(4,128)(2,1)S(1)} %get-tuple-element.5), channel_id=1, source_target_pairs={{1,2},{2,1},{3,4},{4,3},{5,6},{6,5},{7,8},{8,7},{9,10},{10,9},{11,... | collective-permute-start | bytes 147464 | tf_op jit(solution)/shard_map/ppermute | solution.py:239
  53.4 0.1 add_convert_fusion.par
  53.5 0.1 copy.43.b1
  53.6 0.1 copy.44.gain
  53.8 1.5 %collective-permute-done.3 = bf16[4,24,256]{2,0,1:T(4,128)(2,1)S(1)} collective-permute-done((bf16[4,24,256]{2,0,1:T(4,128)(2,1)S(1)}, bf16[4,24,256]{2,0,1:T(4,128)(2,1)S(1)}, u32[]{:S(2)}, u32[]{:S(2)}) %collective-permute-start.3) | collective-permute-done | bytes 49184 | tf_op jit(solution)/shard_map/ppermute | solution.py:239
  55.3 5.1 %shard_map.136.den = f32[8,16,256]{2,1,0:T(8,128)S(1)} custom-call(s32[2]{0:T(128)S(1)} %add_convert_fusion.par, bf16[16,8,256]{2,1,0:T(8,128)(2,1)S(1)} %copy.38.own, bf16[16,8,256]{2,1,0:T(8,128)(2,1)S(1)} %copy.39.t1, bf16[16,8,256]{2,1,0:T(8,128)(2,1)S(1)} %copy.40.t2, bf16[4,24,256]{2,1,0:T(8,128)(2,1)S(1)} %copy.41.m1, ...), custom_call_target="tpu_custom_call" | custom-call | flops 8000000000 | bytes 1000000 | tf_op jit(solution)/shard_map/pallas_call | solution.py:191
  60.4 0.6 copy-done
  61.1 0.7 %copy-done.1 = f32[64,8,128]{2,1,0:T(8,128)} copy-done((f32[64,8,128]{2,1,0:T(8,128)}, f32[64,8,128]{2,1,0:T(8,128)S(1)}, u32[]{:S(2)}) %copy-start.1) | copy-done | bytes 262168
  61.8 2.4 %shard_map.138 = f32[8,16,256]{2,1,0:T(8,128)} custom-call(f32[3]{0:T(128)} %pad_maximum_fusion.1.scal, f32[8,16,256]{2,1,0:T(8,128)} %bitcast.34, f32[8,16,256]{2,1,0:T(8,128)} %bitcast.36, f32[8,16,256]{2,1,0:T(8,128)} %copy-done, f32[512,128]{1,0:T(8,128)} %bitcast.33), custom_call_target="tpu_custom_call" | custom-call | flops 100000000 | bytes 800000 | tf_op jit(solution)/shard_map/pallas_call | solution.py:104
  (33 shorter events, 0.3 us)
Async XLA Ops:
  1.7 37.1 %collective-permute-start = (bf16[16,8,256]{2,0,1:T(8,128)(2,1)S(1)}, bf16[16,8,256]{2,0,1:T(8,128)(2,1)S(1)}, u32[]{:S(2)}, u32[]{:S(2)}) collective-permute-start(bf16[16,8,256]{2,0,1:T(8,128)(2,1)S(1)} %fusion.13), channel_id=1, source_target_pairs={{0,64},{64,0},{128,192},{192,128},{256,320},{320,256},{384,448},{4... | collective-permute-start | bytes 196616 | tf_op jit(solution)/shard_map/ppermute | solution.py:239
  4.3 34.4 %collective-permute-start.1 = (bf16[16,8,256]{2,0,1:T(8,128)(2,1)S(1)}, bf16[16,8,256]{2,0,1:T(8,128)(2,1)S(1)}, u32[]{:S(2)}, u32[]{:S(2)}) collective-permute-start(bf16[16,8,256]{2,0,1:T(8,128)(2,1)S(1)} %fusion.13), channel_id=1, source_target_pairs={{64,128},{128,64},{192,256},{256,192},{320,384},{384,320},{65,129}... | collective-permute-start | bytes 196616 | tf_op jit(solution)/shard_map/ppermute | solution.py:239
  20.6 0.7 %copy-start.6 = (s32[128,1]{0,1:T(1,128)S(1)}, s32[128,1]{0,1:T(1,128)}, u32[]{:S(2)}) copy-start(s32[128,1]{0,1:T(1,128)} %param.19) | copy-start | bytes 1540
  24.5 36.5 %all-to-all-start = ((f32[64,8,128]{2,1,0:T(8,128)}), f32[64,8,128]{2,1,0:T(8,128)S(1)}, u32[]{:S(2)}, u32[]{:S(2)}) async-start(f32[64,8,128]{2,1,0:T(8,128)} %bitcast.32), calls=%async_computation | async-start | bytes 524288 | tf_op jit(solution)/shard_map/all_to_all | solution.py:281
  33.0 0.8 %copy-start.4 = (bf16[3,64,48]{1,2,0:T(8,128)(2,1)S(1)}, bf16[3,64,48]{1,2,0:T(8,128)(2,1)}, u32[]{:S(2)}) copy-start(bf16[3,64,48]{1,2,0:T(8,128)(2,1)} %param.21) | copy-start | bytes 55300
  33.8 0.9 %copy-start.2 = (bf16[3,64,192]{2,1,0:T(8,128)(2,1)S(1)}, bf16[3,64,192]{2,1,0:T(8,128)(2,1)}, u32[]{:S(2)}) copy-start(bf16[3,64,192]{2,1,0:T(8,128)(2,1)} %param.22) | copy-start | bytes 221188
  34.8 0.9 %copy-start.3 = (bf16[3,64,192]{2,1,0:T(8,128)(2,1)S(1)}, bf16[3,64,192]{2,1,0:T(8,128)(2,1)}, u32[]{:S(2)}) copy-start(bf16[3,64,192]{2,1,0:T(8,128)(2,1)} %param.23) | copy-start | bytes 221188
  35.8 0.7 %copy-start.5 = (bf16[3,16,192]{2,1,0:T(8,128)(2,1)S(1)}, bf16[3,16,192]{2,1,0:T(8,128)(2,1)}, u32[]{:S(2)}) copy-start(bf16[3,16,192]{2,1,0:T(8,128)(2,1)} %param.24) | copy-start | bytes 55300
  37.3 0.7 %copy-start.9 = (f32[64]{0:T(128)S(1)}, f32[64]{0:T(128)}, u32[]{:S(2)}) copy-start(f32[64]{0:T(128)} %param.27) | copy-start | bytes 772
  38.1 0.7 %copy-start.7 = (f32[64]{0:T(128)S(1)}, f32[64]{0:T(128)}, u32[]{:S(2)}) copy-start(f32[64]{0:T(128)} %param.25) | copy-start | bytes 772
  38.1 0.7 %copy-start.8 = (f32[64]{0:T(128)S(1)}, f32[64]{0:T(128)}, u32[]{:S(2)}) copy-start(f32[64]{0:T(128)} %param.26) | copy-start | bytes 772
  38.9 14.9 %collective-permute-start.2 = (bf16[4,24,256]{2,0,1:T(4,128)(2,1)S(1)}, bf16[4,24,256]{2,0,1:T(4,128)(2,1)S(1)}, u32[]{:S(2)}, u32[]{:S(2)}) collective-permute-start(bf16[4,24,256]{2,0,1:T(4,128)(2,1)S(1)} %get-tuple-element.6), channel_id=1, source_target_pairs={{0,1},{1,0},{2,3},{3,2},{4,5},{5,4},{6,7},{7,6},{8,9},{9,8},{10,11... | collective-permute-start | bytes 147464 | tf_op jit(solution)/shard_map/ppermute | solution.py:239
  40.8 14.4 %collective-permute-start.3 = (bf16[4,24,256]{2,0,1:T(4,128)(2,1)S(1)}, bf16[4,24,256]{2,0,1:T(4,128)(2,1)S(1)}, u32[]{:S(2)}, u32[]{:S(2)}) collective-permute-start(bf16[4,24,256]{2,0,1:T(4,128)(2,1)S(1)} %get-tuple-element.5), channel_id=1, source_target_pairs={{1,2},{2,1},{3,4},{4,3},{5,6},{6,5},{7,8},{8,7},{9,10},{10,9},{11,... | collective-permute-start | bytes 147464 | tf_op jit(solution)/shard_map/ppermute | solution.py:239
  60.4 0.6 %copy-start = (f32[8,16,256]{2,1,0:T(8,128)}, f32[8,16,256]{2,1,0:T(8,128)S(1)}, u32[]{:S(2)}) copy-start(f32[8,16,256]{2,1,0:T(8,128)S(1)} %shard_map.136.den) | copy-start | bytes 393220
  61.1 0.7 %copy-start.1 = (f32[64,8,128]{2,1,0:T(8,128)}, f32[64,8,128]{2,1,0:T(8,128)S(1)}, u32[]{:S(2)}) copy-start(f32[64,8,128]{2,1,0:T(8,128)S(1)} %all-to-all-done) | copy-start | bytes 786436

commit v2 on v1

v2 whole, which is shorter than its diff:
```python
import math

import jax
import jax.numpy as jnp
from jax import lax
from jax.experimental import pallas as pl
from jax.experimental.pallas import tpu as pltpu
from jax.sharding import PartitionSpec as P

LEVELS = 32
BF = jnp.bfloat16
F32 = jnp.float32
OUT_GROUP = 4
INNER_COST = 8_000_000_000
VM = pl.BlockSpec(memory_space=pltpu.VMEM)
SM = pl.BlockSpec(memory_space=pltpu.SMEM)
ANY = pl.BlockSpec(memory_space=pl.ANY)


def scale_at(level, shape):
    steps = jnp.full(shape, level, jnp.int32).astype(F32)
    return 0.3 * jnp.exp(math.log(5.0) * steps / (LEVELS - 1))


def rolled(x, k):
    return pltpu.roll(x, k % x.shape[1], 1)


def parts_of(v):
    high = v.astype(BF)
    rest = v - high.astype(F32)
    middle = rest.astype(BF)
    low = (rest - middle.astype(F32)).astype(BF)
    return high, middle, low


def silu_half(h):
    return h + h * jnp.tanh(h)


def column_of(row):
    size = row.shape[1]
    line = lax.broadcasted_iota(jnp.int32, (size, size), 0)
    lane = lax.broadcasted_iota(jnp.int32, (size, size), 1)
    return jnp.sum(jnp.where(line == lane, row, 0.0), axis=1, keepdims=True)


def pack_body(level, noisy, obs, var, owner, cell, own, out, turned):
    count = obs.shape[2]
    slots = out.shape[0]
    noise = scale_at(level[0], (16, 256))
    inverse = 1.0 / jnp.sqrt(1.0 + noise * noise)
    for v in range(8):
        turned[:, v, :] = noisy[v] * inverse
    own[...] = turned[...].astype(BF)

    own_row = owner[...].astype(F32)
    own_col = column_of(own_row)
    row = lax.broadcasted_iota(jnp.int32, (count, count), 0)
    col = lax.broadcasted_iota(jnp.int32, (count, count), 1)
    same = (own_col == own_row) & (row < col)
    rank = jnp.sum(jnp.where(same, 1.0, 0.0), axis=0, keepdims=True)
    slot = (own_row * 8.0 + rank).astype(jnp.int32)
    near = noise[:1, :count]
    weight = 1.0 / (var[...] + near * near)
    values = jnp.concatenate([obs[k] for k in range(obs.shape[0])], axis=0) * weight
    spot = cell[...]
    extra = [weight, (spot // 256).astype(F32), (spot % 256).astype(F32)]
    spare = jnp.zeros((128 - values.shape[0] - len(extra), count), F32)
    table = jnp.concatenate([values] + extra + [spare], axis=0)
    hot = jnp.where(
        lax.broadcasted_iota(jnp.int32, (slots, count), 0) == slot, 1.0, 0.0
    ).astype(BF)
    total = None
    for part in parts_of(table):
        piece = lax.dot_general(
            hot, part, (((1,), (1,)), ((), ())), preferred_element_type=F32
        )
        total = piece if total is None else total + piece
    out[...] = total


def pack(level, noisy, obs, var, owner, cell):
    return pl.pallas_call(
        pack_body,
        out_shape=(
            jax.ShapeDtypeStruct((16, 8, 256), BF),
            jax.ShapeDtypeStruct((512, 128), F32),
        ),
        in_specs=[SM, VM, VM, VM, VM, VM],
        out_specs=(VM, VM),
        scratch_shapes=[pltpu.VMEM((16, 8, 256), F32)],
        cost_estimate=pl.CostEstimate(flops=50_000_000, bytes_accessed=400_000, transcendentals=0),
    )(level, noisy, obs, var, owner, cell)


def shifts(v):
    b = v.astype(BF)
    left, right = b[:, :256], b[:, 256:]
    return (
        jnp.concatenate([rolled(left, 1), rolled(right, 1)], 1),
        b,
        jnp.concatenate([rolled(left, -1), rolled(right, -1)], 1),
    )


def store_taps(x, row, taps):
    for k in range(3):
        at = row * 192 + k * 64
        x[at : at + 64, :] = taps[k]


def row_in(x1, row, even_t, o, a, b):
    o, a, b = o.astype(F32), a.astype(F32), b.astype(F32)
    before = jnp.where(even_t, b, a)
    later = jnp.where(even_t, a, b)
    tap_b, tap_o, tap_l = [(rolled(z, 1), z, rolled(z, -1)) for z in (before, o, later)]
    left = jnp.concatenate([z for k in range(3) for z in (tap_b[k], tap_o[k])], 0)
    right = jnp.concatenate([z for k in range(3) for z in (tap_o[k], tap_l[k])], 0)
    x1[row * 48 : (row + 1) * 48, :256] = left.astype(BF)
    x1[row * 48 : (row + 1) * 48, 256:] = right.astype(BF)


def first_rows(w1, bias, x1, x2, at, new):
    acc = jnp.dot(w1, x1[at * 48 : at * 48 + 240, :], preferred_element_type=F32)
    for r in range(3 - new, 3):
        store_taps(x2, at + r, shifts(silu_half(acc[r * 64 : (r + 1) * 64] + bias)))


def summed(weight, x, at, rows, done):
    held = []
    for y in range(rows + 2):
        piece = x[(at + y) * 192 : (at + y + 1) * 192, :]
        held.append(jnp.dot(weight, piece, preferred_element_type=F32))
        if y >= 2:
            a, b, c = held[y - 2 :]
            done(y - 2, a[128:] + b[64:128] + c[:64])


def normed(m, gain):
    mean = jnp.sum(m * m, axis=0, keepdims=True) * (1 / 64)
    return silu_half(m * lax.rsqrt(mean + 1e-05) * gain)


def store_third(x4, row, f, h):
    third = (f.astype(F32) + silu_half(h)).astype(BF)
    x4[row * 128 : row * 128 + 64, :] = third[:, :256]
    x4[row * 128 + 64 : row * 128 + 128, :] = third[:, 256:]


def out_rows(wo, x4, at, den, row):
    size = OUT_GROUP * 8
    acc = jnp.dot(wo, x4[at * 128 : (at + OUT_GROUP + 2) * 128, :], preferred_element_type=F32)
    res = rolled(acc[:size], 1) + acc[size : 2 * size] + rolled(acc[2 * size :], -1)
    for r in range(OUT_GROUP):
        den[:, row + r, :] = res[r * 8 : (r + 1) * 8]


def inner_body(
    level,
    own,
    t2,
    t1,
    conv_in,
    conv_mid,
    conv_res,
    conv_out,
    in_bias,
    noise_embed,
    norm_gain,
    w1_out,
    wm_out,
    wr_out,
    wo_out,
    columns,
    first,
    second,
    x4_edge,
    den,
    x1,
    x2,
    x3,
    x4,
):
    time_rank = lax.axis_index("tm")
    times = lax.axis_size("tm")
    even_t = time_rank % 2 == 0

    noise64 = scale_at(level[0], (1, 64))
    bias_row = 0.5 * (in_bias[...] + noise_embed[...] * jnp.log(10.0 * noise64))
    bias = column_of(bias_row)
    gain = column_of(0.5 * norm_gain[...])
    columns[0] = jnp.broadcast_to(bias, (64, 128))
    columns[1] = jnp.broadcast_to(gain, (64, 128))

    taps_in = [0.5 * conv_in[a].astype(F32).T for a in range(3)]
    spare = jnp.zeros((64, 48), F32)
    w1 = jnp.concatenate(
        [
            jnp.concatenate([taps_in[j - r] if 0 <= j - r < 3 else spare for j in range(5)], 1)
            for r in range(3)
        ],
        0,
    ).astype(BF)
    wm = jnp.concatenate([conv_mid[2], conv_mid[1], conv_mid[0]], 0)
    wr = (
        0.5 * jnp.concatenate([conv_res[2], conv_res[1], conv_res[0]], 0).astype(F32)
    ).astype(BF)
    coef0 = jnp.where(time_rank == 0, 0.0, jnp.where(time_rank == times - 1, 1.0, 0.5))
    coef1 = jnp.where(time_rank == 0, 1.0, jnp.where(time_rank == times - 1, 0.0, 0.5))
    tap_out = [conv_out[a].astype(F32) for a in range(3)]
    blank = jnp.zeros((8, 128), F32)
    banded = []
    for b in range(3):
        cell = [
            jnp.concatenate(
                [
                    coef0 * tap_out[a][8:, b * 64 : (b + 1) * 64],
                    coef1 * tap_out[a][:8, b * 64 : (b + 1) * 64],
                ],
                1,
            )
            for a in range(3)
        ]
        for r in range(OUT_GROUP):
            banded.append(
                jnp.concatenate(
                    [
                        cell[j - r] if 0 <= j - r < 3 else blank
                        for j in range(OUT_GROUP + 2)
                    ],
                    1,
                )
            )
    wo = jnp.concatenate(banded, 0).astype(BF)
    w1_out[...] = w1
    wm_out[...] = wm
    wr_out[...] = wr
    wo_out[...] = wo

    for y in range(16):
        row_in(x1, y, even_t, own[y], t1[y], t2[y])
    for at, new in ((0, 3), (3, 3), (6, 3), (9, 3), (11, 2)):
        first_rows(w1, bias, x1, x2, at, new)
    summed(wm, x2, 0, 12, lambda y, m: store_taps(x3, y, shifts(normed(m, gain))))
    summed(
        wr, x3, 0, 10, lambda y, h: store_third(x4, y, x2[(y + 2) * 192 + 64 : (y + 2) * 192 + 128, :], h)
    )
    for g in range(2):
        out_rows(wo, x4, g * 4, den, g * 4)
    for k, y in enumerate((0, 1, 12, 13)):
        first[k] = x2[y * 192 + 64 : y * 192 + 128, :]
    for k, y in enumerate((0, 1, 10, 11)):
        second[k] = x3[y * 192 + 64 : y * 192 + 128, :]
    x4_edge[:256] = x4[:256]
    x4_edge[256:] = x4[8 * 128 :]


def inner(level, *arrays):
    return pl.pallas_call(
        inner_body,
        out_shape=(
            jax.ShapeDtypeStruct((192, 240), BF),
            jax.ShapeDtypeStruct((192, 192), BF),
            jax.ShapeDtypeStruct((192, 192), BF),
            jax.ShapeDtypeStruct((96, 768), BF),
            jax.ShapeDtypeStruct((2, 64, 128), F32),
            jax.ShapeDtypeStruct((4, 64, 512), BF),
            jax.ShapeDtypeStruct((4, 64, 512), BF),
            jax.ShapeDtypeStruct((512, 256), BF),
            jax.ShapeDtypeStruct((8, 8, 256), F32),
        ),
        in_specs=[SM] + [VM] * 10,
        out_specs=(VM,) * 9,
        scratch_shapes=[
            pltpu.VMEM((16 * 48, 512), BF),
            pltpu.VMEM((14 * 192, 512), BF),
            pltpu.VMEM((12 * 192, 512), BF),
            pltpu.VMEM((10 * 128, 256), BF),
        ],
        compiler_params=pltpu.CompilerParams(vmem_limit_bytes=40 * 2**20),
        cost_estimate=pl.CostEstimate(
            flops=INNER_COST, bytes_accessed=1_000_000, transcendentals=2_000_000
        ),
    )(level, *arrays)


def outer_body(
    level,
    own,
    t2,
    t1,
    edges,
    w1,
    wm,
    wr,
    wo,
    columns,
    first,
    second,
    x4_edge,
    den_inner,
    noisy_far,
    fresh_far,
    got_far,
    out,
    x1,
    x2,
    x3,
    x4,
    den,
    noisy,
    fresh,
    got,
    sems,
):
    copies = [
        pltpu.make_async_copy(far, near, sems.at[k])
        for k, (far, near) in enumerate(((noisy_far, noisy), (fresh_far, fresh), (got_far, got)))
    ]
    for copy in copies:
        copy.start()
    even_t = lax.axis_index("tm") % 2 == 0
    even_s = lax.axis_index("space") % 2 == 0
    bias = columns[0][:, :1]
    gain = columns[1][:, :1]

    for y in range(4):
        u, v = edges[4 + y].astype(F32), edges[y].astype(F32)
        top = jnp.where(even_s, v, u)
        low = jnp.where(even_s, u, v)
        row_in(x1, y, even_t, top[16:], top[8:16], top[:8])
        row_in(x1, 8 + y, even_t, low[16:], low[8:16], low[:8])
    for y, row in ((0, 4), (1, 5), (14, 6), (15, 7)):
        row_in(x1, row, even_t, own[y], t1[y], t2[y])
    for k, row in enumerate((4, 5, 6, 7)):
        store_taps(x2, row, shifts(first[k]))
        store_taps(x3, row, shifts(second[k]))
    x4[4 * 128 : 8 * 128, :] = x4_edge[...]

    acc = [
        jnp.dot(w1[...], x1[at * 48 : at * 48 + 240, :], preferred_element_type=F32)
        for at in (0, 1, 6, 7)
    ]
    for row, k, r in (
        (0, 0, 0),
        (1, 0, 1),
        (2, 0, 2),
        (3, 1, 2),
        (8, 2, 0),
        (9, 2, 1),
        (10, 2, 2),
        (11, 3, 2),
    ):
        store_taps(x2, row, shifts(silu_half(acc[k][r * 64 : (r + 1) * 64] + bias)))

    def middle(at):
        return lambda y, m: store_taps(x3, at + y, shifts(normed(m, gain)))

    def last(at, from_first):
        def done(y, h):
            row = from_first + y
            store_third(x4, at + y, x2[row * 192 + 64 : row * 192 + 128, :], h)

        return done

    summed(wm[...], x2, 0, 4, middle(0))
    summed(wm[...], x2, 6, 4, middle(8))
    summed(wr[...], x3, 0, 4, last(0, 2))
    summed(wr[...], x3, 6, 4, last(8, 6))
    out_rows(wo[...], x4, 0, den, 0)
    den[:, 4:12, :] = den_inner[...]
    out_rows(wo[...], x4, 6, den, 12)

    for copy in copies:
        copy.wait()
    slots = got.shape[0]
    table = got[...].T
    masks = (
        lax.broadcasted_iota(jnp.int32, (16, slots), 0) == table[9:10].astype(jnp.int32)
    )
    cols = jnp.where(
        lax.broadcasted_iota(jnp.int32, (256, slots), 0) == table[10:11].astype(jnp.int32),
        1.0,
        0.0,
    ).astype(BF)
    left = jnp.concatenate(
        [jnp.where(masks, table[v : v + 1], 0.0) for v in range(9)], axis=0
    )
    total = None
    for part in parts_of(left):
        piece = lax.dot_general(
            part, cols, (((1,), (1,)), ((), ())), preferred_element_type=F32
        )
        total = piece if total is None else total + piece
    scale = scale_at(level[0], (16, 256))
    after = scale_at(level[0] - 1, (16, 256))
    square = scale * scale
    weight = 1.0 - square * total[128:144]
    for v in range(8):
        estimate = noisy[v] - scale * den[v]
        out[v] = estimate * weight + square * total[v * 16 : (v + 1) * 16] + after * fresh[v]


def outer(level, *arrays):
    return pl.pallas_call(
        outer_body,
        out_shape=jax.ShapeDtypeStruct((8, 16, 256), F32),
        in_specs=[SM] + [VM] * 13 + [ANY] * 3,
        out_specs=VM,
        scratch_shapes=[
            pltpu.VMEM((12 * 48, 512), BF),
            pltpu.VMEM((12 * 192, 512), BF),
            pltpu.VMEM((12 * 192, 512), BF),
            pltpu.VMEM((12 * 128, 256), BF),
            pltpu.VMEM((8, 16, 256), F32),
            pltpu.VMEM((8, 16, 256), F32),
            pltpu.VMEM((8, 16, 256), F32),
            pltpu.VMEM((512, 128), F32),
            pltpu.SemaphoreType.DMA((3,)),
        ],
        compiler_params=pltpu.CompilerParams(vmem_limit_bytes=40 * 2**20),
        cost_estimate=pl.CostEstimate(
            flops=4_000_000_000, bytes_accessed=1_000_000, transcendentals=1_000_000
        ),
    )(level, *arrays)


def swapped(value, axis, first):
    count = lax.axis_size(axis)
    wrap = axis == "space"
    pairs = []
    for i in range(first, count if wrap else count - 1, 2):
        j = (i + 1) % count
        pairs += [(i, j), (j, i)]
    return lax.ppermute(value, axis, pairs)


def local(
    noisy_state,
    fresh_noise,
    level_index,
    station_obs,
    obs_variance,
    station_owner,
    station_cell,
    conv_in,
    conv_mid,
    conv_res,
    conv_out,
    in_bias,
    noise_embed,
    norm_gain,
):
    even_s = lax.axis_index("space") % 2 == 0
    noisy = noisy_state.reshape(8, 16, 256)
    own, slots = pack(
        level_index,
        noisy,
        station_obs,
        obs_variance.reshape(1, 128),
        station_owner.reshape(1, 128),
        station_cell.reshape(1, 128),
    )
    t2 = swapped(own, "tm", 1)
    t1 = swapped(own, "tm", 0)
    got = lax.all_to_all(slots.reshape(64, 8, 128), "space", 0, 0, tiled=True).reshape(512, 128)

    edge = jnp.where(even_s, 12, 0)
    both = jnp.concatenate([t2, t1, own], axis=1)
    m2 = swapped(lax.dynamic_slice_in_dim(both, 12 - edge, 4, 0), "space", 1)
    m1 = swapped(lax.dynamic_slice_in_dim(both, edge, 4, 0), "space", 0)

    edges = jnp.concatenate([m2, m1], axis=0)
    held = inner(
        level_index,
        own,
        t2,
        t1,
        conv_in.transpose(0, 2, 1),
        conv_mid,
        conv_res,
        conv_out,
        in_bias.reshape(1, 64),
        noise_embed.reshape(1, 64),
        norm_gain.reshape(1, 64),
    )
    result = outer(
        level_index, own, t2, t1, edges, *held, noisy, fresh_noise.reshape(8, 16, 256), got
    )
    return result.reshape(noisy_state.shape)


def solution(mesh):
    rest = (P(),) * 7
    placed = (
        P("tm", None, "space", None),
        P("tm", None, "space", None),
        P(),
        P("tm", None, "space"),
        P("space"),
        P("space", None),
        P("space"),
    ) + rest
    return jax.shard_map(
        local, mesh=mesh, in_specs=placed, out_specs=P("tm", None, "space", None), check_vma=False
    )
```

time: 64.7 us -> 54.3 us (0.84)
  the two profiles are of different devices: /device:TPU:24 before, /device:TPU:16 now
where the time goes in v2:
time: 54.3 us; the launch traced here: 53.9 us
  starting transfers between devices  41.4 us (76%)
  Pallas kernels  7.94 us (15%)
  waiting for transfers between devices  2.24 us (4%)
  local copies, waits for them, and re-layouts  1.5 us (3%)
  between operations  0.87 us (2%)
    ppermute x4, starting transfers between devices, swapped(): return lax.ppermute(value, axis, pairs)  32.9 us
    all_to_all x1, starting transfers between devices, local(): lax.all_to_all(slots.reshape(64, 8, 128), 'space', 0, 0, tiled=True)  8.51 us
    pallas_call x1, Pallas kernels, outer(): pl.pallas_call(outer_body, out_shape=jax.ShapeDtypeStruct((8, 16, 256), F...  3.58 us
    pallas_call x1, Pallas kernels, inner(): pl.pallas_call(inner_body, out_shape=(jax.ShapeDtypeStruct((192, 240), BF...  2.33 us
    all_to_all x1, waiting for transfers between devices, local(): lax.all_to_all(slots.reshape(64, 8, 128), 'space', 0, 0, tiled=True)  2.23 us
    pallas_call x1, Pallas kernels, pack(): pl.pallas_call(pack_body, out_shape=(jax.ShapeDtypeStruct((16, 8, 256), B...  2.02 us
    unnamed x22, local copies, waits for them, and re-layouts  1.48 us
  transfers between devices with their start and end apart: 5, of which 1 were waited for; matrix products, arithmetic and copies ran while one was open for 0% of the time, Pallas kernels for 4%

profile of v2, /device:TPU:16, one launch (start us, length us, event | category | flops | bytes accessed | tf_op | source)
XLA Modules:
  0.0 53.9 jit_solution(9733909272211075300)
XLA Ops:
  0.7 2.0 %shard_map.136 = (bf16[16,8,256]{2,1,0:T(8,128)(2,1)}, f32[512,128]{1,0:T(8,128)}) custom-call(s32[1]{0:T(128)S(6)} %copy.17.level, f32[8,16,256]{2,1,0:T(8,128)} %bitcast.13, f32[4,2,128]{2,1,0:T(2,128)} %obs.1, f32[1,128]{1,0:T(1,128)} %bitcast.21, s32[1,128]{1,0:T(1,128)} %bitcast.22, s32[1,128]{1,0:T(1,128)} %bitcast.23), custom_call_target="tpu_custom_call" | custom-call | flops 50000000 | bytes 400000 | tf_op jit(solution)/shard_map/pallas_call | solution.py:84
  2.7 2.3 %collective-permute-start = (bf16[16,8,256]{2,1,0:T(8,128)(2,1)}, bf16[16,8,256]{2,1,0:T(8,128)(2,1)S(1)}, u32[]{:S(2)}, u32[]{:S(2)}) collective-permute-start(bf16[16,8,256]{2,1,0:T(8,128)(2,1)} %get-tuple-element.16.own), channel_id=1, source_target_pairs={{64,128},{128,64},{192,256},{256,192},{320,384},{384,320},{65,129}... | collective-permute-start | bytes 196616 | tf_op jit(solution)/shard_map/ppermute | solution.py:436
  5.0 16.2 %collective-permute-start.1 = (bf16[16,8,256]{2,1,0:T(8,128)(2,1)}, bf16[16,8,256]{2,1,0:T(8,128)(2,1)S(1)}, u32[]{:S(2)}, u32[]{:S(2)}) collective-permute-start(bf16[16,8,256]{2,1,0:T(8,128)(2,1)} %get-tuple-element.16.own), channel_id=1, source_target_pairs={{0,64},{64,0},{128,192},{192,128},{256,320},{320,256},{384,448},{4... | collective-permute-start | bytes 196616 | tf_op jit(solution)/shard_map/ppermute | solution.py:436
  21.2 8.5 %all-to-all-start = ((f32[64,8,128]{2,1,0:T(8,128)}), f32[64,8,128]{2,1,0:T(8,128)S(1)}, u32[]{:S(2)}, u32[]{:S(2)}) async-start(f32[64,8,128]{2,1,0:T(8,128)} %bitcast.20), calls=%async_computation | async-start | bytes 524288 | tf_op jit(solution)/shard_map/all_to_all | solution.py:467
  29.8 0.0 collective-permute-done.t2
  29.8 0.0 copy-start
  29.8 0.0 collective-permute-done.1.t1
  29.8 0.8 %copy-done = bf16[16,8,256]{2,1,0:T(8,128)(2,1)S(1)} copy-done((bf16[16,8,256]{2,1,0:T(8,128)(2,1)S(1)}, bf16[16,8,256]{2,1,0:T(8,128)(2,1)}, u32[]{:S(2)}) %copy-start) | copy-done | bytes 65560
  30.6 0.0 copy-start.5
  30.6 0.0 copy-start.6
  30.7 0.0 copy-start.3
  30.7 0.0 copy-start.4
  30.7 12.4 %collective-permute-start.2 = (bf16[4,24,256]{2,1,0:T(8,128)(2,1)S(1)}, bf16[4,24,256]{2,1,0:T(8,128)(2,1)S(1)}, u32[]{:S(2)}, u32[]{:S(2)}) collective-permute-start(bf16[4,24,256]{2,1,0:T(8,128)(2,1)S(1)} %get-tuple-element.27), channel_id=1, source_target_pairs={{1,2},{2,1},{3,4},{4,3},{5,6},{6,5},{7,8},{8,7},{9,10},{10,9},{11,... | collective-permute-start | bytes 147464 | tf_op jit(solution)/shard_map/ppermute | solution.py:436
  43.1 1.9 %collective-permute-start.3 = (bf16[4,24,256]{2,1,0:T(8,128)(2,1)S(1)}, bf16[4,24,256]{2,1,0:T(8,128)(2,1)S(1)}, u32[]{:S(2)}, u32[]{:S(2)}) collective-permute-start(bf16[4,24,256]{2,1,0:T(8,128)(2,1)S(1)} %get-tuple-element.28), channel_id=1, source_target_pairs={{0,1},{1,0},{2,3},{3,2},{4,5},{5,4},{6,7},{7,6},{8,9},{9,8},{10,11... | collective-permute-start | bytes 147464 | tf_op jit(solution)/shard_map/ppermute | solution.py:436
  45.0 0.0 copy-start.7
  45.0 0.0 copy-start.8
  45.1 0.0 copy-start.9
  45.1 0.0 copy-done.5
  45.1 0.0 copy-done.6
  45.1 0.0 copy-done.3
  45.1 0.0 copy-done.4
  45.1 0.6 %copy-done.7 = f32[64]{0:T(128)S(1)} copy-done((f32[64]{0:T(128)S(1)}, f32[64]{0:T(128)}, u32[]{:S(2)}) %copy-start.7) | copy-done | bytes 280
  45.7 0.0 copy-done.8
  45.7 0.0 copy-done.9
  45.7 0.0 copy-start.2
  45.7 2.3 %shard_map.137 = (bf16[192,240]{1,0:T(8,128)(2,1)S(1)}, bf16[192,192]{1,0:T(8,128)(2,1)S(1)}, bf16[192,192]{1,0:T(8,128)(2,1)S(1)}, bf16[96,768]{1,0:T(8,128)(2,...) custom-call(s32[1]{0:T(128)S(6)} %copy.17.level, ...), custom_call_target="tpu_custom_call" | custom-call | flops 8000000000 | bytes 1000000 | tf_op jit(solution)/shard_map/pallas_call | solution.py:260
  48.1 0.0 copy-start.1
  48.1 0.0 collective-permute-done.2
  48.1 0.0 collective-permute-done.3
  48.1 2.2 %all-to-all-done = f32[64,8,128]{2,1,0:T(8,128)S(1)} async-done(((f32[64,8,128]{2,1,0:T(8,128)}), f32[64,8,128]{2,1,0:T(8,128)S(1)}, u32[]{:S(2)}, u32[]{:S(2)}) %all-to-all-start) | async-done | bytes 262176 | tf_op jit(solution)/shard_map/all_to_all | solution.py:467
  50.3 0.0 copy-done.2
  50.3 0.0 copy-done.1
  50.3 3.6 %shard_map.138 = f32[8,16,256]{2,1,0:T(8,128)} custom-call(s32[1]{0:T(128)S(6)} %copy.17.level, bf16[16,8,256]{2,1,0:T(8,128)(2,1)S(1)} %copy-done, bf16[16,8,256]{2,1,0:T(8,128)(2,1)S(1)} %collective-permute-done.t2, bf16[16,8,256]{2,1,0:T(8,128)(2,1)S(1)} %collective-permute-done.1.t1, bf16[8,24,256]{2,1,0:T(8,128)(2,1)S(1)} %pad_maximum_fusion.edges, ...), custom_call_target="tpu_custom_call" | custom-call | flops 4000000000 | bytes 1000000 | tf_op jit(solution)/shard_map/pallas_call | solution.py:406
  (5 shorter events, 0.0 us)
Async XLA Ops:
  2.7 27.1 %collective-permute-start = (bf16[16,8,256]{2,1,0:T(8,128)(2,1)}, bf16[16,8,256]{2,1,0:T(8,128)(2,1)S(1)}, u32[]{:S(2)}, u32[]{:S(2)}) collective-permute-start(bf16[16,8,256]{2,1,0:T(8,128)(2,1)} %get-tuple-element.16.own), channel_id=1, source_target_pairs={{64,128},{128,64},{192,256},{256,192},{320,384},{384,320},{65,129}... | collective-permute-start | bytes 196616 | tf_op jit(solution)/shard_map/ppermute | solution.py:436
  5.0 24.8 %collective-permute-start.1 = (bf16[16,8,256]{2,1,0:T(8,128)(2,1)}, bf16[16,8,256]{2,1,0:T(8,128)(2,1)S(1)}, u32[]{:S(2)}, u32[]{:S(2)}) collective-permute-start(bf16[16,8,256]{2,1,0:T(8,128)(2,1)} %get-tuple-element.16.own), channel_id=1, source_target_pairs={{0,64},{64,0},{128,192},{192,128},{256,320},{320,256},{384,448},{4... | collective-permute-start | bytes 196616 | tf_op jit(solution)/shard_map/ppermute | solution.py:436
  21.2 29.1 %all-to-all-start = ((f32[64,8,128]{2,1,0:T(8,128)}), f32[64,8,128]{2,1,0:T(8,128)S(1)}, u32[]{:S(2)}, u32[]{:S(2)}) async-start(f32[64,8,128]{2,1,0:T(8,128)} %bitcast.20), calls=%async_computation | async-start | bytes 524288 | tf_op jit(solution)/shard_map/all_to_all | solution.py:467
  29.8 0.8 %copy-start = (bf16[16,8,256]{2,1,0:T(8,128)(2,1)S(1)}, bf16[16,8,256]{2,1,0:T(8,128)(2,1)}, u32[]{:S(2)}) copy-start(bf16[16,8,256]{2,1,0:T(8,128)(2,1)} %get-tuple-element.16.own) | copy-start | bytes 196612
  30.6 14.4 %copy-start.5 = (bf16[3,64,48]{1,2,0:T(8,128)(2,1)S(1)}, bf16[3,64,48]{1,2,0:T(8,128)(2,1)}, u32[]{:S(2)}) copy-start(bf16[3,64,48]{1,2,0:T(8,128)(2,1)} %param.21) | copy-start | bytes 55300
  30.6 14.4 %copy-start.6 = (bf16[3,16,192]{2,1,0:T(8,128)(2,1)S(1)}, bf16[3,16,192]{2,1,0:T(8,128)(2,1)}, u32[]{:S(2)}) copy-start(bf16[3,16,192]{2,1,0:T(8,128)(2,1)} %conv_out.1) | copy-start | bytes 55300
  30.7 14.4 %copy-start.3 = (bf16[3,64,192]{2,1,0:T(8,128)(2,1)S(1)}, bf16[3,64,192]{2,1,0:T(8,128)(2,1)}, u32[]{:S(2)}) copy-start(bf16[3,64,192]{2,1,0:T(8,128)(2,1)} %conv_mid.1) | copy-start | bytes 221188
  30.7 14.4 %copy-start.4 = (bf16[3,64,192]{2,1,0:T(8,128)(2,1)S(1)}, bf16[3,64,192]{2,1,0:T(8,128)(2,1)}, u32[]{:S(2)}) copy-start(bf16[3,64,192]{2,1,0:T(8,128)(2,1)} %conv_res.1) | copy-start | bytes 221188
  30.7 17.4 %collective-permute-start.2 = (bf16[4,24,256]{2,1,0:T(8,128)(2,1)S(1)}, bf16[4,24,256]{2,1,0:T(8,128)(2,1)S(1)}, u32[]{:S(2)}, u32[]{:S(2)}) collective-permute-start(bf16[4,24,256]{2,1,0:T(8,128)(2,1)S(1)} %get-tuple-element.27), channel_id=1, source_target_pairs={{1,2},{2,1},{3,4},{4,3},{5,6},{6,5},{7,8},{8,7},{9,10},{10,9},{11,... | collective-permute-start | bytes 147464 | tf_op jit(solution)/shard_map/ppermute | solution.py:436
  43.1 5.0 %collective-permute-start.3 = (bf16[4,24,256]{2,1,0:T(8,128)(2,1)S(1)}, bf16[4,24,256]{2,1,0:T(8,128)(2,1)S(1)}, u32[]{:S(2)}, u32[]{:S(2)}) collective-permute-start(bf16[4,24,256]{2,1,0:T(8,128)(2,1)S(1)} %get-tuple-element.28), channel_id=1, source_target_pairs={{0,1},{1,0},{2,3},{3,2},{4,5},{5,4},{6,7},{7,6},{8,9},{9,8},{10,11... | collective-permute-start | bytes 147464 | tf_op jit(solution)/shard_map/ppermute | solution.py:436
  45.0 0.7 %copy-start.7 = (f32[64]{0:T(128)S(1)}, f32[64]{0:T(128)}, u32[]{:S(2)}) copy-start(f32[64]{0:T(128)} %param.25) | copy-start | bytes 772
  45.0 0.7 %copy-start.8 = (f32[64]{0:T(128)S(1)}, f32[64]{0:T(128)}, u32[]{:S(2)}) copy-start(f32[64]{0:T(128)} %param.26) | copy-start | bytes 772
  45.1 0.7 %copy-start.9 = (f32[64]{0:T(128)S(1)}, f32[64]{0:T(128)}, u32[]{:S(2)}) copy-start(f32[64]{0:T(128)} %param.27) | copy-start | bytes 772
  45.7 4.6 %copy-start.2 = (f32[4,2,16,256]{3,2,1,0:T(8,128)S(1)}, f32[4,2,16,256]{3,2,1,0:T(8,128)}, u32[]{:S(2)}) copy-start(f32[4,2,16,256]{3,2,1,0:T(8,128)} %param.15) | copy-start | bytes 393220
  48.1 2.3 %copy-start.1 = (f32[4,2,16,256]{3,2,1,0:T(8,128)S(1)}, f32[4,2,16,256]{3,2,1,0:T(8,128)}, u32[]{:S(2)}) copy-start(f32[4,2,16,256]{3,2,1,0:T(8,128)} %param.14) | copy-start | bytes 393220

commit v3 on v2

--- a/solution.py
+++ b/solution.py
@@ -5,13 +5,16 @@
 from jax import lax
 from jax.experimental import pallas as pl
 from jax.experimental.pallas import tpu as pltpu
+from jax.sharding import Mesh
 from jax.sharding import PartitionSpec as P
 
 LEVELS = 32
+SPACE = ("x", "z", "core")
+X_SIZE, Z_SIZE, CORES = 4, 8, 2
 BF = jnp.bfloat16
 F32 = jnp.float32
 OUT_GROUP = 4
-INNER_COST = 8_000_000_000
+INNER_COST = 16_000_000_000
 VM = pl.BlockSpec(memory_space=pltpu.VMEM)
 SM = pl.BlockSpec(memory_space=pltpu.SMEM)
 ANY = pl.BlockSpec(memory_space=pl.ANY)
@@ -60,7 +63,10 @@
     col = lax.broadcasted_iota(jnp.int32, (count, count), 1)
     same = (own_col == own_row) & (row < col)
     rank = jnp.sum(jnp.where(same, 1.0, 0.0), axis=0, keepdims=True)
-    slot = (own_row * 8.0 + rank).astype(jnp.int32)
+    strip = owner[...]
+    x_core = (strip // (Z_SIZE * CORES)) * CORES + strip % CORES
+    block = x_core * Z_SIZE + (strip // CORES) % Z_SIZE
+    slot = block * 8 + rank.astype(jnp.int32)
     near = noise[:1, :count]
     weight = 1.0 / (var[...] + near * near)
     values = jnp.concatenate([obs[k] for k in range(obs.shape[0])], axis=0) * weight
@@ -321,7 +327,7 @@
     for copy in copies:
         copy.start()
     even_t = lax.axis_index("tm") % 2 == 0
-    even_s = lax.axis_index("space") % 2 == 0
+    even_s = lax.axis_index(SPACE) % 2 == 0
     bias = columns[0][:, :1]
     gain = columns[1][:, :1]
 
@@ -428,7 +434,7 @@
 
 def swapped(value, axis, first):
     count = lax.axis_size(axis)
-    wrap = axis == "space"
+    wrap = axis == SPACE
     pairs = []
     for i in range(first, count if wrap else count - 1, 2):
         j = (i + 1) % count
@@ -452,7 +458,7 @@
     noise_embed,
     norm_gain,
 ):
-    even_s = lax.axis_index("space") % 2 == 0
+    even_s = lax.axis_index(SPACE) % 2 == 0
     noisy = noisy_state.reshape(8, 16, 256)
     own, slots = pack(
         level_index,
@@ -464,12 +470,14 @@
     )
     t2 = swapped(own, "tm", 1)
     t1 = swapped(own, "tm", 0)
-    got = lax.all_to_all(slots.reshape(64, 8, 128), "space", 0, 0, tiled=True).reshape(512, 128)
+    near = lax.all_to_all(slots.reshape(8, 8, 8, 128), ("x", "core"), 0, 0, tiled=True)
+    near = near.transpose(1, 0, 2, 3)
+    got = lax.all_to_all(near, "z", 0, 0, tiled=True).reshape(512, 128)
 
     edge = jnp.where(even_s, 12, 0)
     both = jnp.concatenate([t2, t1, own], axis=1)
-    m2 = swapped(lax.dynamic_slice_in_dim(both, 12 - edge, 4, 0), "space", 1)
-    m1 = swapped(lax.dynamic_slice_in_dim(both, edge, 4, 0), "space", 0)
+    m2 = swapped(lax.dynamic_slice_in_dim(both, 12 - edge, 4, 0), SPACE, 1)
+    m1 = swapped(lax.dynamic_slice_in_dim(both, edge, 4, 0), SPACE, 0)
 
     edges = jnp.concatenate([m2, m1], axis=0)
     held = inner(
@@ -492,16 +500,18 @@
 
 
 def solution(mesh):
+    times = mesh.shape["tm"]
+    fine = Mesh(mesh.devices.reshape(times, X_SIZE, Z_SIZE, CORES), ("tm",) + SPACE)
     rest = (P(),) * 7
     placed = (
-        P("tm", None, "space", None),
-        P("tm", None, "space", None),
+        P("tm", None, SPACE, None),
+        P("tm", None, SPACE, None),
         P(),
-        P("tm", None, "space"),
-        P("space"),
-        P("space", None),
-        P("space"),
+        P("tm", None, SPACE),
+        P(SPACE),
+        P(SPACE, None),
+        P(SPACE),
     ) + rest
     return jax.shard_map(
-        local, mesh=mesh, in_specs=placed, out_specs=P("tm", None, "space", None), check_vma=False
-    )
+        local, mesh=fine, in_specs=placed, out_specs=P("tm", None, SPACE, None), check_vma=False
+    )

time: 54.3 us -> 63.5 us (1.17)
  waiting for transfers between devices: 2.24 us -> 13.8 us
  starting transfers between devices: 41.4 us -> 38.3 us
  local copies, waits for them, and re-layouts: 1.5 us -> 2.21 us
    all_to_all x1 -> x2, waiting for transfers between devices: 2.23 us -> 13.8 us  [the longest x1 13.7 us: local(): got = lax.all_to_all(near, 'z', 0, 0, tiled=True).reshape(512, 128)]
    ppermute x4, starting transfers between devices: 32.9 us -> 28.5 us  [swapped(): return lax.ppermute(value, axis, pairs)]
    all_to_all x1 -> x2, starting transfers between devices: 8.51 us -> 9.76 us  [the longest x1 5.44 us: local(): got = lax.all_to_all(near, 'z', 0, 0, tiled=True).reshape(512, 128)]
    transpose x0 -> x1, local copies, waits for them, and re-layouts: none -> 0.72 us  [local(): near = near.transpose(1, 0, 2, 3)]
  transfers between devices with their start and end apart: 5 -> 6, of which waited for: 1 -> 1; matrix products, arithmetic and copies ran while one was open for 0% -> 1% of each run, Pallas kernels for 4% -> 4%
where the time goes in v3:
time: 63.5 us; the launch traced here: 63 us
  starting transfers between devices  38.3 us (60%)
  waiting for transfers between devices  13.8 us (22%)
  Pallas kernels  7.92 us (12%)
  local copies, waits for them, and re-layouts  2.21 us (3%)
  between operations  0.83 us (1%)
    ppermute x4, starting transfers between devices, swapped(): return lax.ppermute(value, axis, pairs)  28.5 us
    all_to_all x1, waiting for transfers between devices, local(): got = lax.all_to_all(near, 'z', 0, 0, tiled=True).reshape(512, 128)  13.7 us
    all_to_all x1, starting transfers between devices, local(): got = lax.all_to_all(near, 'z', 0, 0, tiled=True).reshape(512, 128)  5.44 us
    all_to_all x1, starting transfers between devices, local(): lax.all_to_all(slots.reshape(8, 8, 8, 128), ('x', 'core'), 0, 0, tiled=True)  4.32 us
    pallas_call x1, Pallas kernels, outer(): pl.pallas_call(outer_body, out_shape=jax.ShapeDtypeStruct((8, 16, 256), F...  3.58 us
    pallas_call x1, Pallas kernels, inner(): pl.pallas_call(inner_body, out_shape=(jax.ShapeDtypeStruct((192, 240), BF...  2.32 us
    pallas_call x1, Pallas kernels, pack(): pl.pallas_call(pack_body, out_shape=(jax.ShapeDtypeStruct((16, 8, 256), B...  2.02 us
    unnamed x22, local copies, waits for them, and re-layouts  1.47 us
  transfers between devices with their start and end apart: 6, of which 1 were waited for; matrix products, arithmetic and copies ran while one was open for 1% of the time, Pallas kernels for 4%

profile of v3, /device:TPU:16, one launch (start us, length us, event | category | flops | bytes accessed | tf_op | source)
XLA Modules:
  0.0 63.0 jit_solution(14217430389140449934)
XLA Ops:
  0.7 2.0 %shard_map.136 = (bf16[16,8,256]{2,1,0:T(8,128)(2,1)}, f32[512,128]{1,0:T(8,128)}) custom-call(s32[1]{0:T(128)S(6)} %copy.20.level, f32[8,16,256]{2,1,0:T(8,128)} %bitcast.14, f32[4,2,128]{2,1,0:T(2,128)} %obs.1, f32[1,128]{1,0:T(1,128)} %bitcast.23, s32[1,128]{1,0:T(1,128)} %bitcast.24, s32[1,128]{1,0:T(1,128)} %bitcast.25), custom_call_target="tpu_custom_call" | custom-call | flops 50000000 | bytes 400000 | tf_op jit(solution)/shard_map/pallas_call | solution.py:90
  2.7 2.3 %collective-permute-start = (bf16[16,8,256]{2,1,0:T(8,128)(2,1)}, bf16[16,8,256]{2,1,0:T(8,128)(2,1)S(1)}, u32[]{:S(2)}, u32[]{:S(2)}) collective-permute-start(bf16[16,8,256]{2,1,0:T(8,128)(2,1)} %get-tuple-element.16.own), channel_id=1, source_target_pairs={{64,128},{128,64},{192,256},{256,192},{320,384},{384,320},{65,129}... | collective-permute-start | bytes 196616 | tf_op jit(solution)/shard_map/ppermute | solution.py:442
  5.0 16.2 %collective-permute-start.1 = (bf16[16,8,256]{2,1,0:T(8,128)(2,1)}, bf16[16,8,256]{2,1,0:T(8,128)(2,1)S(1)}, u32[]{:S(2)}, u32[]{:S(2)}) collective-permute-start(bf16[16,8,256]{2,1,0:T(8,128)(2,1)} %get-tuple-element.16.own), channel_id=1, source_target_pairs={{0,64},{64,0},{128,192},{192,128},{256,320},{320,256},{384,448},{4... | collective-permute-start | bytes 196616 | tf_op jit(solution)/shard_map/ppermute | solution.py:442
  21.2 4.3 %all-to-all-start = ((f32[8,8,8,128]{3,2,1,0:T(8,128)}), f32[8,8,8,128]{3,2,1,0:T(8,128)S(1)}, u32[]{:S(2)}, u32[]{:S(2)}) async-start(f32[8,8,8,128]{3,2,1,0:T(8,128)} %bitcast.22), calls=%async_computation | async-start | bytes 524288 | tf_op jit(solution)/shard_map/all_to_all | solution.py:473
  25.6 0.0 collective-permute-done.t2
  25.6 0.0 copy-start
  25.6 0.0 collective-permute-done.1.t1
  25.6 0.8 %copy-done = bf16[16,8,256]{2,1,0:T(8,128)(2,1)S(1)} copy-done((bf16[16,8,256]{2,1,0:T(8,128)(2,1)S(1)}, bf16[16,8,256]{2,1,0:T(8,128)(2,1)}, u32[]{:S(2)}) %copy-start) | copy-done | bytes 65560
  26.4 8.1 %collective-permute-start.2 = (bf16[4,24,256]{2,1,0:T(8,128)(2,1)S(1)}, bf16[4,24,256]{2,1,0:T(8,128)(2,1)S(1)}, u32[]{:S(2)}, u32[]{:S(2)}) collective-permute-start(bf16[4,24,256]{2,1,0:T(8,128)(2,1)S(1)} %get-tuple-element.27), channel_id=1, source_target_pairs={{1,2},{2,1},{3,4},{4,3},{5,6},{6,5},{7,8},{8,7},{9,10},{10,9},{11,... | collective-permute-start | bytes 147464 | tf_op jit(solution)/shard_map/ppermute | solution.py:442
  34.5 1.9 %collective-permute-start.3 = (bf16[4,24,256]{2,1,0:T(8,128)(2,1)S(1)}, bf16[4,24,256]{2,1,0:T(8,128)(2,1)S(1)}, u32[]{:S(2)}, u32[]{:S(2)}) collective-permute-start(bf16[4,24,256]{2,1,0:T(8,128)(2,1)S(1)} %get-tuple-element.28), channel_id=1, source_target_pairs={{0,1},{1,0},{2,3},{3,2},{4,5},{5,4},{6,7},{7,6},{8,9},{9,8},{10,11... | collective-permute-start | bytes 147464 | tf_op jit(solution)/shard_map/ppermute | solution.py:442
  36.4 0.0 all-to-all-done
  36.5 0.7 %copy.17 = f32[8,8,8,128]{3,2,1,0:T(8,128)} copy(f32[8,8,8,128]{3,2,0,1:T(8,128)S(1)} %bitcast.21) | data formatting | bytes 524288 | tf_op jit(solution)/shard_map/transpose | solution.py:474
  37.2 0.0 copy-start.3
  37.2 0.0 copy-start.4
  37.2 0.0 copy-start.5
  37.2 0.0 copy-start.6
  37.2 5.4 %all-to-all-start.1 = ((f32[8,8,8,128]{3,2,1,0:T(8,128)}), f32[8,8,8,128]{3,2,1,0:T(8,128)S(1)}, u32[]{:S(2)}, u32[]{:S(2)}) async-start(f32[8,8,8,128]{3,2,1,0:T(8,128)} %copy.17), calls=%async_computation.1 | async-start | bytes 524288 | tf_op jit(solution)/shard_map/all_to_all | solution.py:475
  42.6 0.0 copy-start.7
  42.6 0.0 copy-start.8
  42.6 0.0 copy-start.9
  42.7 0.0 copy-done.3
  42.7 0.0 copy-done.4
  42.7 0.0 copy-done.5
  42.7 0.0 copy-done.6
  42.7 0.6 copy-done.7
  43.3 0.0 copy-done.8
  43.3 0.0 copy-done.9
  43.3 0.0 copy-start.2
  43.3 2.3 %shard_map.137 = (bf16[192,240]{1,0:T(8,128)(2,1)S(1)}, bf16[192,192]{1,0:T(8,128)(2,1)S(1)}, bf16[192,192]{1,0:T(8,128)(2,1)S(1)}, bf16[96,768]{1,0:T(8,128)(2,...) custom-call(s32[1]{0:T(128)S(6)} %copy.20.level, ...), custom_call_target="tpu_custom_call" | custom-call | flops 16000000000 | bytes 1000000 | tf_op jit(solution)/shard_map/pallas_call | solution.py:266
  45.6 0.0 copy-start.1
  45.7 0.0 collective-permute-done.2
  45.7 0.0 collective-permute-done.3
  45.7 13.7 %all-to-all-done.1 = f32[8,8,8,128]{3,2,1,0:T(8,128)S(1)} async-done(((f32[8,8,8,128]{3,2,1,0:T(8,128)}), f32[8,8,8,128]{3,2,1,0:T(8,128)S(1)}, u32[]{:S(2)}, u32[]{:S(2)}) %all-to-all-start.1) | async-done | bytes 262176 | tf_op jit(solution)/shard_map/all_to_all | solution.py:475
  59.4 0.0 copy-done.2
  59.5 0.0 copy-done.1
  59.5 3.6 %shard_map.138 = f32[8,16,256]{2,1,0:T(8,128)} custom-call(s32[1]{0:T(128)S(6)} %copy.20.level, bf16[16,8,256]{2,1,0:T(8,128)(2,1)S(1)} %copy-done, bf16[16,8,256]{2,1,0:T(8,128)(2,1)S(1)} %collective-permute-done.t2, bf16[16,8,256]{2,1,0:T(8,128)(2,1)S(1)} %collective-permute-done.1.t1, bf16[8,24,256]{2,1,0:T(8,128)(2,1)S(1)} %pad_maximum_fusion.edges, ...), custom_call_target="tpu_custom_call" | custom-call | flops 4000000000 | bytes 1000000 | tf_op jit(solution)/shard_map/pallas_call | solution.py:412
  (5 shorter events, 0.0 us)
Async XLA Ops:
  2.7 22.9 %collective-permute-start = (bf16[16,8,256]{2,1,0:T(8,128)(2,1)}, bf16[16,8,256]{2,1,0:T(8,128)(2,1)S(1)}, u32[]{:S(2)}, u32[]{:S(2)}) collective-permute-start(bf16[16,8,256]{2,1,0:T(8,128)(2,1)} %get-tuple-element.16.own), channel_id=1, source_target_pairs={{64,128},{128,64},{192,256},{256,192},{320,384},{384,320},{65,129}... | collective-permute-start | bytes 196616 | tf_op jit(solution)/shard_map/ppermute | solution.py:442
  5.0 20.6 %collective-permute-start.1 = (bf16[16,8,256]{2,1,0:T(8,128)(2,1)}, bf16[16,8,256]{2,1,0:T(8,128)(2,1)S(1)}, u32[]{:S(2)}, u32[]{:S(2)}) collective-permute-start(bf16[16,8,256]{2,1,0:T(8,128)(2,1)} %get-tuple-element.16.own), channel_id=1, source_target_pairs={{0,64},{64,0},{128,192},{192,128},{256,320},{320,256},{384,448},{4... | collective-permute-start | bytes 196616 | tf_op jit(solution)/shard_map/ppermute | solution.py:442
  21.2 15.2 %all-to-all-start = ((f32[8,8,8,128]{3,2,1,0:T(8,128)}), f32[8,8,8,128]{3,2,1,0:T(8,128)S(1)}, u32[]{:S(2)}, u32[]{:S(2)}) async-start(f32[8,8,8,128]{3,2,1,0:T(8,128)} %bitcast.22), calls=%async_computation | async-start | bytes 524288 | tf_op jit(solution)/shard_map/all_to_all | solution.py:473
  25.6 0.8 %copy-start = (bf16[16,8,256]{2,1,0:T(8,128)(2,1)S(1)}, bf16[16,8,256]{2,1,0:T(8,128)(2,1)}, u32[]{:S(2)}) copy-start(bf16[16,8,256]{2,1,0:T(8,128)(2,1)} %get-tuple-element.16.own) | copy-start | bytes 196612
  26.4 19.2 %collective-permute-start.2 = (bf16[4,24,256]{2,1,0:T(8,128)(2,1)S(1)}, bf16[4,24,256]{2,1,0:T(8,128)(2,1)S(1)}, u32[]{:S(2)}, u32[]{:S(2)}) collective-permute-start(bf16[4,24,256]{2,1,0:T(8,128)(2,1)S(1)} %get-tuple-element.27), channel_id=1, source_target_pairs={{1,2},{2,1},{3,4},{4,3},{5,6},{6,5},{7,8},{8,7},{9,10},{10,9},{11,... | collective-permute-start | bytes 147464 | tf_op jit(solution)/shard_map/ppermute | solution.py:442
  34.5 11.2 %collective-permute-start.3 = (bf16[4,24,256]{2,1,0:T(8,128)(2,1)S(1)}, bf16[4,24,256]{2,1,0:T(8,128)(2,1)S(1)}, u32[]{:S(2)}, u32[]{:S(2)}) collective-permute-start(bf16[4,24,256]{2,1,0:T(8,128)(2,1)S(1)} %get-tuple-element.28), channel_id=1, source_target_pairs={{0,1},{1,0},{2,3},{3,2},{4,5},{5,4},{6,7},{7,6},{8,9},{9,8},{10,11... | collective-permute-start | bytes 147464 | tf_op jit(solution)/shard_map/ppermute | solution.py:442
  37.2 5.5 %copy-start.3 = (bf16[3,64,192]{2,1,0:T(8,128)(2,1)S(1)}, bf16[3,64,192]{2,1,0:T(8,128)(2,1)}, u32[]{:S(2)}) copy-start(bf16[3,64,192]{2,1,0:T(8,128)(2,1)} %conv_mid.1) | copy-start | bytes 221188
  37.2 5.5 %copy-start.4 = (bf16[3,64,192]{2,1,0:T(8,128)(2,1)S(1)}, bf16[3,64,192]{2,1,0:T(8,128)(2,1)}, u32[]{:S(2)}) copy-start(bf16[3,64,192]{2,1,0:T(8,128)(2,1)} %conv_res.1) | copy-start | bytes 221188
  37.2 5.5 %copy-start.5 = (bf16[3,64,48]{1,2,0:T(8,128)(2,1)S(1)}, bf16[3,64,48]{1,2,0:T(8,128)(2,1)}, u32[]{:S(2)}) copy-start(bf16[3,64,48]{1,2,0:T(8,128)(2,1)} %param.21) | copy-start | bytes 55300
  37.2 5.5 %copy-start.6 = (bf16[3,16,192]{2,1,0:T(8,128)(2,1)S(1)}, bf16[3,16,192]{2,1,0:T(8,128)(2,1)}, u32[]{:S(2)}) copy-start(bf16[3,16,192]{2,1,0:T(8,128)(2,1)} %conv_out.1) | copy-start | bytes 55300
  37.2 22.3 %all-to-all-start.1 = ((f32[8,8,8,128]{3,2,1,0:T(8,128)}), f32[8,8,8,128]{3,2,1,0:T(8,128)S(1)}, u32[]{:S(2)}, u32[]{:S(2)}) async-start(f32[8,8,8,128]{3,2,1,0:T(8,128)} %copy.17), calls=%async_computation.1 | async-start | bytes 524288 | tf_op jit(solution)/shard_map/all_to_all | solution.py:475
  42.6 0.7 %copy-start.7 = (f32[64]{0:T(128)S(1)}, f32[64]{0:T(128)}, u32[]{:S(2)}) copy-start(f32[64]{0:T(128)} %param.25) | copy-start | bytes 772
  42.6 0.7 %copy-start.8 = (f32[64]{0:T(128)S(1)}, f32[64]{0:T(128)}, u32[]{:S(2)}) copy-start(f32[64]{0:T(128)} %param.26) | copy-start | bytes 772
  42.6 0.7 %copy-start.9 = (f32[64]{0:T(128)S(1)}, f32[64]{0:T(128)}, u32[]{:S(2)}) copy-start(f32[64]{0:T(128)} %param.27) | copy-start | bytes 772
  43.3 16.1 %copy-start.2 = (f32[4,2,16,256]{3,2,1,0:T(8,128)S(1)}, f32[4,2,16,256]{3,2,1,0:T(8,128)}, u32[]{:S(2)}) copy-start(f32[4,2,16,256]{3,2,1,0:T(8,128)} %param.15) | copy-start | bytes 393220
  45.6 13.8 %copy-start.1 = (f32[4,2,16,256]{3,2,1,0:T(8,128)S(1)}, f32[4,2,16,256]{3,2,1,0:T(8,128)}, u32[]{:S(2)}) copy-start(f32[4,2,16,256]{3,2,1,0:T(8,128)} %param.14) | copy-start | bytes 393220

commit v4 on v2

--- a/solution.py
+++ b/solution.py
@@ -8,6 +8,7 @@
 from jax.sharding import PartitionSpec as P
 
 LEVELS = 32
+LEADER = 8
 BF = jnp.bfloat16
 F32 = jnp.float32
 OUT_GROUP = 4
@@ -47,37 +48,38 @@
 
 def pack_body(level, noisy, obs, var, owner, cell, own, out, turned):
     count = obs.shape[2]
-    slots = out.shape[0]
+    peers = out.shape[0]
     noise = scale_at(level[0], (16, 256))
     inverse = 1.0 / jnp.sqrt(1.0 + noise * noise)
     for v in range(8):
         turned[:, v, :] = noisy[v] * inverse
     own[...] = turned[...].astype(BF)
 
-    own_row = owner[...].astype(F32)
+    strip = owner[...]
+    own_row = strip.astype(F32)
     own_col = column_of(own_row)
     row = lax.broadcasted_iota(jnp.int32, (count, count), 0)
     col = lax.broadcasted_iota(jnp.int32, (count, count), 1)
     same = (own_col == own_row) & (row < col)
     rank = jnp.sum(jnp.where(same, 1.0, 0.0), axis=0, keepdims=True)
-    slot = (own_row * 8.0 + rank).astype(jnp.int32)
     near = noise[:1, :count]
     weight = 1.0 / (var[...] + near * near)
     values = jnp.concatenate([obs[k] for k in range(obs.shape[0])], axis=0) * weight
     spot = cell[...]
     extra = [weight, (spot // 256).astype(F32), (spot % 256).astype(F32)]
-    spare = jnp.zeros((128 - values.shape[0] - len(extra), count), F32)
+    spare = jnp.zeros((16 - values.shape[0] - len(extra), count), F32)
     table = jnp.concatenate([values] + extra + [spare], axis=0)
+    ranked = jnp.concatenate([jnp.where(rank == float(k), table, 0.0) for k in range(8)], axis=0)
     hot = jnp.where(
-        lax.broadcasted_iota(jnp.int32, (slots, count), 0) == slot, 1.0, 0.0
+        lax.broadcasted_iota(jnp.int32, (peers, count), 0) == (strip + (peers - LEADER)) % peers, 1.0, 0.0
     ).astype(BF)
     total = None
-    for part in parts_of(table):
+    for part in parts_of(ranked):
         piece = lax.dot_general(
             hot, part, (((1,), (1,)), ((), ())), preferred_element_type=F32
         )
         total = piece if total is None else total + piece
-    out[...] = total
+    out[:, 0, :] = total
 
 
 def pack(level, noisy, obs, var, owner, cell):
@@ -85,7 +87,7 @@
         pack_body,
         out_shape=(
             jax.ShapeDtypeStruct((16, 8, 256), BF),
-            jax.ShapeDtypeStruct((512, 128), F32),
+            jax.ShapeDtypeStruct((64, 1, 128), F32),
         ),
         in_specs=[SM, VM, VM, VM, VM, VM],
         out_specs=(VM, VM),
@@ -374,8 +376,9 @@
 
     for copy in copies:
         copy.wait()
-    slots = got.shape[0]
-    table = got[...].T
+    wide = got[:, 0, :].T
+    table = jnp.concatenate([wide[k * 16 : (k + 1) * 16] for k in range(8)], axis=1)
+    slots = table.shape[1]
     masks = (
         lax.broadcasted_iota(jnp.int32, (16, slots), 0) == table[9:10].astype(jnp.int32)
     )
@@ -416,7 +419,7 @@
             pltpu.VMEM((8, 16, 256), F32),
             pltpu.VMEM((8, 16, 256), F32),
             pltpu.VMEM((8, 16, 256), F32),
-            pltpu.VMEM((512, 128), F32),
+            pltpu.VMEM((64, 1, 128), F32),
             pltpu.SemaphoreType.DMA((3,)),
         ],
         compiler_params=pltpu.CompilerParams(vmem_limit_bytes=40 * 2**20),
@@ -424,6 +427,10 @@
             flops=4_000_000_000, bytes_accessed=1_000_000, transcendentals=1_000_000
         ),
     )(level, *arrays)
+
+
+def order_of(count):
+    return [(k + LEADER) % count for k in range(count)]
 
 
 def swapped(value, axis, first):
@@ -464,7 +471,9 @@
     )
     t2 = swapped(own, "tm", 1)
     t1 = swapped(own, "tm", 0)
-    got = lax.all_to_all(slots.reshape(64, 8, 128), "space", 0, 0, tiled=True).reshape(512, 128)
+    got = lax.all_to_all(
+        slots, "space", 0, 0, axis_index_groups=[order_of(slots.shape[0])], tiled=True
+    )
 
     edge = jnp.where(even_s, 12, 0)
     both = jnp.concatenate([t2, t1, own], axis=1)

time: 54.3 us -> 50.9 us (0.937)
  starting transfers between devices: 41.4 us -> 38.1 us
    ppermute x4, starting transfers between devices: 32.9 us -> 27.6 us  [swapped(): return lax.ppermute(value, axis, pairs)]
    all_to_all x1, waiting for transfers between devices: 2.23 us -> 0.01 us  [local(): lax.all_to_all(slots, 'space', 0, 0, axis_index_groups=[order_of(slots.sh...]
    ppermute x4, waiting for transfers between devices: 0.01 us -> 2.14 us  [swapped(): return lax.ppermute(value, axis, pairs)]
    all_to_all x1, starting transfers between devices: 8.51 us -> 10.5 us  [local(): lax.all_to_all(slots, 'space', 0, 0, axis_index_groups=[order_of(slots.sh...]
  transfers between devices with their start and end apart: 5 -> 5, of which waited for: 1 -> 1; matrix products, arithmetic and copies ran while one was open for 0% -> 0% of each run, Pallas kernels for 4% -> 5%
where the time goes in v4:
time: 50.9 us; the launch traced here: 50.5 us
  starting transfers between devices  38.1 us (75%)
  Pallas kernels  7.88 us (15%)
  waiting for transfers between devices  2.14 us (4%)
  local copies, waits for them, and re-layouts  1.5 us (3%)
  between operations  0.88 us (2%)
    ppermute x4, starting transfers between devices, swapped(): return lax.ppermute(value, axis, pairs)  27.6 us
    all_to_all x1, starting transfers between devices, local(): lax.all_to_all(slots, 'space', 0, 0, axis_index_groups=[order_of(slots.sh...  10.5 us
    pallas_call x1, Pallas kernels, outer(): pl.pallas_call(outer_body, out_shape=jax.ShapeDtypeStruct((8, 16, 256), F...  3.68 us
    pallas_call x1, Pallas kernels, inner(): pl.pallas_call(inner_body, out_shape=(jax.ShapeDtypeStruct((192, 240), BF...  2.33 us
    ppermute x4, waiting for transfers between devices, swapped(): return lax.ppermute(value, axis, pairs)  2.14 us
    pallas_call x1, Pallas kernels, pack(): pl.pallas_call(pack_body, out_shape=(jax.ShapeDtypeStruct((16, 8, 256), B...  1.87 us
    unnamed x22, local copies, waits for them, and re-layouts  1.48 us
  transfers between devices with their start and end apart: 5, of which 1 were waited for; matrix products, arithmetic and copies ran while one was open for 0% of the time, Pallas kernels for 5%

profile of v4, /device:TPU:16, one launch (start us, length us, event | category | flops | bytes accessed | tf_op | source)
XLA Modules:
  0.0 50.5 jit_solution(8044462615559144509)
XLA Ops:
  0.7 1.9 %shard_map.136 = (bf16[16,8,256]{2,1,0:T(8,128)(2,1)}, f32[64,1,128]{2,1,0:T(1,128)}) custom-call(s32[1]{0:T(128)S(6)} %copy.17.level, f32[8,16,256]{2,1,0:T(8,128)} %bitcast.10, f32[4,2,128]{2,1,0:T(2,128)} %obs.1, f32[1,128]{1,0:T(1,128)} %bitcast.17, s32[1,128]{1,0:T(1,128)} %bitcast.18, s32[1,128]{1,0:T(1,128)} %bitcast.19), custom_call_target="tpu_custom_call" | custom-call | flops 50000000 | bytes 400000 | tf_op jit(solution)/shard_map/pallas_call | solution.py:86
  2.5 2.3 %collective-permute-start = (bf16[16,8,256]{2,1,0:T(8,128)(2,1)}, bf16[16,8,256]{2,1,0:T(8,128)(2,1)S(1)}, u32[]{:S(2)}, u32[]{:S(2)}) collective-permute-start(bf16[16,8,256]{2,1,0:T(8,128)(2,1)} %get-tuple-element.16.own), channel_id=1, source_target_pairs={{64,128},{128,64},{192,256},{256,192},{320,384},{384,320},{65,129}... | collective-permute-start | bytes 196616 | tf_op jit(solution)/shard_map/ppermute | solution.py:443
  4.9 16.2 %collective-permute-start.1 = (bf16[16,8,256]{2,1,0:T(8,128)(2,1)}, bf16[16,8,256]{2,1,0:T(8,128)(2,1)S(1)}, u32[]{:S(2)}, u32[]{:S(2)}) collective-permute-start(bf16[16,8,256]{2,1,0:T(8,128)(2,1)} %get-tuple-element.16.own), channel_id=1, source_target_pairs={{0,64},{64,0},{128,192},{192,128},{256,320},{320,256},{384,448},{4... | collective-permute-start | bytes 196616 | tf_op jit(solution)/shard_map/ppermute | solution.py:443
  21.1 10.5 %all-to-all-start = ((f32[64,1,128]{2,1,0:T(1,128)}), f32[64,1,128]{2,1,0:T(1,128)S(1)}, u32[]{:S(2)}, u32[]{:S(2)}) async-start(f32[64,1,128]{2,1,0:T(1,128)} %get-tuple-element.26), calls=%async_computation | async-start | bytes 65536 | tf_op jit(solution)/shard_map/all_to_all | solution.py:474
  31.6 0.0 collective-permute-done.t2
  31.6 0.0 copy-start
  31.7 0.0 collective-permute-done.1.t1
  31.7 0.8 %copy-done = bf16[16,8,256]{2,1,0:T(8,128)(2,1)S(1)} copy-done((bf16[16,8,256]{2,1,0:T(8,128)(2,1)S(1)}, bf16[16,8,256]{2,1,0:T(8,128)(2,1)}, u32[]{:S(2)}) %copy-start) | copy-done | bytes 65560
  32.5 0.0 copy-start.5
  32.5 0.0 copy-start.6
  32.5 0.0 copy-start.3
  32.5 0.0 copy-start.4
  32.6 7.1 %collective-permute-start.2 = (bf16[4,24,256]{2,1,0:T(8,128)(2,1)S(1)}, bf16[4,24,256]{2,1,0:T(8,128)(2,1)S(1)}, u32[]{:S(2)}, u32[]{:S(2)}) collective-permute-start(bf16[4,24,256]{2,1,0:T(8,128)(2,1)S(1)} %get-tuple-element.27), channel_id=1, source_target_pairs={{1,2},{2,1},{3,4},{4,3},{5,6},{6,5},{7,8},{8,7},{9,10},{10,9},{11,... | collective-permute-start | bytes 147464 | tf_op jit(solution)/shard_map/ppermute | solution.py:443
  39.7 1.9 %collective-permute-start.3 = (bf16[4,24,256]{2,1,0:T(8,128)(2,1)S(1)}, bf16[4,24,256]{2,1,0:T(8,128)(2,1)S(1)}, u32[]{:S(2)}, u32[]{:S(2)}) collective-permute-start(bf16[4,24,256]{2,1,0:T(8,128)(2,1)S(1)} %get-tuple-element.28), channel_id=1, source_target_pairs={{0,1},{1,0},{2,3},{3,2},{4,5},{5,4},{6,7},{7,6},{8,9},{9,8},{10,11... | collective-permute-start | bytes 147464 | tf_op jit(solution)/shard_map/ppermute | solution.py:443
  41.6 0.0 copy-start.7
  41.6 0.0 copy-start.8
  41.7 0.0 copy-start.9
  41.7 0.0 copy-done.5
  41.7 0.0 copy-done.6
  41.7 0.0 copy-done.3
  41.7 0.0 copy-done.4
  41.7 0.6 %copy-done.7 = f32[64]{0:T(128)S(1)} copy-done((f32[64]{0:T(128)S(1)}, f32[64]{0:T(128)}, u32[]{:S(2)}) %copy-start.7) | copy-done | bytes 280
  42.3 0.0 copy-done.8
  42.3 0.0 copy-done.9
  42.3 0.0 copy-start.2
  42.3 2.3 %shard_map.137 = (bf16[192,240]{1,0:T(8,128)(2,1)S(1)}, bf16[192,192]{1,0:T(8,128)(2,1)S(1)}, bf16[192,192]{1,0:T(8,128)(2,1)S(1)}, bf16[96,768]{1,0:T(8,128)(2,...) custom-call(s32[1]{0:T(128)S(6)} %copy.17.level, ...), custom_call_target="tpu_custom_call" | custom-call | flops 8000000000 | bytes 1000000 | tf_op jit(solution)/shard_map/pallas_call | solution.py:262
  44.7 0.0 copy-start.1
  44.7 2.1 %collective-permute-done.2 = bf16[4,24,256]{2,1,0:T(8,128)(2,1)S(1)} collective-permute-done((bf16[4,24,256]{2,1,0:T(8,128)(2,1)S(1)}, bf16[4,24,256]{2,1,0:T(8,128)(2,1)S(1)}, u32[]{:S(2)}, u32[]{:S(2)}) %collective-permute-start.2) | collective-permute-done | bytes 49184 | tf_op jit(solution)/shard_map/ppermute | solution.py:443
  46.8 0.0 collective-permute-done.3
  46.8 0.0 all-to-all-done.got_far
  46.8 0.0 copy-done.2
  46.8 0.0 copy-done.1
  46.9 3.7 %shard_map.138 = f32[8,16,256]{2,1,0:T(8,128)} custom-call(s32[1]{0:T(128)S(6)} %copy.17.level, bf16[16,8,256]{2,1,0:T(8,128)(2,1)S(1)} %copy-done, bf16[16,8,256]{2,1,0:T(8,128)(2,1)S(1)} %collective-permute-done.t2, bf16[16,8,256]{2,1,0:T(8,128)(2,1)S(1)} %collective-permute-done.1.t1, bf16[8,24,256]{2,1,0:T(8,128)(2,1)S(1)} %pad_maximum_fusion.edges, ...), custom_call_target="tpu_custom_call" | custom-call | flops 4000000000 | bytes 1000000 | tf_op jit(solution)/shard_map/pallas_call | solution.py:409
  (5 shorter events, 0.0 us)
Async XLA Ops:
  2.5 29.1 %collective-permute-start = (bf16[16,8,256]{2,1,0:T(8,128)(2,1)}, bf16[16,8,256]{2,1,0:T(8,128)(2,1)S(1)}, u32[]{:S(2)}, u32[]{:S(2)}) collective-permute-start(bf16[16,8,256]{2,1,0:T(8,128)(2,1)} %get-tuple-element.16.own), channel_id=1, source_target_pairs={{64,128},{128,64},{192,256},{256,192},{320,384},{384,320},{65,129}... | collective-permute-start | bytes 196616 | tf_op jit(solution)/shard_map/ppermute | solution.py:443
  4.9 26.8 %collective-permute-start.1 = (bf16[16,8,256]{2,1,0:T(8,128)(2,1)}, bf16[16,8,256]{2,1,0:T(8,128)(2,1)S(1)}, u32[]{:S(2)}, u32[]{:S(2)}) collective-permute-start(bf16[16,8,256]{2,1,0:T(8,128)(2,1)} %get-tuple-element.16.own), channel_id=1, source_target_pairs={{0,64},{64,0},{128,192},{192,128},{256,320},{320,256},{384,448},{4... | collective-permute-start | bytes 196616 | tf_op jit(solution)/shard_map/ppermute | solution.py:443
  21.1 25.7 %all-to-all-start = ((f32[64,1,128]{2,1,0:T(1,128)}), f32[64,1,128]{2,1,0:T(1,128)S(1)}, u32[]{:S(2)}, u32[]{:S(2)}) async-start(f32[64,1,128]{2,1,0:T(1,128)} %get-tuple-element.26), calls=%async_computation | async-start | bytes 65536 | tf_op jit(solution)/shard_map/all_to_all | solution.py:474
  31.6 0.8 %copy-start = (bf16[16,8,256]{2,1,0:T(8,128)(2,1)S(1)}, bf16[16,8,256]{2,1,0:T(8,128)(2,1)}, u32[]{:S(2)}) copy-start(bf16[16,8,256]{2,1,0:T(8,128)(2,1)} %get-tuple-element.16.own) | copy-start | bytes 196612
  32.5 9.2 %copy-start.5 = (bf16[3,64,48]{1,2,0:T(8,128)(2,1)S(1)}, bf16[3,64,48]{1,2,0:T(8,128)(2,1)}, u32[]{:S(2)}) copy-start(bf16[3,64,48]{1,2,0:T(8,128)(2,1)} %param.21) | copy-start | bytes 55300
  32.5 9.2 %copy-start.6 = (bf16[3,16,192]{2,1,0:T(8,128)(2,1)S(1)}, bf16[3,16,192]{2,1,0:T(8,128)(2,1)}, u32[]{:S(2)}) copy-start(bf16[3,16,192]{2,1,0:T(8,128)(2,1)} %conv_out.1) | copy-start | bytes 55300
  32.5 9.2 %copy-start.3 = (bf16[3,64,192]{2,1,0:T(8,128)(2,1)S(1)}, bf16[3,64,192]{2,1,0:T(8,128)(2,1)}, u32[]{:S(2)}) copy-start(bf16[3,64,192]{2,1,0:T(8,128)(2,1)} %conv_mid.1) | copy-start | bytes 221188
  32.5 9.2 %copy-start.4 = (bf16[3,64,192]{2,1,0:T(8,128)(2,1)S(1)}, bf16[3,64,192]{2,1,0:T(8,128)(2,1)}, u32[]{:S(2)}) copy-start(bf16[3,64,192]{2,1,0:T(8,128)(2,1)} %conv_res.1) | copy-start | bytes 221188
  32.6 14.3 %collective-permute-start.2 = (bf16[4,24,256]{2,1,0:T(8,128)(2,1)S(1)}, bf16[4,24,256]{2,1,0:T(8,128)(2,1)S(1)}, u32[]{:S(2)}, u32[]{:S(2)}) collective-permute-start(bf16[4,24,256]{2,1,0:T(8,128)(2,1)S(1)} %get-tuple-element.27), channel_id=1, source_target_pairs={{1,2},{2,1},{3,4},{4,3},{5,6},{6,5},{7,8},{8,7},{9,10},{10,9},{11,... | collective-permute-start | bytes 147464 | tf_op jit(solution)/shard_map/ppermute | solution.py:443
  39.7 7.1 %collective-permute-start.3 = (bf16[4,24,256]{2,1,0:T(8,128)(2,1)S(1)}, bf16[4,24,256]{2,1,0:T(8,128)(2,1)S(1)}, u32[]{:S(2)}, u32[]{:S(2)}) collective-permute-start(bf16[4,24,256]{2,1,0:T(8,128)(2,1)S(1)} %get-tuple-element.28), channel_id=1, source_target_pairs={{0,1},{1,0},{2,3},{3,2},{4,5},{5,4},{6,7},{7,6},{8,9},{9,8},{10,11... | collective-permute-start | bytes 147464 | tf_op jit(solution)/shard_map/ppermute | solution.py:443
  41.6 0.7 %copy-start.7 = (f32[64]{0:T(128)S(1)}, f32[64]{0:T(128)}, u32[]{:S(2)}) copy-start(f32[64]{0:T(128)} %param.25) | copy-start | bytes 772
  41.6 0.7 %copy-start.8 = (f32[64]{0:T(128)S(1)}, f32[64]{0:T(128)}, u32[]{:S(2)}) copy-start(f32[64]{0:T(128)} %param.26) | copy-start | bytes 772
  41.7 0.7 %copy-start.9 = (f32[64]{0:T(128)S(1)}, f32[64]{0:T(128)}, u32[]{:S(2)}) copy-start(f32[64]{0:T(128)} %param.27) | copy-start | bytes 772
  42.3 4.5 %copy-start.2 = (f32[4,2,16,256]{3,2,1,0:T(8,128)S(1)}, f32[4,2,16,256]{3,2,1,0:T(8,128)}, u32[]{:S(2)}) copy-start(f32[4,2,16,256]{3,2,1,0:T(8,128)} %param.15) | copy-start | bytes 393220
  44.7 2.2 %copy-start.1 = (f32[4,2,16,256]{3,2,1,0:T(8,128)S(1)}, f32[4,2,16,256]{3,2,1,0:T(8,128)}, u32[]{:S(2)}) copy-start(f32[4,2,16,256]{3,2,1,0:T(8,128)} %param.14) | copy-start | bytes 393220

commit v5 on v4

--- a/solution.py
+++ b/solution.py
@@ -129,11 +129,14 @@
         store_taps(x2, at + r, shifts(silu_half(acc[r * 64 : (r + 1) * 64] + bias)))
 
 
-def summed(weight, x, at, rows, done):
+def pieces_of(*sources):
+    return [ref.at[(at + k) * 192 : (at + k + 1) * 192] for ref, at, rows in sources for k in range(rows)]
+
+
+def summed(weight, pieces, done):
     held = []
-    for y in range(rows + 2):
-        piece = x[(at + y) * 192 : (at + y + 1) * 192, :]
-        held.append(jnp.dot(weight, piece, preferred_element_type=F32))
+    for y, piece in enumerate(pieces):
+        held.append(jnp.dot(weight, piece[...], preferred_element_type=F32))
         if y >= 2:
             a, b, c = held[y - 2 :]
             done(y - 2, a[128:] + b[64:128] + c[:64])
@@ -158,11 +161,35 @@
         den[:, row + r, :] = res[r * 8 : (r + 1) * 8]
 
 
+def station_sums(got):
+    wide = got[:, 0, :].T
+    table = jnp.concatenate([wide[k * 16 : (k + 1) * 16] for k in range(8)], axis=1)
+    slots = table.shape[1]
+    masks = (
+        lax.broadcasted_iota(jnp.int32, (16, slots), 0) == table[9:10].astype(jnp.int32)
+    )
+    cols = jnp.where(
+        lax.broadcasted_iota(jnp.int32, (256, slots), 0) == table[10:11].astype(jnp.int32),
+        1.0,
+        0.0,
+    ).astype(BF)
+    left = jnp.concatenate(
+        [jnp.where(masks, table[v : v + 1], 0.0) for v in range(9)], axis=0
+    )
+    total = None
+    for part in parts_of(left):
+        piece = lax.dot_general(
+            part, cols, (((1,), (1,)), ((), ())), preferred_element_type=F32
+        )
+        total = piece if total is None else total + piece
+    return total
+
+
 def inner_body(
     level,
     own,
+    t1,
     t2,
-    t1,
     conv_in,
     conv_mid,
     conv_res,
@@ -175,8 +202,9 @@
     wr_out,
     wo_out,
     columns,
-    first,
-    second,
+    x1_edge,
+    x2_edge,
+    x3_edge,
     x4_edge,
     den,
     x1,
@@ -244,16 +272,20 @@
         row_in(x1, y, even_t, own[y], t1[y], t2[y])
     for at, new in ((0, 3), (3, 3), (6, 3), (9, 3), (11, 2)):
         first_rows(w1, bias, x1, x2, at, new)
-    summed(wm, x2, 0, 12, lambda y, m: store_taps(x3, y, shifts(normed(m, gain))))
-    summed(
-        wr, x3, 0, 10, lambda y, h: store_third(x4, y, x2[(y + 2) * 192 + 64 : (y + 2) * 192 + 128, :], h)
-    )
+    summed(wm, pieces_of((x2, 0, 14)), lambda y, m: store_taps(x3, y, shifts(normed(m, gain))))
+
+    def last(y, h):
+        store_third(x4, y, x2[(y + 2) * 192 + 64 : (y + 2) * 192 + 128, :], h)
+
+    summed(wr, pieces_of((x3, 0, 12)), last)
     for g in range(2):
         out_rows(wo, x4, g * 4, den, g * 4)
-    for k, y in enumerate((0, 1, 12, 13)):
-        first[k] = x2[y * 192 + 64 : y * 192 + 128, :]
-    for k, y in enumerate((0, 1, 10, 11)):
-        second[k] = x3[y * 192 + 64 : y * 192 + 128, :]
+    x1_edge[:96] = x1[:96]
+    x1_edge[96:] = x1[14 * 48 :]
+    x2_edge[:384] = x2[:384]
+    x2_edge[384:] = x2[12 * 192 :]
+    x3_edge[:384] = x3[:384]
+    x3_edge[384:] = x3[10 * 192 :]
     x4_edge[:256] = x4[:256]
     x4_edge[256:] = x4[8 * 128 :]
 
@@ -267,13 +299,14 @@
             jax.ShapeDtypeStruct((192, 192), BF),
             jax.ShapeDtypeStruct((96, 768), BF),
             jax.ShapeDtypeStruct((2, 64, 128), F32),
-            jax.ShapeDtypeStruct((4, 64, 512), BF),
-            jax.ShapeDtypeStruct((4, 64, 512), BF),
+            jax.ShapeDtypeStruct((4 * 48, 512), BF),
+            jax.ShapeDtypeStruct((4 * 192, 512), BF),
+            jax.ShapeDtypeStruct((4 * 192, 512), BF),
             jax.ShapeDtypeStruct((512, 256), BF),
             jax.ShapeDtypeStruct((8, 8, 256), F32),
         ),
         in_specs=[SM] + [VM] * 10,
-        out_specs=(VM,) * 9,
+        out_specs=(VM,) * 10,
         scratch_shapes=[
             pltpu.VMEM((16 * 48, 512), BF),
             pltpu.VMEM((14 * 192, 512), BF),
@@ -289,22 +322,20 @@
 
 def outer_body(
     level,
-    own,
-    t2,
-    t1,
     edges,
     w1,
     wm,
     wr,
     wo,
     columns,
-    first,
-    second,
+    x1_edge,
+    x2_edge,
+    x3_edge,
     x4_edge,
     den_inner,
+    got,
     noisy_far,
     fresh_far,
-    got_far,
     out,
     x1,
     x2,
@@ -313,17 +344,17 @@
     den,
     noisy,
     fresh,
-    got,
     sems,
 ):
     copies = [
         pltpu.make_async_copy(far, near, sems.at[k])
-        for k, (far, near) in enumerate(((noisy_far, noisy), (fresh_far, fresh), (got_far, got)))
+        for k, (far, near) in enumerate(((noisy_far, noisy), (fresh_far, fresh)))
     ]
     for copy in copies:
         copy.start()
     even_t = lax.axis_index("tm") % 2 == 0
     even_s = lax.axis_index("space") % 2 == 0
+    total = station_sums(got)
     bias = columns[0][:, :1]
     gain = columns[1][:, :1]
 
@@ -331,13 +362,9 @@
         u, v = edges[4 + y].astype(F32), edges[y].astype(F32)
         top = jnp.where(even_s, v, u)
         low = jnp.where(even_s, u, v)
-        row_in(x1, y, even_t, top[16:], top[8:16], top[:8])
-        row_in(x1, 8 + y, even_t, low[16:], low[8:16], low[:8])
-    for y, row in ((0, 4), (1, 5), (14, 6), (15, 7)):
-        row_in(x1, row, even_t, own[y], t1[y], t2[y])
-    for k, row in enumerate((4, 5, 6, 7)):
-        store_taps(x2, row, shifts(first[k]))
-        store_taps(x3, row, shifts(second[k]))
+        row_in(x1, y, even_t, top[:8], top[16:], top[8:16])
+        row_in(x1, 8 + y, even_t, low[:8], low[16:], low[8:16])
+    x1[4 * 48 : 8 * 48, :] = x1_edge[...]
     x4[4 * 128 : 8 * 128, :] = x4_edge[...]
 
     acc = [
@@ -349,53 +376,33 @@
         (1, 0, 1),
         (2, 0, 2),
         (3, 1, 2),
-        (8, 2, 0),
-        (9, 2, 1),
-        (10, 2, 2),
-        (11, 3, 2),
+        (4, 2, 0),
+        (5, 2, 1),
+        (6, 2, 2),
+        (7, 3, 2),
     ):
         store_taps(x2, row, shifts(silu_half(acc[k][r * 64 : (r + 1) * 64] + bias)))
 
     def middle(at):
         return lambda y, m: store_taps(x3, at + y, shifts(normed(m, gain)))
 
-    def last(at, from_first):
+    def last(at, ref, from_first, more):
         def done(y, h):
-            row = from_first + y
-            store_third(x4, at + y, x2[row * 192 + 64 : row * 192 + 128, :], h)
+            source, row = (ref, from_first + y) if y < 2 else (more, y - 2)
+            store_third(x4, at + y, source[row * 192 + 64 : row * 192 + 128, :], h)
 
         return done
 
-    summed(wm[...], x2, 0, 4, middle(0))
-    summed(wm[...], x2, 6, 4, middle(8))
-    summed(wr[...], x3, 0, 4, last(0, 2))
-    summed(wr[...], x3, 6, 4, last(8, 6))
+    summed(wm[...], pieces_of((x2, 0, 4), (x2_edge, 0, 2)), middle(0))
+    summed(wm[...], pieces_of((x2_edge, 2, 2), (x2, 4, 4)), middle(4))
+    summed(wr[...], pieces_of((x3, 0, 4), (x3_edge, 0, 2)), last(0, x2, 2, x2_edge))
+    summed(wr[...], pieces_of((x3_edge, 2, 2), (x3, 4, 4)), last(8, x2_edge, 2, x2.at[4 * 192 :]))
     out_rows(wo[...], x4, 0, den, 0)
     den[:, 4:12, :] = den_inner[...]
     out_rows(wo[...], x4, 6, den, 12)
 
     for copy in copies:
         copy.wait()
-    wide = got[:, 0, :].T
-    table = jnp.concatenate([wide[k * 16 : (k + 1) * 16] for k in range(8)], axis=1)
-    slots = table.shape[1]
-    masks = (
-        lax.broadcasted_iota(jnp.int32, (16, slots), 0) == table[9:10].astype(jnp.int32)
-    )
-    cols = jnp.where(
-        lax.broadcasted_iota(jnp.int32, (256, slots), 0) == table[10:11].astype(jnp.int32),
-        1.0,
-        0.0,
-    ).astype(BF)
-    left = jnp.concatenate(
-        [jnp.where(masks, table[v : v + 1], 0.0) for v in range(9)], axis=0
-    )
-    total = None
-    for part in parts_of(left):
-        piece = lax.dot_general(
-            part, cols, (((1,), (1,)), ((), ())), preferred_element_type=F32
-        )
-        total = piece if total is None else total + piece
     scale = scale_at(level[0], (16, 256))
     after = scale_at(level[0] - 1, (16, 256))
     square = scale * scale
@@ -409,18 +416,17 @@
     return pl.pallas_call(
         outer_body,
         out_shape=jax.ShapeDtypeStruct((8, 16, 256), F32),
-        in_specs=[SM] + [VM] * 13 + [ANY] * 3,
+        in_specs=[SM] + [VM] * 12 + [ANY] * 2,
         out_specs=VM,
         scratch_shapes=[
             pltpu.VMEM((12 * 48, 512), BF),
-            pltpu.VMEM((12 * 192, 512), BF),
-            pltpu.VMEM((12 * 192, 512), BF),
+            pltpu.VMEM((8 * 192, 512), BF),
+            pltpu.VMEM((8 * 192, 512), BF),
             pltpu.VMEM((12 * 128, 256), BF),
             pltpu.VMEM((8, 16, 256), F32),
             pltpu.VMEM((8, 16, 256), F32),
             pltpu.VMEM((8, 16, 256), F32),
-            pltpu.VMEM((64, 1, 128), F32),
-            pltpu.SemaphoreType.DMA((3,)),
+            pltpu.SemaphoreType.DMA((2,)),
         ],
         compiler_params=pltpu.CompilerParams(vmem_limit_bytes=40 * 2**20),
         cost_estimate=pl.CostEstimate(
@@ -469,14 +475,14 @@
         station_owner.reshape(1, 128),
         station_cell.reshape(1, 128),
     )
+    t1 = swapped(own, "tm", 0)
     t2 = swapped(own, "tm", 1)
-    t1 = swapped(own, "tm", 0)
     got = lax.all_to_all(
         slots, "space", 0, 0, axis_index_groups=[order_of(slots.shape[0])], tiled=True
     )
 
     edge = jnp.where(even_s, 12, 0)
-    both = jnp.concatenate([t2, t1, own], axis=1)
+    both = jnp.concatenate([own, t2, t1], axis=1)
     m2 = swapped(lax.dynamic_slice_in_dim(both, 12 - edge, 4, 0), "space", 1)
     m1 = swapped(lax.dynamic_slice_in_dim(both, edge, 4, 0), "space", 0)
 
@@ -484,8 +490,8 @@
     held = inner(
         level_index,
         own,
+        t1,
         t2,
-        t1,
         conv_in.transpose(0, 2, 1),
         conv_mid,
         conv_res,
@@ -495,7 +501,7 @@
         norm_gain.reshape(1, 64),
     )
     result = outer(
-        level_index, own, t2, t1, edges, *held, noisy, fresh_noise.reshape(8, 16, 256), got
+        level_index, edges, *held, got, noisy, fresh_noise.reshape(8, 16, 256)
     )
     return result.reshape(noisy_state.shape)
 

time: 50.9 us -> 50.1 us (0.984)
  the two profiles are of different devices: /device:TPU:16 before, /device:TPU:24 now
where the time goes in v5:
time: 50.1 us; the launch traced here: 49.8 us
  starting transfers between devices  38.6 us (77%)
  Pallas kernels  7.52 us (15%)
  waiting for transfers between devices  2.09 us (4%)
  between operations  0.9 us (2%)
  local copies, waits for them, and re-layouts  0.7 us (1%)
    ppermute x4, starting transfers between devices, swapped(): return lax.ppermute(value, axis, pairs)  28.1 us
    all_to_all x1, starting transfers between devices, local(): lax.all_to_all(slots, 'space', 0, 0, axis_index_groups=[order_of(slots.sh...  10.5 us
    pallas_call x1, Pallas kernels, outer(): pl.pallas_call(outer_body, out_shape=jax.ShapeDtypeStruct((8, 16, 256), F...  3.28 us
    pallas_call x1, Pallas kernels, inner(): pl.pallas_call(inner_body, out_shape=(jax.ShapeDtypeStruct((192, 240), BF...  2.37 us
    ppermute x4, waiting for transfers between devices, swapped(): return lax.ppermute(value, axis, pairs)  2.09 us
    pallas_call x1, Pallas kernels, pack(): pl.pallas_call(pack_body, out_shape=(jax.ShapeDtypeStruct((16, 8, 256), B...  1.87 us
  transfers between devices with their start and end apart: 5, of which 1 were waited for; matrix products, arithmetic and copies ran while one was open for 0% of the time, Pallas kernels for 5%

profile of v5, /device:TPU:24, one launch (start us, length us, event | category | flops | bytes accessed | tf_op | source)
XLA Modules:
  0.0 49.8 jit_solution(14891319452233321110)
XLA Ops:
  0.7 1.9 %shard_map.136 = (bf16[16,8,256]{2,1,0:T(8,128)(2,1)}, f32[64,1,128]{2,1,0:T(1,128)}) custom-call(s32[1]{0:T(128)S(6)} %copy.17.level, f32[8,16,256]{2,1,0:T(8,128)} %bitcast.10, f32[4,2,128]{2,1,0:T(2,128)} %obs.1, f32[1,128]{1,0:T(1,128)} %bitcast.17, s32[1,128]{1,0:T(1,128)} %bitcast.18, s32[1,128]{1,0:T(1,128)} %bitcast.19), custom_call_target="tpu_custom_call" | custom-call | flops 50000000 | bytes 400000 | tf_op jit(solution)/shard_map/pallas_call | solution.py:86
  2.5 0.0 copy-start
  2.5 2.8 %collective-permute-start.1 = (bf16[16,8,256]{2,1,0:T(8,128)(2,1)}, bf16[16,8,256]{2,1,0:T(8,128)(2,1)S(1)}, u32[]{:S(2)}, u32[]{:S(2)}) collective-permute-start(bf16[16,8,256]{2,1,0:T(8,128)(2,1)} %get-tuple-element.17.own), channel_id=1, source_target_pairs={{0,64},{64,0},{128,192},{192,128},{256,320},{320,256},{384,448},{4... | collective-permute-start | bytes 196616 | tf_op jit(solution)/shard_map/ppermute | solution.py:449
  5.3 16.2 %collective-permute-start = (bf16[16,8,256]{2,1,0:T(8,128)(2,1)}, bf16[16,8,256]{2,1,0:T(8,128)(2,1)S(1)}, u32[]{:S(2)}, u32[]{:S(2)}) collective-permute-start(bf16[16,8,256]{2,1,0:T(8,128)(2,1)} %get-tuple-element.17.own), channel_id=1, source_target_pairs={{64,128},{128,64},{192,256},{256,192},{320,384},{384,320},{65,129}... | collective-permute-start | bytes 196616 | tf_op jit(solution)/shard_map/ppermute | solution.py:449
  21.5 10.5 %all-to-all-start = ((f32[64,1,128]{2,1,0:T(1,128)}), f32[64,1,128]{2,1,0:T(1,128)S(1)}, u32[]{:S(2)}, u32[]{:S(2)}) async-start(f32[64,1,128]{2,1,0:T(1,128)} %get-tuple-element.28), calls=%async_computation | async-start | bytes 65536 | tf_op jit(solution)/shard_map/all_to_all | solution.py:480
  32.0 0.0 copy-done
  32.1 0.0 collective-permute-done.t2
  32.1 0.0 collective-permute-done.1.t1
  32.1 0.0 copy-start.5
  32.1 0.0 copy-start.6
  32.1 0.0 copy-start.3
  32.2 0.0 copy-start.4
  32.2 7.1 %collective-permute-start.2 = (bf16[4,24,256]{2,1,0:T(8,128)(2,1)S(1)}, bf16[4,24,256]{2,1,0:T(8,128)(2,1)S(1)}, u32[]{:S(2)}, u32[]{:S(2)}) collective-permute-start(bf16[4,24,256]{2,1,0:T(8,128)(2,1)S(1)} %get-tuple-element.29), channel_id=1, source_target_pairs={{1,2},{2,1},{3,4},{4,3},{5,6},{6,5},{7,8},{8,7},{9,10},{10,9},{11,... | collective-permute-start | bytes 147464 | tf_op jit(solution)/shard_map/ppermute | solution.py:449
  39.4 1.9 %collective-permute-start.3 = (bf16[4,24,256]{2,1,0:T(8,128)(2,1)S(1)}, bf16[4,24,256]{2,1,0:T(8,128)(2,1)S(1)}, u32[]{:S(2)}, u32[]{:S(2)}) collective-permute-start(bf16[4,24,256]{2,1,0:T(8,128)(2,1)S(1)} %get-tuple-element.30), channel_id=1, source_target_pairs={{0,1},{1,0},{2,3},{3,2},{4,5},{5,4},{6,7},{7,6},{8,9},{9,8},{10,11... | collective-permute-start | bytes 147464 | tf_op jit(solution)/shard_map/ppermute | solution.py:449
  41.3 0.0 copy-start.7
  41.3 0.0 copy-start.8
  41.3 0.0 copy-start.9
  41.3 0.0 copy-done.5
  41.3 0.0 copy-done.6
  41.3 0.0 copy-done.3
  41.3 0.0 copy-done.4
  41.4 0.6 %copy-done.7 = f32[64]{0:T(128)S(1)} copy-done((f32[64]{0:T(128)S(1)}, f32[64]{0:T(128)}, u32[]{:S(2)}) %copy-start.7) | copy-done | bytes 280
  41.9 0.0 copy-done.8
  42.0 0.0 copy-done.9
  42.0 0.0 copy-start.2
  42.0 2.4 %shard_map.137 = (bf16[192,240]{1,0:T(8,128)(2,1)S(1)}, bf16[192,192]{1,0:T(8,128)(2,1)S(1)}, bf16[192,192]{1,0:T(8,128)(2,1)S(1)}, bf16[96,768]{1,0:T(8,128)(2,...) custom-call(s32[1]{0:T(128)S(6)} %copy.17.level, ...), custom_call_target="tpu_custom_call" | custom-call | flops 8000000000 | bytes 1000000 | tf_op jit(solution)/shard_map/pallas_call | solution.py:294
  44.4 0.0 copy-start.1
  44.4 2.1 %collective-permute-done.2 = bf16[4,24,256]{2,1,0:T(8,128)(2,1)S(1)} collective-permute-done((bf16[4,24,256]{2,1,0:T(8,128)(2,1)S(1)}, bf16[4,24,256]{2,1,0:T(8,128)(2,1)S(1)}, u32[]{:S(2)}, u32[]{:S(2)}) %collective-permute-start.2) | collective-permute-done | bytes 49184 | tf_op jit(solution)/shard_map/ppermute | solution.py:449
  46.5 0.0 collective-permute-done.3
  46.5 0.0 all-to-all-done.got
  46.5 0.0 copy-done.2
  46.5 0.0 copy-done.1
  46.5 3.3 %shard_map.138 = f32[8,16,256]{2,1,0:T(8,128)} custom-call(s32[1]{0:T(128)S(6)} %copy.17.level, bf16[8,24,256]{2,1,0:T(8,128)(2,1)S(1)} %pad_maximum_fusion.edges, bf16[192,240]{1,0:T(8,128)(2,1)S(1)} %get-tuple-element.18.w1, bf16[192,192]{1,0:T(8,128)(2,1)S(1)} %get-tuple-element.19.wm, bf16[192,192]{1,0:T(8,128)(2,1)S(1)} %get-tuple-element.20.wr, ...), custom_call_target="tpu_custom_call" | custom-call | flops 4000000000 | bytes 1000000 | tf_op jit(solution)/shard_map/pallas_call | solution.py:416
  (5 shorter events, 0.0 us)
Async XLA Ops:
  2.5 29.5 %copy-start = (bf16[16,8,256]{2,1,0:T(8,128)(2,1)S(1)}, bf16[16,8,256]{2,1,0:T(8,128)(2,1)}, u32[]{:S(2)}) copy-start(bf16[16,8,256]{2,1,0:T(8,128)(2,1)} %get-tuple-element.17.own) | copy-start | bytes 196612
  2.5 29.6 %collective-permute-start.1 = (bf16[16,8,256]{2,1,0:T(8,128)(2,1)}, bf16[16,8,256]{2,1,0:T(8,128)(2,1)S(1)}, u32[]{:S(2)}, u32[]{:S(2)}) collective-permute-start(bf16[16,8,256]{2,1,0:T(8,128)(2,1)} %get-tuple-element.17.own), channel_id=1, source_target_pairs={{0,64},{64,0},{128,192},{192,128},{256,320},{320,256},{384,448},{4... | collective-permute-start | bytes 196616 | tf_op jit(solution)/shard_map/ppermute | solution.py:449
  5.3 26.8 %collective-permute-start = (bf16[16,8,256]{2,1,0:T(8,128)(2,1)}, bf16[16,8,256]{2,1,0:T(8,128)(2,1)S(1)}, u32[]{:S(2)}, u32[]{:S(2)}) collective-permute-start(bf16[16,8,256]{2,1,0:T(8,128)(2,1)} %get-tuple-element.17.own), channel_id=1, source_target_pairs={{64,128},{128,64},{192,256},{256,192},{320,384},{384,320},{65,129}... | collective-permute-start | bytes 196616 | tf_op jit(solution)/shard_map/ppermute | solution.py:449
  21.5 24.9 %all-to-all-start = ((f32[64,1,128]{2,1,0:T(1,128)}), f32[64,1,128]{2,1,0:T(1,128)S(1)}, u32[]{:S(2)}, u32[]{:S(2)}) async-start(f32[64,1,128]{2,1,0:T(1,128)} %get-tuple-element.28), calls=%async_computation | async-start | bytes 65536 | tf_op jit(solution)/shard_map/all_to_all | solution.py:480
  32.1 9.2 %copy-start.5 = (bf16[3,64,48]{1,2,0:T(8,128)(2,1)S(1)}, bf16[3,64,48]{1,2,0:T(8,128)(2,1)}, u32[]{:S(2)}) copy-start(bf16[3,64,48]{1,2,0:T(8,128)(2,1)} %param.21) | copy-start | bytes 55300
  32.1 9.2 %copy-start.6 = (bf16[3,16,192]{2,1,0:T(8,128)(2,1)S(1)}, bf16[3,16,192]{2,1,0:T(8,128)(2,1)}, u32[]{:S(2)}) copy-start(bf16[3,16,192]{2,1,0:T(8,128)(2,1)} %conv_out.1) | copy-start | bytes 55300
  32.1 9.2 %copy-start.3 = (bf16[3,64,192]{2,1,0:T(8,128)(2,1)S(1)}, bf16[3,64,192]{2,1,0:T(8,128)(2,1)}, u32[]{:S(2)}) copy-start(bf16[3,64,192]{2,1,0:T(8,128)(2,1)} %conv_mid.1) | copy-start | bytes 221188
  32.2 9.2 %copy-start.4 = (bf16[3,64,192]{2,1,0:T(8,128)(2,1)S(1)}, bf16[3,64,192]{2,1,0:T(8,128)(2,1)}, u32[]{:S(2)}) copy-start(bf16[3,64,192]{2,1,0:T(8,128)(2,1)} %conv_res.1) | copy-start | bytes 221188
  32.2 14.3 %collective-permute-start.2 = (bf16[4,24,256]{2,1,0:T(8,128)(2,1)S(1)}, bf16[4,24,256]{2,1,0:T(8,128)(2,1)S(1)}, u32[]{:S(2)}, u32[]{:S(2)}) collective-permute-start(bf16[4,24,256]{2,1,0:T(8,128)(2,1)S(1)} %get-tuple-element.29), channel_id=1, source_target_pairs={{1,2},{2,1},{3,4},{4,3},{5,6},{6,5},{7,8},{8,7},{9,10},{10,9},{11,... | collective-permute-start | bytes 147464 | tf_op jit(solution)/shard_map/ppermute | solution.py:449
  39.4 7.1 %collective-permute-start.3 = (bf16[4,24,256]{2,1,0:T(8,128)(2,1)S(1)}, bf16[4,24,256]{2,1,0:T(8,128)(2,1)S(1)}, u32[]{:S(2)}, u32[]{:S(2)}) collective-permute-start(bf16[4,24,256]{2,1,0:T(8,128)(2,1)S(1)} %get-tuple-element.30), channel_id=1, source_target_pairs={{0,1},{1,0},{2,3},{3,2},{4,5},{5,4},{6,7},{7,6},{8,9},{9,8},{10,11... | collective-permute-start | bytes 147464 | tf_op jit(solution)/shard_map/ppermute | solution.py:449
  41.3 0.7 %copy-start.7 = (f32[64]{0:T(128)S(1)}, f32[64]{0:T(128)}, u32[]{:S(2)}) copy-start(f32[64]{0:T(128)} %param.25) | copy-start | bytes 772
  41.3 0.7 %copy-start.8 = (f32[64]{0:T(128)S(1)}, f32[64]{0:T(128)}, u32[]{:S(2)}) copy-start(f32[64]{0:T(128)} %param.26) | copy-start | bytes 772
  41.3 0.7 %copy-start.9 = (f32[64]{0:T(128)S(1)}, f32[64]{0:T(128)}, u32[]{:S(2)}) copy-start(f32[64]{0:T(128)} %param.27) | copy-start | bytes 772
  42.0 4.5 %copy-start.2 = (f32[4,2,16,256]{3,2,1,0:T(8,128)S(1)}, f32[4,2,16,256]{3,2,1,0:T(8,128)}, u32[]{:S(2)}) copy-start(f32[4,2,16,256]{3,2,1,0:T(8,128)} %param.15) | copy-start | bytes 393220
  44.4 2.1 %copy-start.1 = (f32[4,2,16,256]{3,2,1,0:T(8,128)S(1)}, f32[4,2,16,256]{3,2,1,0:T(8,128)}, u32[]{:S(2)}) copy-start(f32[4,2,16,256]{3,2,1,0:T(8,128)} %param.14) | copy-start | bytes 393220

commit v6 on v5

--- a/solution.py
+++ b/solution.py
@@ -12,10 +12,10 @@
 BF = jnp.bfloat16
 F32 = jnp.float32
 OUT_GROUP = 4
+STATION_COST = 400_000_000
 INNER_COST = 8_000_000_000
 VM = pl.BlockSpec(memory_space=pltpu.VMEM)
 SM = pl.BlockSpec(memory_space=pltpu.SMEM)
-ANY = pl.BlockSpec(memory_space=pl.ANY)
 
 
 def scale_at(level, shape):
@@ -161,7 +161,7 @@
         den[:, row + r, :] = res[r * 8 : (r + 1) * 8]
 
 
-def station_sums(got):
+def station_body(level, noisy, fresh, got, base, slope):
     wide = got[:, 0, :].T
     table = jnp.concatenate([wide[k * 16 : (k + 1) * 16] for k in range(8)], axis=1)
     slots = table.shape[1]
@@ -182,14 +182,36 @@
             part, cols, (((1,), (1,)), ((), ())), preferred_element_type=F32
         )
         total = piece if total is None else total + piece
-    return total
+    scale = scale_at(level[0], (16, 256))
+    after = scale_at(level[0] - 1, (16, 256))
+    square = scale * scale
+    weight = 1.0 - square * total[128:144]
+    slope[...] = scale * weight
+    for v in range(8):
+        base[v] = noisy[v] * weight + square * total[v * 16 : (v + 1) * 16] + after * fresh[v]
+
+
+def station_terms(level, noisy, fresh, got):
+    return pl.pallas_call(
+        station_body,
+        out_shape=(
+            jax.ShapeDtypeStruct((8, 16, 256), F32),
+            jax.ShapeDtypeStruct((16, 256), F32),
+        ),
+        in_specs=[SM, VM, VM, VM],
+        out_specs=(VM, VM),
+        cost_estimate=pl.CostEstimate(
+            flops=STATION_COST, bytes_accessed=400_000, transcendentals=0
+        ),
+    )(level, noisy, fresh, got)
 
 
 def inner_body(
     level,
     own,
-    t1,
+    low,
     t2,
+    high,
     conv_in,
     conv_mid,
     conv_res,
@@ -215,6 +237,7 @@
     time_rank = lax.axis_index("tm")
     times = lax.axis_size("tm")
     even_t = time_rank % 2 == 0
+    lower = time_rank < times // 2
 
     noise64 = scale_at(level[0], (1, 64))
     bias_row = 0.5 * (in_bias[...] + noise_embed[...] * jnp.log(10.0 * noise64))
@@ -269,7 +292,7 @@
     wo_out[...] = wo
 
     for y in range(16):
-        row_in(x1, y, even_t, own[y], t1[y], t2[y])
+        row_in(x1, y, even_t, own[y], jnp.where(lower, low[y], high[y]), t2[y])
     for at, new in ((0, 3), (3, 3), (6, 3), (9, 3), (11, 2)):
         first_rows(w1, bias, x1, x2, at, new)
     summed(wm, pieces_of((x2, 0, 14)), lambda y, m: store_taps(x3, y, shifts(normed(m, gain))))
@@ -305,7 +328,7 @@
             jax.ShapeDtypeStruct((512, 256), BF),
             jax.ShapeDtypeStruct((8, 8, 256), F32),
         ),
-        in_specs=[SM] + [VM] * 10,
+        in_specs=[SM] + [VM] * 11,
         out_specs=(VM,) * 10,
         scratch_shapes=[
             pltpu.VMEM((16 * 48, 512), BF),
@@ -321,7 +344,6 @@
 
 
 def outer_body(
-    level,
     edges,
     w1,
     wm,
@@ -333,28 +355,19 @@
     x3_edge,
     x4_edge,
     den_inner,
-    got,
-    noisy_far,
-    fresh_far,
+    base,
+    slope,
     out,
     x1,
     x2,
     x3,
     x4,
     den,
-    noisy,
-    fresh,
-    sems,
 ):
-    copies = [
-        pltpu.make_async_copy(far, near, sems.at[k])
-        for k, (far, near) in enumerate(((noisy_far, noisy), (fresh_far, fresh)))
-    ]
-    for copy in copies:
-        copy.start()
-    even_t = lax.axis_index("tm") % 2 == 0
+    time_rank = lax.axis_index("tm")
+    even_t = time_rank % 2 == 0
+    lower = time_rank < lax.axis_size("tm") // 2
     even_s = lax.axis_index("space") % 2 == 0
-    total = station_sums(got)
     bias = columns[0][:, :1]
     gain = columns[1][:, :1]
 
@@ -362,8 +375,8 @@
         u, v = edges[4 + y].astype(F32), edges[y].astype(F32)
         top = jnp.where(even_s, v, u)
         low = jnp.where(even_s, u, v)
-        row_in(x1, y, even_t, top[:8], top[16:], top[8:16])
-        row_in(x1, 8 + y, even_t, low[:8], low[16:], low[8:16])
+        row_in(x1, y, even_t, top[:8], jnp.where(lower, top[8:16], top[24:]), top[16:24])
+        row_in(x1, 8 + y, even_t, low[:8], jnp.where(lower, low[8:16], low[24:]), low[16:24])
     x1[4 * 48 : 8 * 48, :] = x1_edge[...]
     x4[4 * 128 : 8 * 128, :] = x4_edge[...]
 
@@ -401,22 +414,15 @@
     den[:, 4:12, :] = den_inner[...]
     out_rows(wo[...], x4, 6, den, 12)
 
-    for copy in copies:
-        copy.wait()
-    scale = scale_at(level[0], (16, 256))
-    after = scale_at(level[0] - 1, (16, 256))
-    square = scale * scale
-    weight = 1.0 - square * total[128:144]
     for v in range(8):
-        estimate = noisy[v] - scale * den[v]
-        out[v] = estimate * weight + square * total[v * 16 : (v + 1) * 16] + after * fresh[v]
-
-
-def outer(level, *arrays):
+        out[v] = base[v] - slope[...] * den[v]
+
+
+def outer(*arrays):
     return pl.pallas_call(
         outer_body,
         out_shape=jax.ShapeDtypeStruct((8, 16, 256), F32),
-        in_specs=[SM] + [VM] * 12 + [ANY] * 2,
+        in_specs=[VM] * 13,
         out_specs=VM,
         scratch_shapes=[
             pltpu.VMEM((12 * 48, 512), BF),
@@ -424,26 +430,23 @@
             pltpu.VMEM((8 * 192, 512), BF),
             pltpu.VMEM((12 * 128, 256), BF),
             pltpu.VMEM((8, 16, 256), F32),
-            pltpu.VMEM((8, 16, 256), F32),
-            pltpu.VMEM((8, 16, 256), F32),
-            pltpu.SemaphoreType.DMA((2,)),
         ],
         compiler_params=pltpu.CompilerParams(vmem_limit_bytes=40 * 2**20),
         cost_estimate=pl.CostEstimate(
             flops=4_000_000_000, bytes_accessed=1_000_000, transcendentals=1_000_000
         ),
-    )(level, *arrays)
+    )(*arrays)
 
 
 def order_of(count):
     return [(k + LEADER) % count for k in range(count)]
 
 
-def swapped(value, axis, first):
+def swapped(value, axis, first, stop=None):
     count = lax.axis_size(axis)
     wrap = axis == "space"
     pairs = []
-    for i in range(first, count if wrap else count - 1, 2):
+    for i in range(first, count if wrap else stop or count - 1, 2):
         j = (i + 1) % count
         pairs += [(i, j), (j, i)]
     return lax.ppermute(value, axis, pairs)
@@ -475,14 +478,16 @@
         station_owner.reshape(1, 128),
         station_cell.reshape(1, 128),
     )
-    t1 = swapped(own, "tm", 0)
+    half = lax.axis_size("tm") // 2
+    low = swapped(own, "tm", 0, half)
     t2 = swapped(own, "tm", 1)
+    high = swapped(own, "tm", half)
     got = lax.all_to_all(
         slots, "space", 0, 0, axis_index_groups=[order_of(slots.shape[0])], tiled=True
     )
 
     edge = jnp.where(even_s, 12, 0)
-    both = jnp.concatenate([own, t2, t1], axis=1)
+    both = jnp.concatenate([own, low, t2, high], axis=1)
     m2 = swapped(lax.dynamic_slice_in_dim(both, 12 - edge, 4, 0), "space", 1)
     m1 = swapped(lax.dynamic_slice_in_dim(both, edge, 4, 0), "space", 0)
 
@@ -490,8 +495,9 @@
     held = inner(
         level_index,
         own,
-        t1,
+        low,
         t2,
+        high,
         conv_in.transpose(0, 2, 1),
         conv_mid,
         conv_res,
@@ -500,9 +506,8 @@
         noise_embed.reshape(1, 64),
         norm_gain.reshape(1, 64),
     )
-    result = outer(
-        level_index, edges, *held, got, noisy, fresh_noise.reshape(8, 16, 256)
-    )
+    base, slope = station_terms(level_index, noisy, fresh_noise.reshape(8, 16, 256), got)
+    result = outer(edges, *held, base, slope)
     return result.reshape(noisy_state.shape)
 
 

time: 50.1 us -> 49.7 us (level)
  the two profiles are of different devices: /device:TPU:24 before, /device:TPU:25 now
where the time goes in v6:
time: 49.7 us; the launch traced here: 49.3 us
  starting transfers between devices  37.1 us (75%)
  Pallas kernels  9.14 us (18%)
  local copies, waits for them, and re-layouts  2.16 us (4%)
  between operations  0.92 us (2%)
    ppermute x5, starting transfers between devices, swapped(): return lax.ppermute(value, axis, pairs)  26 us
    all_to_all x1, starting transfers between devices, local(): lax.all_to_all(slots, 'space', 0, 0, axis_index_groups=[order_of(slots.sh...  11.1 us
    pallas_call x1, Pallas kernels, outer(): pl.pallas_call(outer_body, out_shape=jax.ShapeDtypeStruct((8, 16, 256), F...  2.65 us
    pallas_call x1, Pallas kernels, inner(): pl.pallas_call(inner_body, out_shape=(jax.ShapeDtypeStruct((192, 240), BF...  2.4 us
    pallas_call x1, Pallas kernels, station_terms(): pl.pallas_call(station_body, out_shape=(jax.ShapeDtypeStruct((8, 16, 256)...  2.22 us
    unnamed x25, local copies, waits for them, and re-layouts  2.14 us
    pallas_call x1, Pallas kernels, pack(): pl.pallas_call(pack_body, out_shape=(jax.ShapeDtypeStruct((16, 8, 256), B...  1.86 us
  transfers between devices with their start and end apart: 6, of which 0 were waited for; matrix products, arithmetic and copies ran while one was open for 0% of the time, Pallas kernels for 9%

profile of v6, /device:TPU:25, one launch (start us, length us, event | category | flops | bytes accessed | tf_op | source)
XLA Modules:
  0.0 49.3 jit_solution(7175261531090150578)
XLA Ops:
  0.7 1.9 %shard_map.136 = (bf16[16,8,256]{2,1,0:T(8,128)(2,1)}, f32[64,1,128]{2,1,0:T(1,128)}) custom-call(s32[1]{0:T(128)S(6)} %copy.18.level, f32[8,16,256]{2,1,0:T(8,128)} %bitcast.14, f32[4,2,128]{2,1,0:T(2,128)} %obs.1, f32[1,128]{1,0:T(1,128)} %bitcast.17, s32[1,128]{1,0:T(1,128)} %bitcast.18, s32[1,128]{1,0:T(1,128)} %bitcast.19), custom_call_target="tpu_custom_call" | custom-call | flops 50000000 | bytes 400000 | tf_op jit(solution)/shard_map/pallas_call | solution.py:86
  2.5 0.0 copy-start
  2.5 2.5 %collective-permute-start = (bf16[16,8,256]{2,1,0:T(8,128)(2,1)}, bf16[16,8,256]{2,1,0:T(8,128)(2,1)S(1)}, u32[]{:S(2)}, u32[]{:S(2)}) collective-permute-start(bf16[16,8,256]{2,1,0:T(8,128)(2,1)} %get-tuple-element.19.own), channel_id=1, source_target_pairs={{0,64},{64,0},{128,192},{192,128},{1,65},{65,1},{129,193},{193,129... | collective-permute-start | bytes 196616 | tf_op jit(solution)/shard_map/ppermute | solution.py:452
  5.0 13.4 %collective-permute-start.1 = (bf16[16,8,256]{2,1,0:T(8,128)(2,1)}, bf16[16,8,256]{2,1,0:T(8,128)(2,1)S(1)}, u32[]{:S(2)}, u32[]{:S(2)}) collective-permute-start(bf16[16,8,256]{2,1,0:T(8,128)(2,1)} %get-tuple-element.19.own), channel_id=1, source_target_pairs={{64,128},{128,64},{192,256},{256,192},{320,384},{384,320},{65,129}... | collective-permute-start | bytes 196616 | tf_op jit(solution)/shard_map/ppermute | solution.py:452
  18.4 0.7 %collective-permute-start.2 = (bf16[16,8,256]{2,1,0:T(8,128)(2,1)}, bf16[16,8,256]{2,1,0:T(8,128)(2,1)S(1)}, u32[]{:S(2)}, u32[]{:S(2)}) collective-permute-start(bf16[16,8,256]{2,1,0:T(8,128)(2,1)} %get-tuple-element.19.own), channel_id=1, source_target_pairs={{256,320},{320,256},{384,448},{448,384},{257,321},{321,257},{385,4... | collective-permute-start | bytes 196616 | tf_op jit(solution)/shard_map/ppermute | solution.py:452
  19.1 11.1 %all-to-all-start = ((f32[64,1,128]{2,1,0:T(1,128)}), f32[64,1,128]{2,1,0:T(1,128)S(1)}, u32[]{:S(2)}, u32[]{:S(2)}) async-start(f32[64,1,128]{2,1,0:T(1,128)} %get-tuple-element.30), calls=%async_computation | async-start | bytes 65536 | tf_op jit(solution)/shard_map/all_to_all | solution.py:485
  30.2 0.0 copy-done
  30.2 0.0 collective-permute-done.low
  30.3 0.0 collective-permute-done.1.t2
  30.3 0.0 collective-permute-done.2.high
  30.3 0.0 copy-start.1
  30.3 0.0 copy-start.2
  30.3 0.0 copy-start.3
  30.3 0.0 copy-start.4
  30.4 2.6 %collective-permute-start.3 = (bf16[4,32,256]{2,1,0:T(8,128)(2,1)S(1)}, bf16[4,32,256]{2,1,0:T(8,128)(2,1)S(1)}, u32[]{:S(2)}, u32[]{:S(2)}) collective-permute-start(bf16[4,32,256]{2,1,0:T(8,128)(2,1)S(1)} %get-tuple-element.33), channel_id=1, source_target_pairs={{1,2},{2,1},{3,4},{4,3},{5,6},{6,5},{7,8},{8,7},{9,10},{10,9},{11,... | collective-permute-start | bytes 196616 | tf_op jit(solution)/shard_map/ppermute | solution.py:452
  33.0 6.8 %collective-permute-start.4 = (bf16[4,32,256]{2,1,0:T(8,128)(2,1)S(1)}, bf16[4,32,256]{2,1,0:T(8,128)(2,1)S(1)}, u32[]{:S(2)}, u32[]{:S(2)}) collective-permute-start(bf16[4,32,256]{2,1,0:T(8,128)(2,1)S(1)} %get-tuple-element.34), channel_id=1, source_target_pairs={{0,1},{1,0},{2,3},{3,2},{4,5},{5,4},{6,7},{7,6},{8,9},{9,8},{10,11... | collective-permute-start | bytes 196616 | tf_op jit(solution)/shard_map/ppermute | solution.py:452
  39.8 0.0 copy-start.5
  39.8 0.0 copy-start.6
  39.8 0.0 copy-start.7
  39.9 0.0 copy-done.1
  39.9 0.0 copy-done.2
  39.9 0.0 copy-done.3
  39.9 0.0 copy-done.4
  39.9 0.6 %copy-done.5 = f32[64]{0:T(128)S(1)} copy-done((f32[64]{0:T(128)S(1)}, f32[64]{0:T(128)}, u32[]{:S(2)}) %copy-start.5) | copy-done | bytes 280
  40.5 0.0 copy-done.6
  40.5 0.0 copy-done.7
  40.5 2.4 %shard_map.137 = (bf16[192,240]{1,0:T(8,128)(2,1)S(1)}, bf16[192,192]{1,0:T(8,128)(2,1)S(1)}, bf16[192,192]{1,0:T(8,128)(2,1)S(1)}, bf16[96,768]{1,0:T(8,128)(2,...) custom-call(s32[1]{0:T(128)S(6)} %copy.18.level, ...), custom_call_target="tpu_custom_call" | custom-call | flops 8000000000 | bytes 1000000 | tf_op jit(solution)/shard_map/pallas_call | solution.py:317
  42.9 0.0 all-to-all-done.got
  42.9 0.0 copy-start.10
  42.9 0.6 %copy-done.10 = f32[64,1,128]{2,1,0:T(1,128)} copy-done((f32[64,1,128]{2,1,0:T(1,128)}, f32[64,1,128]{2,1,0:T(1,128)S(1)}, u32[]{:S(2)}) %copy-start.10) | copy-done | bytes 32792
  43.5 2.2 %shard_map.138 = (f32[8,16,256]{2,1,0:T(8,128)}, f32[16,256]{1,0:T(8,128)}) custom-call(s32[1]{0:T(128)S(6)} %copy.18.level, f32[8,16,256]{2,1,0:T(8,128)} %bitcast.15, f32[8,16,256]{2,1,0:T(8,128)} %bitcast.16, f32[64,1,128]{2,1,0:T(1,128)} %copy-done.10), custom_call_target="tpu_custom_call" | custom-call | flops 400000000 | bytes 400000 | tf_op jit(solution)/shard_map/pallas_call | solution.py:195
  45.8 0.0 copy-start.8
  45.8 0.0 collective-permute-done.3
  45.8 0.0 collective-permute-done.4
  45.8 0.0 copy-start.9
  45.8 0.9 %copy-done.8 = f32[8,16,256]{2,1,0:T(8,128)S(1)} copy-done((f32[8,16,256]{2,1,0:T(8,128)S(1)}, f32[8,16,256]{2,1,0:T(8,128)}, u32[]{:S(2)}) %copy-start.8) | copy-done | bytes 131096
  46.7 0.0 copy-done.9
  46.7 2.7 %shard_map.139 = f32[8,16,256]{2,1,0:T(8,128)} custom-call(bf16[8,32,256]{2,1,0:T(8,128)(2,1)S(1)} %pad_maximum_fusion.edges, bf16[192,240]{1,0:T(8,128)(2,1)S(1)} %get-tuple-element.20.w1, bf16[192,192]{1,0:T(8,128)(2,1)S(1)} %get-tuple-element.21.wm, bf16[192,192]{1,0:T(8,128)(2,1)S(1)} %get-tuple-element.22.wr, bf16[96,768]{1,0:T(8,128)(2,1)S(1)} %get-tuple-element.23.wo, ...), custom_call_target="tpu_custom_call" | custom-call | flops 4000000000 | bytes 1000000 | tf_op jit(solution)/shard_map/pallas_call | solution.py:422
  (6 shorter events, 0.1 us)
Async XLA Ops:
  2.5 27.7 %copy-start = (bf16[16,8,256]{2,1,0:T(8,128)(2,1)S(1)}, bf16[16,8,256]{2,1,0:T(8,128)(2,1)}, u32[]{:S(2)}) copy-start(bf16[16,8,256]{2,1,0:T(8,128)(2,1)} %get-tuple-element.19.own) | copy-start | bytes 196612
  2.5 27.7 %collective-permute-start = (bf16[16,8,256]{2,1,0:T(8,128)(2,1)}, bf16[16,8,256]{2,1,0:T(8,128)(2,1)S(1)}, u32[]{:S(2)}, u32[]{:S(2)}) collective-permute-start(bf16[16,8,256]{2,1,0:T(8,128)(2,1)} %get-tuple-element.19.own), channel_id=1, source_target_pairs={{0,64},{64,0},{128,192},{192,128},{1,65},{65,1},{129,193},{193,129... | collective-permute-start | bytes 196616 | tf_op jit(solution)/shard_map/ppermute | solution.py:452
  5.0 25.2 %collective-permute-start.1 = (bf16[16,8,256]{2,1,0:T(8,128)(2,1)}, bf16[16,8,256]{2,1,0:T(8,128)(2,1)S(1)}, u32[]{:S(2)}, u32[]{:S(2)}) collective-permute-start(bf16[16,8,256]{2,1,0:T(8,128)(2,1)} %get-tuple-element.19.own), channel_id=1, source_target_pairs={{64,128},{128,64},{192,256},{256,192},{320,384},{384,320},{65,129}... | collective-permute-start | bytes 196616 | tf_op jit(solution)/shard_map/ppermute | solution.py:452
  18.4 11.9 %collective-permute-start.2 = (bf16[16,8,256]{2,1,0:T(8,128)(2,1)}, bf16[16,8,256]{2,1,0:T(8,128)(2,1)S(1)}, u32[]{:S(2)}, u32[]{:S(2)}) collective-permute-start(bf16[16,8,256]{2,1,0:T(8,128)(2,1)} %get-tuple-element.19.own), channel_id=1, source_target_pairs={{256,320},{320,256},{384,448},{448,384},{257,321},{321,257},{385,4... | collective-permute-start | bytes 196616 | tf_op jit(solution)/shard_map/ppermute | solution.py:452
  19.1 23.8 %all-to-all-start = ((f32[64,1,128]{2,1,0:T(1,128)}), f32[64,1,128]{2,1,0:T(1,128)S(1)}, u32[]{:S(2)}, u32[]{:S(2)}) async-start(f32[64,1,128]{2,1,0:T(1,128)} %get-tuple-element.30), calls=%async_computation | async-start | bytes 65536 | tf_op jit(solution)/shard_map/all_to_all | solution.py:485
  30.3 9.5 %copy-start.1 = (bf16[3,64,192]{2,1,0:T(8,128)(2,1)S(1)}, bf16[3,64,192]{2,1,0:T(8,128)(2,1)}, u32[]{:S(2)}) copy-start(bf16[3,64,192]{2,1,0:T(8,128)(2,1)} %conv_mid.1) | copy-start | bytes 221188
  30.3 9.5 %copy-start.2 = (bf16[3,64,192]{2,1,0:T(8,128)(2,1)S(1)}, bf16[3,64,192]{2,1,0:T(8,128)(2,1)}, u32[]{:S(2)}) copy-start(bf16[3,64,192]{2,1,0:T(8,128)(2,1)} %conv_res.1) | copy-start | bytes 221188
  30.3 9.5 %copy-start.3 = (bf16[3,64,48]{1,2,0:T(8,128)(2,1)S(1)}, bf16[3,64,48]{1,2,0:T(8,128)(2,1)}, u32[]{:S(2)}) copy-start(bf16[3,64,48]{1,2,0:T(8,128)(2,1)} %param.21) | copy-start | bytes 55300
  30.3 9.5 %copy-start.4 = (bf16[3,16,192]{2,1,0:T(8,128)(2,1)S(1)}, bf16[3,16,192]{2,1,0:T(8,128)(2,1)}, u32[]{:S(2)}) copy-start(bf16[3,16,192]{2,1,0:T(8,128)(2,1)} %conv_out.1) | copy-start | bytes 55300
  30.4 15.4 %collective-permute-start.3 = (bf16[4,32,256]{2,1,0:T(8,128)(2,1)S(1)}, bf16[4,32,256]{2,1,0:T(8,128)(2,1)S(1)}, u32[]{:S(2)}, u32[]{:S(2)}) collective-permute-start(bf16[4,32,256]{2,1,0:T(8,128)(2,1)S(1)} %get-tuple-element.33), channel_id=1, source_target_pairs={{1,2},{2,1},{3,4},{4,3},{5,6},{6,5},{7,8},{8,7},{9,10},{10,9},{11,... | collective-permute-start | bytes 196616 | tf_op jit(solution)/shard_map/ppermute | solution.py:452
  33.0 12.8 %collective-permute-start.4 = (bf16[4,32,256]{2,1,0:T(8,128)(2,1)S(1)}, bf16[4,32,256]{2,1,0:T(8,128)(2,1)S(1)}, u32[]{:S(2)}, u32[]{:S(2)}) collective-permute-start(bf16[4,32,256]{2,1,0:T(8,128)(2,1)S(1)} %get-tuple-element.34), channel_id=1, source_target_pairs={{0,1},{1,0},{2,3},{3,2},{4,5},{5,4},{6,7},{7,6},{8,9},{9,8},{10,11... | collective-permute-start | bytes 196616 | tf_op jit(solution)/shard_map/ppermute | solution.py:452
  39.8 0.7 %copy-start.5 = (f32[64]{0:T(128)S(1)}, f32[64]{0:T(128)}, u32[]{:S(2)}) copy-start(f32[64]{0:T(128)} %param.25) | copy-start | bytes 772
  39.8 0.7 %copy-start.6 = (f32[64]{0:T(128)S(1)}, f32[64]{0:T(128)}, u32[]{:S(2)}) copy-start(f32[64]{0:T(128)} %param.26) | copy-start | bytes 772
  39.8 0.7 %copy-start.7 = (f32[64]{0:T(128)S(1)}, f32[64]{0:T(128)}, u32[]{:S(2)}) copy-start(f32[64]{0:T(128)} %param.27) | copy-start | bytes 772
  42.9 0.6 %copy-start.10 = (f32[64,1,128]{2,1,0:T(1,128)}, f32[64,1,128]{2,1,0:T(1,128)S(1)}, u32[]{:S(2)}) copy-start(f32[64,1,128]{2,1,0:T(1,128)S(1)} %all-to-all-done.got) | copy-start | bytes 98308
  45.8 0.9 %copy-start.8 = (f32[8,16,256]{2,1,0:T(8,128)S(1)}, f32[8,16,256]{2,1,0:T(8,128)}, u32[]{:S(2)}) copy-start(f32[8,16,256]{2,1,0:T(8,128)} %get-tuple-element.31.base) | copy-start | bytes 393220
  45.8 0.9 %copy-start.9 = (f32[16,256]{1,0:T(8,128)S(1)}, f32[16,256]{1,0:T(8,128)}, u32[]{:S(2)}) copy-start(f32[16,256]{1,0:T(8,128)} %get-tuple-element.32.slope) | copy-start | bytes 49156

commit v7 on v6

--- a/solution.py
+++ b/solution.py
@@ -200,6 +200,7 @@
         ),
         in_specs=[SM, VM, VM, VM],
         out_specs=(VM, VM),
+        compiler_params=pltpu.CompilerParams(vmem_limit_bytes=16 * 2**20),
         cost_estimate=pl.CostEstimate(
             flops=STATION_COST, bytes_accessed=400_000, transcendentals=0
         ),

time: 49.7 us -> 47.5 us (0.956)
  the two profiles are of different devices: /device:TPU:25 before, /device:TPU:24 now
where the time goes in v7:
time: 47.5 us; the launch traced here: 47.2 us
  starting transfers between devices  36.4 us (77%)
  Pallas kernels  7.53 us (16%)
  waiting for transfers between devices  1.61 us (3%)
  between operations  0.92 us (2%)
  local copies, waits for them, and re-layouts  0.71 us (1%)
    ppermute x5, starting transfers between devices, swapped(): return lax.ppermute(value, axis, pairs)  25.9 us
    all_to_all x1, starting transfers between devices, local(): lax.all_to_all(slots, 'space', 0, 0, axis_index_groups=[order_of(slots.sh...  10.5 us
    pallas_call x1, Pallas kernels, outer(): pl.pallas_call(outer_body, out_shape=jax.ShapeDtypeStruct((8, 16, 256), F...  2.65 us
    pallas_call x1, Pallas kernels, inner(): pl.pallas_call(inner_body, out_shape=(jax.ShapeDtypeStruct((192, 240), BF...  2.41 us
    pallas_call x1, Pallas kernels, pack(): pl.pallas_call(pack_body, out_shape=(jax.ShapeDtypeStruct((16, 8, 256), B...  1.86 us
    ppermute x5, waiting for transfers between devices, swapped(): return lax.ppermute(value, axis, pairs)  1.61 us
  transfers between devices with their start and end apart: 6, of which 1 were waited for; matrix products, arithmetic and copies ran while one was open for 0% of the time, Pallas kernels for 6%

profile of v7, /device:TPU:24, one launch (start us, length us, event | category | flops | bytes accessed | tf_op | source)
XLA Modules:
  0.0 47.2 jit_solution(11331001110736869742)
XLA Ops:
  0.7 1.9 %shard_map.136 = (bf16[16,8,256]{2,1,0:T(8,128)(2,1)}, f32[64,1,128]{2,1,0:T(1,128)}) custom-call(s32[1]{0:T(128)S(6)} %copy.18.level, f32[8,16,256]{2,1,0:T(8,128)} %bitcast.10, f32[4,2,128]{2,1,0:T(2,128)} %obs.1, f32[1,128]{1,0:T(1,128)} %bitcast.17, s32[1,128]{1,0:T(1,128)} %bitcast.18, s32[1,128]{1,0:T(1,128)} %bitcast.19), custom_call_target="tpu_custom_call" | custom-call | flops 50000000 | bytes 400000 | tf_op jit(solution)/shard_map/pallas_call | solution.py:86
  2.5 0.0 copy-start
  2.5 2.8 %collective-permute-start = (bf16[16,8,256]{2,1,0:T(8,128)(2,1)}, bf16[16,8,256]{2,1,0:T(8,128)(2,1)S(1)}, u32[]{:S(2)}, u32[]{:S(2)}) collective-permute-start(bf16[16,8,256]{2,1,0:T(8,128)(2,1)} %get-tuple-element.19.own), channel_id=1, source_target_pairs={{0,64},{64,0},{128,192},{192,128},{1,65},{65,1},{129,193},{193,129... | collective-permute-start | bytes 196616 | tf_op jit(solution)/shard_map/ppermute | solution.py:453
  5.3 13.4 %collective-permute-start.1 = (bf16[16,8,256]{2,1,0:T(8,128)(2,1)}, bf16[16,8,256]{2,1,0:T(8,128)(2,1)S(1)}, u32[]{:S(2)}, u32[]{:S(2)}) collective-permute-start(bf16[16,8,256]{2,1,0:T(8,128)(2,1)} %get-tuple-element.19.own), channel_id=1, source_target_pairs={{64,128},{128,64},{192,256},{256,192},{320,384},{384,320},{65,129}... | collective-permute-start | bytes 196616 | tf_op jit(solution)/shard_map/ppermute | solution.py:453
  18.7 0.7 %collective-permute-start.2 = (bf16[16,8,256]{2,1,0:T(8,128)(2,1)}, bf16[16,8,256]{2,1,0:T(8,128)(2,1)S(1)}, u32[]{:S(2)}, u32[]{:S(2)}) collective-permute-start(bf16[16,8,256]{2,1,0:T(8,128)(2,1)} %get-tuple-element.19.own), channel_id=1, source_target_pairs={{256,320},{320,256},{384,448},{448,384},{257,321},{321,257},{385,4... | collective-permute-start | bytes 196616 | tf_op jit(solution)/shard_map/ppermute | solution.py:453
  19.4 10.5 %all-to-all-start = ((f32[64,1,128]{2,1,0:T(1,128)}), f32[64,1,128]{2,1,0:T(1,128)S(1)}, u32[]{:S(2)}, u32[]{:S(2)}) async-start(f32[64,1,128]{2,1,0:T(1,128)} %get-tuple-element.30), calls=%async_computation | async-start | bytes 65536 | tf_op jit(solution)/shard_map/all_to_all | solution.py:486
  29.9 0.0 copy-done
  29.9 0.0 collective-permute-done.low
  29.9 0.0 collective-permute-done.1.t2
  30.0 0.0 collective-permute-done.2.high
  30.0 0.0 copy-start.3
  30.0 0.0 copy-start.4
  30.0 0.0 copy-start.5
  30.0 0.0 copy-start.6
  30.1 7.1 %collective-permute-start.3 = (bf16[4,32,256]{2,1,0:T(8,128)(2,1)S(1)}, bf16[4,32,256]{2,1,0:T(8,128)(2,1)S(1)}, u32[]{:S(2)}, u32[]{:S(2)}) collective-permute-start(bf16[4,32,256]{2,1,0:T(8,128)(2,1)S(1)} %get-tuple-element.33), channel_id=1, source_target_pairs={{1,2},{2,1},{3,4},{4,3},{5,6},{6,5},{7,8},{8,7},{9,10},{10,9},{11,... | collective-permute-start | bytes 196616 | tf_op jit(solution)/shard_map/ppermute | solution.py:453
  37.2 1.9 %collective-permute-start.4 = (bf16[4,32,256]{2,1,0:T(8,128)(2,1)S(1)}, bf16[4,32,256]{2,1,0:T(8,128)(2,1)S(1)}, u32[]{:S(2)}, u32[]{:S(2)}) collective-permute-start(bf16[4,32,256]{2,1,0:T(8,128)(2,1)S(1)} %get-tuple-element.34), channel_id=1, source_target_pairs={{0,1},{1,0},{2,3},{3,2},{4,5},{5,4},{6,7},{7,6},{8,9},{9,8},{10,11... | collective-permute-start | bytes 196616 | tf_op jit(solution)/shard_map/ppermute | solution.py:453
  39.2 0.0 copy-start.7
  39.2 0.0 copy-start.8
  39.2 0.0 copy-start.9
  39.2 0.0 copy-done.3
  39.2 0.0 copy-done.4
  39.2 0.0 copy-done.5
  39.2 0.0 copy-done.6
  39.2 0.6 %copy-done.7 = f32[64]{0:T(128)S(1)} copy-done((f32[64]{0:T(128)S(1)}, f32[64]{0:T(128)}, u32[]{:S(2)}) %copy-start.7) | copy-done | bytes 280
  39.8 0.0 copy-done.8
  39.8 0.0 copy-done.9
  39.8 0.0 copy-start.1
  39.8 0.0 copy-start.2
  39.9 2.4 %shard_map.137 = (bf16[192,240]{1,0:T(8,128)(2,1)S(1)}, bf16[192,192]{1,0:T(8,128)(2,1)S(1)}, bf16[192,192]{1,0:T(8,128)(2,1)S(1)}, bf16[96,768]{1,0:T(8,128)(2,...) custom-call(s32[1]{0:T(128)S(6)} %copy.18.level, ...), custom_call_target="tpu_custom_call" | custom-call | flops 8000000000 | bytes 1000000 | tf_op jit(solution)/shard_map/pallas_call | solution.py:318
  42.3 0.0 all-to-all-done.got
  42.3 0.0 copy-done.1
  42.3 0.0 copy-done.2
  42.3 0.6 %shard_map.138 = (f32[8,16,256]{2,1,0:T(8,128)S(1)}, f32[16,256]{1,0:T(8,128)S(1)}) custom-call(s32[1]{0:T(128)S(6)} %copy.18.level, f32[8,16,256]{2,1,0:T(8,128)S(1)} %bitcast.11, f32[8,16,256]{2,1,0:T(8,128)S(1)} %bitcast.12, f32[64,1,128]{2,1,0:T(1,128)S(1)} %all-to-all-done.got), custom_call_target="tpu_custom_call" | custom-call | flops 400000000 | bytes 400000 | tf_op jit(solution)/shard_map/pallas_call | solution.py:195
  42.9 1.6 %collective-permute-done.3 = bf16[4,32,256]{2,1,0:T(8,128)(2,1)S(1)} collective-permute-done((bf16[4,32,256]{2,1,0:T(8,128)(2,1)S(1)}, bf16[4,32,256]{2,1,0:T(8,128)(2,1)S(1)}, u32[]{:S(2)}, u32[]{:S(2)}) %collective-permute-start.3) | collective-permute-done | bytes 65568 | tf_op jit(solution)/shard_map/ppermute | solution.py:453
  44.5 0.0 collective-permute-done.4
  44.5 2.7 %shard_map.139 = f32[8,16,256]{2,1,0:T(8,128)} custom-call(bf16[8,32,256]{2,1,0:T(8,128)(2,1)S(1)} %pad_maximum_fusion.edges, bf16[192,240]{1,0:T(8,128)(2,1)S(1)} %get-tuple-element.20.w1, bf16[192,192]{1,0:T(8,128)(2,1)S(1)} %get-tuple-element.21.wm, bf16[192,192]{1,0:T(8,128)(2,1)S(1)} %get-tuple-element.22.wr, bf16[96,768]{1,0:T(8,128)(2,1)S(1)} %get-tuple-element.23.wo, ...), custom_call_target="tpu_custom_call" | custom-call | flops 4000000000 | bytes 1000000 | tf_op jit(solution)/shard_map/pallas_call | solution.py:423
  (6 shorter events, 0.1 us)
Async XLA Ops:
  2.5 27.4 %copy-start = (bf16[16,8,256]{2,1,0:T(8,128)(2,1)S(1)}, bf16[16,8,256]{2,1,0:T(8,128)(2,1)}, u32[]{:S(2)}) copy-start(bf16[16,8,256]{2,1,0:T(8,128)(2,1)} %get-tuple-element.19.own) | copy-start | bytes 196612
  2.5 27.4 %collective-permute-start = (bf16[16,8,256]{2,1,0:T(8,128)(2,1)}, bf16[16,8,256]{2,1,0:T(8,128)(2,1)S(1)}, u32[]{:S(2)}, u32[]{:S(2)}) collective-permute-start(bf16[16,8,256]{2,1,0:T(8,128)(2,1)} %get-tuple-element.19.own), channel_id=1, source_target_pairs={{0,64},{64,0},{128,192},{192,128},{1,65},{65,1},{129,193},{193,129... | collective-permute-start | bytes 196616 | tf_op jit(solution)/shard_map/ppermute | solution.py:453
  5.3 24.6 %collective-permute-start.1 = (bf16[16,8,256]{2,1,0:T(8,128)(2,1)}, bf16[16,8,256]{2,1,0:T(8,128)(2,1)S(1)}, u32[]{:S(2)}, u32[]{:S(2)}) collective-permute-start(bf16[16,8,256]{2,1,0:T(8,128)(2,1)} %get-tuple-element.19.own), channel_id=1, source_target_pairs={{64,128},{128,64},{192,256},{256,192},{320,384},{384,320},{65,129}... | collective-permute-start | bytes 196616 | tf_op jit(solution)/shard_map/ppermute | solution.py:453
  18.7 11.3 %collective-permute-start.2 = (bf16[16,8,256]{2,1,0:T(8,128)(2,1)}, bf16[16,8,256]{2,1,0:T(8,128)(2,1)S(1)}, u32[]{:S(2)}, u32[]{:S(2)}) collective-permute-start(bf16[16,8,256]{2,1,0:T(8,128)(2,1)} %get-tuple-element.19.own), channel_id=1, source_target_pairs={{256,320},{320,256},{384,448},{448,384},{257,321},{321,257},{385,4... | collective-permute-start | bytes 196616 | tf_op jit(solution)/shard_map/ppermute | solution.py:453
  19.4 22.9 %all-to-all-start = ((f32[64,1,128]{2,1,0:T(1,128)}), f32[64,1,128]{2,1,0:T(1,128)S(1)}, u32[]{:S(2)}, u32[]{:S(2)}) async-start(f32[64,1,128]{2,1,0:T(1,128)} %get-tuple-element.30), calls=%async_computation | async-start | bytes 65536 | tf_op jit(solution)/shard_map/all_to_all | solution.py:486
  30.0 9.2 %copy-start.3 = (bf16[3,64,192]{2,1,0:T(8,128)(2,1)S(1)}, bf16[3,64,192]{2,1,0:T(8,128)(2,1)}, u32[]{:S(2)}) copy-start(bf16[3,64,192]{2,1,0:T(8,128)(2,1)} %conv_mid.1) | copy-start | bytes 221188
  30.0 9.2 %copy-start.4 = (bf16[3,64,192]{2,1,0:T(8,128)(2,1)S(1)}, bf16[3,64,192]{2,1,0:T(8,128)(2,1)}, u32[]{:S(2)}) copy-start(bf16[3,64,192]{2,1,0:T(8,128)(2,1)} %conv_res.1) | copy-start | bytes 221188
  30.0 9.2 %copy-start.5 = (bf16[3,64,48]{1,2,0:T(8,128)(2,1)S(1)}, bf16[3,64,48]{1,2,0:T(8,128)(2,1)}, u32[]{:S(2)}) copy-start(bf16[3,64,48]{1,2,0:T(8,128)(2,1)} %param.21) | copy-start | bytes 55300
  30.0 9.2 %copy-start.6 = (bf16[3,16,192]{2,1,0:T(8,128)(2,1)S(1)}, bf16[3,16,192]{2,1,0:T(8,128)(2,1)}, u32[]{:S(2)}) copy-start(bf16[3,16,192]{2,1,0:T(8,128)(2,1)} %conv_out.1) | copy-start | bytes 55300
  30.1 14.4 %collective-permute-start.3 = (bf16[4,32,256]{2,1,0:T(8,128)(2,1)S(1)}, bf16[4,32,256]{2,1,0:T(8,128)(2,1)S(1)}, u32[]{:S(2)}, u32[]{:S(2)}) collective-permute-start(bf16[4,32,256]{2,1,0:T(8,128)(2,1)S(1)} %get-tuple-element.33), channel_id=1, source_target_pairs={{1,2},{2,1},{3,4},{4,3},{5,6},{6,5},{7,8},{8,7},{9,10},{10,9},{11,... | collective-permute-start | bytes 196616 | tf_op jit(solution)/shard_map/ppermute | solution.py:453
  37.2 7.3 %collective-permute-start.4 = (bf16[4,32,256]{2,1,0:T(8,128)(2,1)S(1)}, bf16[4,32,256]{2,1,0:T(8,128)(2,1)S(1)}, u32[]{:S(2)}, u32[]{:S(2)}) collective-permute-start(bf16[4,32,256]{2,1,0:T(8,128)(2,1)S(1)} %get-tuple-element.34), channel_id=1, source_target_pairs={{0,1},{1,0},{2,3},{3,2},{4,5},{5,4},{6,7},{7,6},{8,9},{9,8},{10,11... | collective-permute-start | bytes 196616 | tf_op jit(solution)/shard_map/ppermute | solution.py:453
  39.2 0.7 %copy-start.7 = (f32[64]{0:T(128)S(1)}, f32[64]{0:T(128)}, u32[]{:S(2)}) copy-start(f32[64]{0:T(128)} %param.25) | copy-start | bytes 772
  39.2 0.7 %copy-start.8 = (f32[64]{0:T(128)S(1)}, f32[64]{0:T(128)}, u32[]{:S(2)}) copy-start(f32[64]{0:T(128)} %param.26) | copy-start | bytes 772
  39.2 0.7 %copy-start.9 = (f32[64]{0:T(128)S(1)}, f32[64]{0:T(128)}, u32[]{:S(2)}) copy-start(f32[64]{0:T(128)} %param.27) | copy-start | bytes 772
  39.8 2.4 %copy-start.1 = (f32[4,2,16,256]{3,2,1,0:T(8,128)S(1)}, f32[4,2,16,256]{3,2,1,0:T(8,128)}, u32[]{:S(2)}) copy-start(f32[4,2,16,256]{3,2,1,0:T(8,128)} %param.14) | copy-start | bytes 393220
  39.8 2.4 %copy-start.2 = (f32[4,2,16,256]{3,2,1,0:T(8,128)S(1)}, f32[4,2,16,256]{3,2,1,0:T(8,128)}, u32[]{:S(2)}) copy-start(f32[4,2,16,256]{3,2,1,0:T(8,128)} %param.15) | copy-start | bytes 393220

commit v8 on v7

--- a/solution.py
+++ b/solution.py
@@ -8,7 +8,7 @@
 from jax.sharding import PartitionSpec as P
 
 LEVELS = 32
-LEADER = 8
+LEADER = 6
 BF = jnp.bfloat16
 F32 = jnp.float32
 OUT_GROUP = 4
@@ -46,7 +46,9 @@
     return jnp.sum(jnp.where(line == lane, row, 0.0), axis=1, keepdims=True)
 
 
-def pack_body(level, noisy, obs, var, owner, cell, own, out, turned):
+def pack_body(
+    level, noisy, obs, var, owner, cell, in_bias, noise_embed, norm_gain, own, out, columns, turned
+):
     count = obs.shape[2]
     peers = out.shape[0]
     noise = scale_at(level[0], (16, 256))
@@ -81,19 +83,24 @@
         total = piece if total is None else total + piece
     out[:, 0, :] = total
 
-
-def pack(level, noisy, obs, var, owner, cell):
+    bias = 0.5 * (in_bias[...] + noise_embed[...] * jnp.log(10.0 * noise[:1, :64]))
+    columns[0] = jnp.broadcast_to(column_of(bias), (64, 128))
+    columns[1] = jnp.broadcast_to(column_of(0.5 * norm_gain[...]), (64, 128))
+
+
+def pack(level, *arrays):
     return pl.pallas_call(
         pack_body,
         out_shape=(
             jax.ShapeDtypeStruct((16, 8, 256), BF),
             jax.ShapeDtypeStruct((64, 1, 128), F32),
+            jax.ShapeDtypeStruct((2, 64, 128), F32),
         ),
-        in_specs=[SM, VM, VM, VM, VM, VM],
-        out_specs=(VM, VM),
+        in_specs=[SM] + [VM] * 8,
+        out_specs=(VM, VM, VM),
         scratch_shapes=[pltpu.VMEM((16, 8, 256), F32)],
         cost_estimate=pl.CostEstimate(flops=50_000_000, bytes_accessed=400_000, transcendentals=0),
-    )(level, noisy, obs, var, owner, cell)
+    )(level, *arrays)
 
 
 def shifts(v):
@@ -217,14 +224,11 @@
     conv_mid,
     conv_res,
     conv_out,
-    in_bias,
-    noise_embed,
-    norm_gain,
+    columns,
     w1_out,
     wm_out,
     wr_out,
     wo_out,
-    columns,
     x1_edge,
     x2_edge,
     x3_edge,
@@ -240,12 +244,8 @@
     even_t = time_rank % 2 == 0
     lower = time_rank < times // 2
 
-    noise64 = scale_at(level[0], (1, 64))
-    bias_row = 0.5 * (in_bias[...] + noise_embed[...] * jnp.log(10.0 * noise64))
-    bias = column_of(bias_row)
-    gain = column_of(0.5 * norm_gain[...])
-    columns[0] = jnp.broadcast_to(bias, (64, 128))
-    columns[1] = jnp.broadcast_to(gain, (64, 128))
+    bias = columns[0][:, :1]
+    gain = columns[1][:, :1]
 
     taps_in = [0.5 * conv_in[a].astype(F32).T for a in range(3)]
     spare = jnp.zeros((64, 48), F32)
@@ -322,15 +322,14 @@
             jax.ShapeDtypeStruct((192, 192), BF),
             jax.ShapeDtypeStruct((192, 192), BF),
             jax.ShapeDtypeStruct((96, 768), BF),
-            jax.ShapeDtypeStruct((2, 64, 128), F32),
             jax.ShapeDtypeStruct((4 * 48, 512), BF),
             jax.ShapeDtypeStruct((4 * 192, 512), BF),
             jax.ShapeDtypeStruct((4 * 192, 512), BF),
             jax.ShapeDtypeStruct((512, 256), BF),
             jax.ShapeDtypeStruct((8, 8, 256), F32),
         ),
-        in_specs=[SM] + [VM] * 11,
-        out_specs=(VM,) * 10,
+        in_specs=[SM] + [VM] * 9,
+        out_specs=(VM,) * 9,
         scratch_shapes=[
             pltpu.VMEM((16 * 48, 512), BF),
             pltpu.VMEM((14 * 192, 512), BF),
@@ -471,13 +470,16 @@
 ):
     even_s = lax.axis_index("space") % 2 == 0
     noisy = noisy_state.reshape(8, 16, 256)
-    own, slots = pack(
+    own, slots, columns = pack(
         level_index,
         noisy,
         station_obs,
         obs_variance.reshape(1, 128),
         station_owner.reshape(1, 128),
         station_cell.reshape(1, 128),
+        in_bias.reshape(1, 64),
+        noise_embed.reshape(1, 64),
+        norm_gain.reshape(1, 64),
     )
     half = lax.axis_size("tm") // 2
     low = swapped(own, "tm", 0, half)
@@ -503,12 +505,10 @@
         conv_mid,
         conv_res,
         conv_out,
-        in_bias.reshape(1, 64),
-        noise_embed.reshape(1, 64),
-        norm_gain.reshape(1, 64),
+        columns,
     )
     base, slope = station_terms(level_index, noisy, fresh_noise.reshape(8, 16, 256), got)
-    result = outer(edges, *held, base, slope)
+    result = outer(edges, *held[:4], columns, *held[4:], base, slope)
     return result.reshape(noisy_state.shape)
 
 

time: 47.5 us -> 46.5 us (0.979); the launches traced: 47.2 us -> 45.6 us
  waiting for transfers between devices: 1.61 us -> 0.1 us
  local copies, waits for them, and re-layouts: 0.71 us -> 0.09 us
  starting transfers between devices: 36.4 us -> 36.9 us
    ppermute x5, starting transfers between devices: 25.9 us -> 28 us  [swapped(): return lax.ppermute(value, axis, pairs)]
    all_to_all x1, starting transfers between devices: 10.5 us -> 8.89 us  [local(): lax.all_to_all(slots, 'space', 0, 0, axis_index_groups=[order_of(slots.sh...]
    ppermute x5, waiting for transfers between devices: 1.61 us -> 0.1 us  [swapped(): return lax.ppermute(value, axis, pairs)]
    unnamed x23 -> x19, local copies, waits for them, and re-layouts: 0.68 us -> 0.07 us
  transfers between devices with their start and end apart: 6 -> 6, of which waited for: 1 -> 1; matrix products, arithmetic and copies ran while one was open for 0% -> 0% of each run, Pallas kernels for 6% -> 7%
where the time goes in v8:
time: 46.5 us; the launch traced here: 45.6 us
  starting transfers between devices  36.9 us (79%)
  Pallas kernels  7.6 us (16%)
  between operations  0.93 us (2%)
    ppermute x5, starting transfers between devices, swapped(): return lax.ppermute(value, axis, pairs)  28 us
    all_to_all x1, starting transfers between devices, local(): lax.all_to_all(slots, 'space', 0, 0, axis_index_groups=[order_of(slots.sh...  8.89 us
    pallas_call x1, Pallas kernels, outer(): pl.pallas_call(outer_body, out_shape=jax.ShapeDtypeStruct((8, 16, 256), F...  2.65 us
    pallas_call x1, Pallas kernels, inner(): pl.pallas_call(inner_body, out_shape=(jax.ShapeDtypeStruct((192, 240), BF...  2.43 us
    pallas_call x1, Pallas kernels, pack(): pl.pallas_call(pack_body, out_shape=(jax.ShapeDtypeStruct((16, 8, 256), B...  1.92 us
  transfers between devices with their start and end apart: 6, of which 1 were waited for; matrix products, arithmetic and copies ran while one was open for 0% of the time, Pallas kernels for 7%

profile of v8, /device:TPU:24, one launch (start us, length us, event | category | flops | bytes accessed | tf_op | source)
XLA Modules:
  0.0 45.6 jit_solution(13303113023365078206)
XLA Ops:
  0.7 1.9 %shard_map.136 = (bf16[16,8,256]{2,1,0:T(8,128)(2,1)}, f32[64,1,128]{2,1,0:T(1,128)}, f32[2,64,128]{2,1,0:T(8,128)}) custom-call(s32[1]{0:T(128)S(6)} %copy.18.level, f32[8,16,256]{2,1,0:T(8,128)} %bitcast.10, f32[4,2,128]{2,1,0:T(2,128)} %obs.1, f32[1,128]{1,0:T(1,128)} %bitcast.14, s32[1,128]{1,0:T(1,128)} %bitcast.15, s32[1,128]{1,0:T(1,128)} %bitcast.16, ...), custom_call_target="tpu_custom_call" | custom-call | flops 50000000 | bytes 400000 | tf_op jit(solution)/shard_map/pallas_call | solution.py:92
  2.6 0.0 copy-start
  2.6 2.8 %collective-permute-start = (bf16[16,8,256]{2,1,0:T(8,128)(2,1)}, bf16[16,8,256]{2,1,0:T(8,128)(2,1)S(1)}, u32[]{:S(2)}, u32[]{:S(2)}) collective-permute-start(bf16[16,8,256]{2,1,0:T(8,128)(2,1)} %get-tuple-element.19.own), channel_id=1, source_target_pairs={{0,64},{64,0},{128,192},{192,128},{1,65},{65,1},{129,193},{193,129... | collective-permute-start | bytes 196616 | tf_op jit(solution)/shard_map/ppermute | solution.py:452
  5.4 13.4 %collective-permute-start.1 = (bf16[16,8,256]{2,1,0:T(8,128)(2,1)}, bf16[16,8,256]{2,1,0:T(8,128)(2,1)S(1)}, u32[]{:S(2)}, u32[]{:S(2)}) collective-permute-start(bf16[16,8,256]{2,1,0:T(8,128)(2,1)} %get-tuple-element.19.own), channel_id=1, source_target_pairs={{64,128},{128,64},{192,256},{256,192},{320,384},{384,320},{65,129}... | collective-permute-start | bytes 196616 | tf_op jit(solution)/shard_map/ppermute | solution.py:452
  18.8 0.7 %collective-permute-start.2 = (bf16[16,8,256]{2,1,0:T(8,128)(2,1)}, bf16[16,8,256]{2,1,0:T(8,128)(2,1)S(1)}, u32[]{:S(2)}, u32[]{:S(2)}) collective-permute-start(bf16[16,8,256]{2,1,0:T(8,128)(2,1)} %get-tuple-element.19.own), channel_id=1, source_target_pairs={{256,320},{320,256},{384,448},{448,384},{257,321},{321,257},{385,4... | collective-permute-start | bytes 196616 | tf_op jit(solution)/shard_map/ppermute | solution.py:452
  19.4 8.9 %all-to-all-start = ((f32[64,1,128]{2,1,0:T(1,128)}), f32[64,1,128]{2,1,0:T(1,128)S(1)}, u32[]{:S(2)}, u32[]{:S(2)}) async-start(f32[64,1,128]{2,1,0:T(1,128)} %get-tuple-element.30), calls=%async_computation | async-start | bytes 65536 | tf_op jit(solution)/shard_map/all_to_all | solution.py:488
  28.3 0.0 copy-done
  28.4 0.0 collective-permute-done.low
  28.4 0.0 collective-permute-done.1.t2
  28.4 0.0 collective-permute-done.2.high
  28.4 0.0 copy-start.7
  28.5 0.0 copy-start.3
  28.5 0.0 copy-start.4
  28.5 0.0 copy-start.5
  28.5 0.0 copy-start.6
  28.5 9.3 %collective-permute-start.3 = (bf16[4,32,256]{2,1,0:T(8,128)(2,1)S(1)}, bf16[4,32,256]{2,1,0:T(8,128)(2,1)S(1)}, u32[]{:S(2)}, u32[]{:S(2)}) collective-permute-start(bf16[4,32,256]{2,1,0:T(8,128)(2,1)S(1)} %get-tuple-element.33), channel_id=1, source_target_pairs={{1,2},{2,1},{3,4},{4,3},{5,6},{6,5},{7,8},{8,7},{9,10},{10,9},{11,... | collective-permute-start | bytes 196616 | tf_op jit(solution)/shard_map/ppermute | solution.py:452
  37.8 1.9 %collective-permute-start.4 = (bf16[4,32,256]{2,1,0:T(8,128)(2,1)S(1)}, bf16[4,32,256]{2,1,0:T(8,128)(2,1)S(1)}, u32[]{:S(2)}, u32[]{:S(2)}) collective-permute-start(bf16[4,32,256]{2,1,0:T(8,128)(2,1)S(1)} %get-tuple-element.34), channel_id=1, source_target_pairs={{0,1},{1,0},{2,3},{3,2},{4,5},{5,4},{6,7},{7,6},{8,9},{9,8},{10,11... | collective-permute-start | bytes 196616 | tf_op jit(solution)/shard_map/ppermute | solution.py:452
  39.7 0.0 copy-done.7
  39.7 0.0 copy-done.3
  39.7 0.0 copy-done.4
  39.8 0.0 copy-done.5
  39.8 0.0 copy-done.6
  39.8 0.0 copy-start.1
  39.8 0.0 copy-start.2
  39.8 2.4 %shard_map.137 = (bf16[192,240]{1,0:T(8,128)(2,1)S(1)}, bf16[192,192]{1,0:T(8,128)(2,1)S(1)}, bf16[192,192]{1,0:T(8,128)(2,1)S(1)}, bf16[96,768]{1,0:T(8,128)(2,...) custom-call(s32[1]{0:T(128)S(6)} %copy.18.level, ...), custom_call_target="tpu_custom_call" | custom-call | flops 8000000000 | bytes 1000000 | tf_op jit(solution)/shard_map/pallas_call | solution.py:318
  42.2 0.0 all-to-all-done.got
  42.2 0.0 copy-done.1
  42.3 0.0 copy-done.2
  42.3 0.6 %shard_map.138 = (f32[8,16,256]{2,1,0:T(8,128)S(1)}, f32[16,256]{1,0:T(8,128)S(1)}) custom-call(s32[1]{0:T(128)S(6)} %copy.18.level, f32[8,16,256]{2,1,0:T(8,128)S(1)} %bitcast.11, f32[8,16,256]{2,1,0:T(8,128)S(1)} %bitcast.12, f32[64,1,128]{2,1,0:T(1,128)S(1)} %all-to-all-done.got), custom_call_target="tpu_custom_call" | custom-call | flops 400000000 | bytes 400000 | tf_op jit(solution)/shard_map/pallas_call | solution.py:202
  42.9 0.1 collective-permute-done.3
  43.0 0.0 collective-permute-done.4
  43.0 2.7 %shard_map.139 = f32[8,16,256]{2,1,0:T(8,128)} custom-call(bf16[8,32,256]{2,1,0:T(8,128)(2,1)S(1)} %pad_maximum_fusion.edges, bf16[192,240]{1,0:T(8,128)(2,1)S(1)} %get-tuple-element.21.w1, bf16[192,192]{1,0:T(8,128)(2,1)S(1)} %get-tuple-element.22.wm, bf16[192,192]{1,0:T(8,128)(2,1)S(1)} %get-tuple-element.23.wr, bf16[96,768]{1,0:T(8,128)(2,1)S(1)} %get-tuple-element.24.wo, ...), custom_call_target="tpu_custom_call" | custom-call | flops 4000000000 | bytes 1000000 | tf_op jit(solution)/shard_map/pallas_call | solution.py:422
  (6 shorter events, 0.1 us)
Async XLA Ops:
  2.6 25.8 %copy-start = (bf16[16,8,256]{2,1,0:T(8,128)(2,1)S(1)}, bf16[16,8,256]{2,1,0:T(8,128)(2,1)}, u32[]{:S(2)}) copy-start(bf16[16,8,256]{2,1,0:T(8,128)(2,1)} %get-tuple-element.19.own) | copy-start | bytes 196612
  2.6 25.8 %collective-permute-start = (bf16[16,8,256]{2,1,0:T(8,128)(2,1)}, bf16[16,8,256]{2,1,0:T(8,128)(2,1)S(1)}, u32[]{:S(2)}, u32[]{:S(2)}) collective-permute-start(bf16[16,8,256]{2,1,0:T(8,128)(2,1)} %get-tuple-element.19.own), channel_id=1, source_target_pairs={{0,64},{64,0},{128,192},{192,128},{1,65},{65,1},{129,193},{193,129... | collective-permute-start | bytes 196616 | tf_op jit(solution)/shard_map/ppermute | solution.py:452
  5.4 23.0 %collective-permute-start.1 = (bf16[16,8,256]{2,1,0:T(8,128)(2,1)}, bf16[16,8,256]{2,1,0:T(8,128)(2,1)S(1)}, u32[]{:S(2)}, u32[]{:S(2)}) collective-permute-start(bf16[16,8,256]{2,1,0:T(8,128)(2,1)} %get-tuple-element.19.own), channel_id=1, source_target_pairs={{64,128},{128,64},{192,256},{256,192},{320,384},{384,320},{65,129}... | collective-permute-start | bytes 196616 | tf_op jit(solution)/shard_map/ppermute | solution.py:452
  18.8 9.7 %collective-permute-start.2 = (bf16[16,8,256]{2,1,0:T(8,128)(2,1)}, bf16[16,8,256]{2,1,0:T(8,128)(2,1)S(1)}, u32[]{:S(2)}, u32[]{:S(2)}) collective-permute-start(bf16[16,8,256]{2,1,0:T(8,128)(2,1)} %get-tuple-element.19.own), channel_id=1, source_target_pairs={{256,320},{320,256},{384,448},{448,384},{257,321},{321,257},{385,4... | collective-permute-start | bytes 196616 | tf_op jit(solution)/shard_map/ppermute | solution.py:452
  19.4 22.8 %all-to-all-start = ((f32[64,1,128]{2,1,0:T(1,128)}), f32[64,1,128]{2,1,0:T(1,128)S(1)}, u32[]{:S(2)}, u32[]{:S(2)}) async-start(f32[64,1,128]{2,1,0:T(1,128)} %get-tuple-element.30), calls=%async_computation | async-start | bytes 65536 | tf_op jit(solution)/shard_map/all_to_all | solution.py:488
  28.4 11.3 %copy-start.7 = (f32[2,64,128]{2,1,0:T(8,128)S(1)}, f32[2,64,128]{2,1,0:T(8,128)}, u32[]{:S(2)}) copy-start(f32[2,64,128]{2,1,0:T(8,128)} %get-tuple-element.20.columns) | copy-start | bytes 196612
  28.5 11.3 %copy-start.3 = (bf16[3,64,192]{2,1,0:T(8,128)(2,1)S(1)}, bf16[3,64,192]{2,1,0:T(8,128)(2,1)}, u32[]{:S(2)}) copy-start(bf16[3,64,192]{2,1,0:T(8,128)(2,1)} %conv_mid.1) | copy-start | bytes 221188
  28.5 11.3 %copy-start.4 = (bf16[3,64,192]{2,1,0:T(8,128)(2,1)S(1)}, bf16[3,64,192]{2,1,0:T(8,128)(2,1)}, u32[]{:S(2)}) copy-start(bf16[3,64,192]{2,1,0:T(8,128)(2,1)} %conv_res.1) | copy-start | bytes 221188
  28.5 11.3 %copy-start.5 = (bf16[3,64,48]{1,2,0:T(8,128)(2,1)S(1)}, bf16[3,64,48]{1,2,0:T(8,128)(2,1)}, u32[]{:S(2)}) copy-start(bf16[3,64,48]{1,2,0:T(8,128)(2,1)} %param.21) | copy-start | bytes 55300
  28.5 11.3 %copy-start.6 = (bf16[3,16,192]{2,1,0:T(8,128)(2,1)S(1)}, bf16[3,16,192]{2,1,0:T(8,128)(2,1)}, u32[]{:S(2)}) copy-start(bf16[3,16,192]{2,1,0:T(8,128)(2,1)} %conv_out.1) | copy-start | bytes 55300
  28.5 14.4 %collective-permute-start.3 = (bf16[4,32,256]{2,1,0:T(8,128)(2,1)S(1)}, bf16[4,32,256]{2,1,0:T(8,128)(2,1)S(1)}, u32[]{:S(2)}, u32[]{:S(2)}) collective-permute-start(bf16[4,32,256]{2,1,0:T(8,128)(2,1)S(1)} %get-tuple-element.33), channel_id=1, source_target_pairs={{1,2},{2,1},{3,4},{4,3},{5,6},{6,5},{7,8},{8,7},{9,10},{10,9},{11,... | collective-permute-start | bytes 196616 | tf_op jit(solution)/shard_map/ppermute | solution.py:452
  37.8 5.2 %collective-permute-start.4 = (bf16[4,32,256]{2,1,0:T(8,128)(2,1)S(1)}, bf16[4,32,256]{2,1,0:T(8,128)(2,1)S(1)}, u32[]{:S(2)}, u32[]{:S(2)}) collective-permute-start(bf16[4,32,256]{2,1,0:T(8,128)(2,1)S(1)} %get-tuple-element.34), channel_id=1, source_target_pairs={{0,1},{1,0},{2,3},{3,2},{4,5},{5,4},{6,7},{7,6},{8,9},{9,8},{10,11... | collective-permute-start | bytes 196616 | tf_op jit(solution)/shard_map/ppermute | solution.py:452
  39.8 2.5 %copy-start.1 = (f32[4,2,16,256]{3,2,1,0:T(8,128)S(1)}, f32[4,2,16,256]{3,2,1,0:T(8,128)}, u32[]{:S(2)}) copy-start(f32[4,2,16,256]{3,2,1,0:T(8,128)} %param.14) | copy-start | bytes 393220
  39.8 2.5 %copy-start.2 = (f32[4,2,16,256]{3,2,1,0:T(8,128)S(1)}, f32[4,2,16,256]{3,2,1,0:T(8,128)}, u32[]{:S(2)}) copy-start(f32[4,2,16,256]{3,2,1,0:T(8,128)} %param.15) | copy-start | bytes 393220

commit v9 on v8

--- a/solution.py
+++ b/solution.py
@@ -75,12 +75,11 @@
     hot = jnp.where(
         lax.broadcasted_iota(jnp.int32, (peers, count), 0) == (strip + (peers - LEADER)) % peers, 1.0, 0.0
     ).astype(BF)
-    total = None
-    for part in parts_of(ranked):
-        piece = lax.dot_general(
-            hot, part, (((1,), (1,)), ((), ())), preferred_element_type=F32
-        )
-        total = piece if total is None else total + piece
+    stacked = jnp.concatenate(parts_of(ranked), axis=0)
+    pieces = lax.dot_general(
+        hot, stacked, (((1,), (1,)), ((), ())), preferred_element_type=F32
+    )
+    total = pieces[:, :128] + pieces[:, 128:256] + pieces[:, 256:]
     out[:, 0, :] = total
 
     bias = 0.5 * (in_bias[...] + noise_embed[...] * jnp.log(10.0 * noise[:1, :64]))
@@ -183,12 +182,11 @@
     left = jnp.concatenate(
         [jnp.where(masks, table[v : v + 1], 0.0) for v in range(9)], axis=0
     )
-    total = None
-    for part in parts_of(left):
-        piece = lax.dot_general(
-            part, cols, (((1,), (1,)), ((), ())), preferred_element_type=F32
-        )
-        total = piece if total is None else total + piece
+    stacked = jnp.concatenate(parts_of(left), axis=0)
+    pieces = lax.dot_general(
+        stacked, cols, (((1,), (1,)), ((), ())), preferred_element_type=F32
+    )
+    total = pieces[:144] + pieces[144:288] + pieces[288:]
     scale = scale_at(level[0], (16, 256))
     after = scale_at(level[0] - 1, (16, 256))
     square = scale * scale

time: 46.5 us -> 46.4 us (level)
  transfers between devices with their start and end apart: 6 -> 6, of which waited for: 1 -> 1; matrix products, arithmetic and copies ran while one was open for 0% -> 0% of each run, Pallas kernels for 7% -> 6%
where the time goes in v9:
time: 46.4 us; the launch traced here: 45.6 us
  starting transfers between devices  36.9 us (80%)
  Pallas kernels  7.49 us (16%)
  between operations  0.93 us (2%)
    ppermute x5, starting transfers between devices, swapped(): return lax.ppermute(value, axis, pairs)  28 us
    all_to_all x1, starting transfers between devices, local(): lax.all_to_all(slots, 'space', 0, 0, axis_index_groups=[order_of(slots.sh...  8.89 us
    pallas_call x1, Pallas kernels, outer(): pl.pallas_call(outer_body, out_shape=jax.ShapeDtypeStruct((8, 16, 256), F...  2.65 us
    pallas_call x1, Pallas kernels, inner(): pl.pallas_call(inner_body, out_shape=(jax.ShapeDtypeStruct((192, 240), BF...  2.43 us
    pallas_call x1, Pallas kernels, pack(): pl.pallas_call(pack_body, out_shape=(jax.ShapeDtypeStruct((16, 8, 256), B...  1.89 us
  transfers between devices with their start and end apart: 6, of which 1 were waited for; matrix products, arithmetic and copies ran while one was open for 0% of the time, Pallas kernels for 6%

profile of v9, /device:TPU:24, one launch (start us, length us, event | category | flops | bytes accessed | tf_op | source)
XLA Modules:
  0.0 45.6 jit_solution(4131026976389559633)
XLA Ops:
  0.7 1.9 %shard_map.136 = (bf16[16,8,256]{2,1,0:T(8,128)(2,1)}, f32[64,1,128]{2,1,0:T(1,128)}, f32[2,64,128]{2,1,0:T(8,128)}) custom-call(s32[1]{0:T(128)S(6)} %copy.18.level, f32[8,16,256]{2,1,0:T(8,128)} %bitcast.10, f32[4,2,128]{2,1,0:T(2,128)} %obs.1, f32[1,128]{1,0:T(1,128)} %bitcast.14, s32[1,128]{1,0:T(1,128)} %bitcast.15, s32[1,128]{1,0:T(1,128)} %bitcast.16, ...), custom_call_target="tpu_custom_call" | custom-call | flops 50000000 | bytes 400000 | tf_op jit(solution)/shard_map/pallas_call | solution.py:91
  2.5 0.0 copy-start
  2.5 2.8 %collective-permute-start = (bf16[16,8,256]{2,1,0:T(8,128)(2,1)}, bf16[16,8,256]{2,1,0:T(8,128)(2,1)S(1)}, u32[]{:S(2)}, u32[]{:S(2)}) collective-permute-start(bf16[16,8,256]{2,1,0:T(8,128)(2,1)} %get-tuple-element.19.own), channel_id=1, source_target_pairs={{0,64},{64,0},{128,192},{192,128},{1,65},{65,1},{129,193},{193,129... | collective-permute-start | bytes 196616 | tf_op jit(solution)/shard_map/ppermute | solution.py:450
  5.3 13.4 %collective-permute-start.1 = (bf16[16,8,256]{2,1,0:T(8,128)(2,1)}, bf16[16,8,256]{2,1,0:T(8,128)(2,1)S(1)}, u32[]{:S(2)}, u32[]{:S(2)}) collective-permute-start(bf16[16,8,256]{2,1,0:T(8,128)(2,1)} %get-tuple-element.19.own), channel_id=1, source_target_pairs={{64,128},{128,64},{192,256},{256,192},{320,384},{384,320},{65,129}... | collective-permute-start | bytes 196616 | tf_op jit(solution)/shard_map/ppermute | solution.py:450
  18.7 0.7 %collective-permute-start.2 = (bf16[16,8,256]{2,1,0:T(8,128)(2,1)}, bf16[16,8,256]{2,1,0:T(8,128)(2,1)S(1)}, u32[]{:S(2)}, u32[]{:S(2)}) collective-permute-start(bf16[16,8,256]{2,1,0:T(8,128)(2,1)} %get-tuple-element.19.own), channel_id=1, source_target_pairs={{256,320},{320,256},{384,448},{448,384},{257,321},{321,257},{385,4... | collective-permute-start | bytes 196616 | tf_op jit(solution)/shard_map/ppermute | solution.py:450
  19.4 8.9 %all-to-all-start = ((f32[64,1,128]{2,1,0:T(1,128)}), f32[64,1,128]{2,1,0:T(1,128)S(1)}, u32[]{:S(2)}, u32[]{:S(2)}) async-start(f32[64,1,128]{2,1,0:T(1,128)} %get-tuple-element.30), calls=%async_computation | async-start | bytes 65536 | tf_op jit(solution)/shard_map/all_to_all | solution.py:486
  28.3 0.0 copy-done
  28.3 0.0 collective-permute-done.low
  28.4 0.0 collective-permute-done.1.t2
  28.4 0.0 collective-permute-done.2.high
  28.4 0.0 copy-start.7
  28.4 0.0 copy-start.3
  28.4 0.0 copy-start.4
  28.4 0.0 copy-start.5
  28.5 0.0 copy-start.6
  28.5 9.3 %collective-permute-start.3 = (bf16[4,32,256]{2,1,0:T(8,128)(2,1)S(1)}, bf16[4,32,256]{2,1,0:T(8,128)(2,1)S(1)}, u32[]{:S(2)}, u32[]{:S(2)}) collective-permute-start(bf16[4,32,256]{2,1,0:T(8,128)(2,1)S(1)} %get-tuple-element.33), channel_id=1, source_target_pairs={{1,2},{2,1},{3,4},{4,3},{5,6},{6,5},{7,8},{8,7},{9,10},{10,9},{11,... | collective-permute-start | bytes 196616 | tf_op jit(solution)/shard_map/ppermute | solution.py:450
  37.8 1.9 %collective-permute-start.4 = (bf16[4,32,256]{2,1,0:T(8,128)(2,1)S(1)}, bf16[4,32,256]{2,1,0:T(8,128)(2,1)S(1)}, u32[]{:S(2)}, u32[]{:S(2)}) collective-permute-start(bf16[4,32,256]{2,1,0:T(8,128)(2,1)S(1)} %get-tuple-element.34), channel_id=1, source_target_pairs={{0,1},{1,0},{2,3},{3,2},{4,5},{5,4},{6,7},{7,6},{8,9},{9,8},{10,11... | collective-permute-start | bytes 196616 | tf_op jit(solution)/shard_map/ppermute | solution.py:450
  39.7 0.0 copy-done.7
  39.7 0.0 copy-done.3
  39.7 0.0 copy-done.4
  39.7 0.0 copy-done.5
  39.7 0.0 copy-done.6
  39.7 0.0 copy-start.1
  39.8 0.0 copy-start.2
  39.8 2.4 %shard_map.137 = (bf16[192,240]{1,0:T(8,128)(2,1)S(1)}, bf16[192,192]{1,0:T(8,128)(2,1)S(1)}, bf16[192,192]{1,0:T(8,128)(2,1)S(1)}, bf16[96,768]{1,0:T(8,128)(2,...) custom-call(s32[1]{0:T(128)S(6)} %copy.18.level, ...), custom_call_target="tpu_custom_call" | custom-call | flops 8000000000 | bytes 1000000 | tf_op jit(solution)/shard_map/pallas_call | solution.py:316
  42.2 0.0 all-to-all-done.got
  42.2 0.0 copy-done.1
  42.2 0.0 copy-done.2
  42.2 0.5 %shard_map.138 = (f32[8,16,256]{2,1,0:T(8,128)S(1)}, f32[16,256]{1,0:T(8,128)S(1)}) custom-call(s32[1]{0:T(128)S(6)} %copy.18.level, f32[8,16,256]{2,1,0:T(8,128)S(1)} %bitcast.11, f32[8,16,256]{2,1,0:T(8,128)S(1)} %bitcast.12, f32[64,1,128]{2,1,0:T(1,128)S(1)} %all-to-all-done.got), custom_call_target="tpu_custom_call" | custom-call | flops 400000000 | bytes 400000 | tf_op jit(solution)/shard_map/pallas_call | solution.py:200
  42.8 0.2 collective-permute-done.3
  42.9 0.0 collective-permute-done.4
  42.9 2.7 %shard_map.139 = f32[8,16,256]{2,1,0:T(8,128)} custom-call(bf16[8,32,256]{2,1,0:T(8,128)(2,1)S(1)} %pad_maximum_fusion.edges, bf16[192,240]{1,0:T(8,128)(2,1)S(1)} %get-tuple-element.21.w1, bf16[192,192]{1,0:T(8,128)(2,1)S(1)} %get-tuple-element.22.wm, bf16[192,192]{1,0:T(8,128)(2,1)S(1)} %get-tuple-element.23.wr, bf16[96,768]{1,0:T(8,128)(2,1)S(1)} %get-tuple-element.24.wo, ...), custom_call_target="tpu_custom_call" | custom-call | flops 4000000000 | bytes 1000000 | tf_op jit(solution)/shard_map/pallas_call | solution.py:420
  (6 shorter events, 0.1 us)
Async XLA Ops:
  2.5 25.8 %copy-start = (bf16[16,8,256]{2,1,0:T(8,128)(2,1)S(1)}, bf16[16,8,256]{2,1,0:T(8,128)(2,1)}, u32[]{:S(2)}) copy-start(bf16[16,8,256]{2,1,0:T(8,128)(2,1)} %get-tuple-element.19.own) | copy-start | bytes 196612
  2.5 25.8 %collective-permute-start = (bf16[16,8,256]{2,1,0:T(8,128)(2,1)}, bf16[16,8,256]{2,1,0:T(8,128)(2,1)S(1)}, u32[]{:S(2)}, u32[]{:S(2)}) collective-permute-start(bf16[16,8,256]{2,1,0:T(8,128)(2,1)} %get-tuple-element.19.own), channel_id=1, source_target_pairs={{0,64},{64,0},{128,192},{192,128},{1,65},{65,1},{129,193},{193,129... | collective-permute-start | bytes 196616 | tf_op jit(solution)/shard_map/ppermute | solution.py:450
  5.3 23.0 %collective-permute-start.1 = (bf16[16,8,256]{2,1,0:T(8,128)(2,1)}, bf16[16,8,256]{2,1,0:T(8,128)(2,1)S(1)}, u32[]{:S(2)}, u32[]{:S(2)}) collective-permute-start(bf16[16,8,256]{2,1,0:T(8,128)(2,1)} %get-tuple-element.19.own), channel_id=1, source_target_pairs={{64,128},{128,64},{192,256},{256,192},{320,384},{384,320},{65,129}... | collective-permute-start | bytes 196616 | tf_op jit(solution)/shard_map/ppermute | solution.py:450
  18.7 9.7 %collective-permute-start.2 = (bf16[16,8,256]{2,1,0:T(8,128)(2,1)}, bf16[16,8,256]{2,1,0:T(8,128)(2,1)S(1)}, u32[]{:S(2)}, u32[]{:S(2)}) collective-permute-start(bf16[16,8,256]{2,1,0:T(8,128)(2,1)} %get-tuple-element.19.own), channel_id=1, source_target_pairs={{256,320},{320,256},{384,448},{448,384},{257,321},{321,257},{385,4... | collective-permute-start | bytes 196616 | tf_op jit(solution)/shard_map/ppermute | solution.py:450
  19.4 22.8 %all-to-all-start = ((f32[64,1,128]{2,1,0:T(1,128)}), f32[64,1,128]{2,1,0:T(1,128)S(1)}, u32[]{:S(2)}, u32[]{:S(2)}) async-start(f32[64,1,128]{2,1,0:T(1,128)} %get-tuple-element.30), calls=%async_computation | async-start | bytes 65536 | tf_op jit(solution)/shard_map/all_to_all | solution.py:486
  28.4 11.3 %copy-start.7 = (f32[2,64,128]{2,1,0:T(8,128)S(1)}, f32[2,64,128]{2,1,0:T(8,128)}, u32[]{:S(2)}) copy-start(f32[2,64,128]{2,1,0:T(8,128)} %get-tuple-element.20.columns) | copy-start | bytes 196612
  28.4 11.3 %copy-start.3 = (bf16[3,64,192]{2,1,0:T(8,128)(2,1)S(1)}, bf16[3,64,192]{2,1,0:T(8,128)(2,1)}, u32[]{:S(2)}) copy-start(bf16[3,64,192]{2,1,0:T(8,128)(2,1)} %conv_mid.1) | copy-start | bytes 221188
  28.4 11.3 %copy-start.4 = (bf16[3,64,192]{2,1,0:T(8,128)(2,1)S(1)}, bf16[3,64,192]{2,1,0:T(8,128)(2,1)}, u32[]{:S(2)}) copy-start(bf16[3,64,192]{2,1,0:T(8,128)(2,1)} %conv_res.1) | copy-start | bytes 221188
  28.4 11.3 %copy-start.5 = (bf16[3,64,48]{1,2,0:T(8,128)(2,1)S(1)}, bf16[3,64,48]{1,2,0:T(8,128)(2,1)}, u32[]{:S(2)}) copy-start(bf16[3,64,48]{1,2,0:T(8,128)(2,1)} %param.21) | copy-start | bytes 55300
  28.5 11.3 %copy-start.6 = (bf16[3,16,192]{2,1,0:T(8,128)(2,1)S(1)}, bf16[3,16,192]{2,1,0:T(8,128)(2,1)}, u32[]{:S(2)}) copy-start(bf16[3,16,192]{2,1,0:T(8,128)(2,1)} %conv_out.1) | copy-start | bytes 55300
  28.5 14.4 %collective-permute-start.3 = (bf16[4,32,256]{2,1,0:T(8,128)(2,1)S(1)}, bf16[4,32,256]{2,1,0:T(8,128)(2,1)S(1)}, u32[]{:S(2)}, u32[]{:S(2)}) collective-permute-start(bf16[4,32,256]{2,1,0:T(8,128)(2,1)S(1)} %get-tuple-element.33), channel_id=1, source_target_pairs={{1,2},{2,1},{3,4},{4,3},{5,6},{6,5},{7,8},{8,7},{9,10},{10,9},{11,... | collective-permute-start | bytes 196616 | tf_op jit(solution)/shard_map/ppermute | solution.py:450
  37.8 5.2 %collective-permute-start.4 = (bf16[4,32,256]{2,1,0:T(8,128)(2,1)S(1)}, bf16[4,32,256]{2,1,0:T(8,128)(2,1)S(1)}, u32[]{:S(2)}, u32[]{:S(2)}) collective-permute-start(bf16[4,32,256]{2,1,0:T(8,128)(2,1)S(1)} %get-tuple-element.34), channel_id=1, source_target_pairs={{0,1},{1,0},{2,3},{3,2},{4,5},{5,4},{6,7},{7,6},{8,9},{9,8},{10,11... | collective-permute-start | bytes 196616 | tf_op jit(solution)/shard_map/ppermute | solution.py:450
  39.7 2.5 %copy-start.1 = (f32[4,2,16,256]{3,2,1,0:T(8,128)S(1)}, f32[4,2,16,256]{3,2,1,0:T(8,128)}, u32[]{:S(2)}) copy-start(f32[4,2,16,256]{3,2,1,0:T(8,128)} %param.14) | copy-start | bytes 393220
  39.8 2.5 %copy-start.2 = (f32[4,2,16,256]{3,2,1,0:T(8,128)S(1)}, f32[4,2,16,256]{3,2,1,0:T(8,128)}, u32[]{:S(2)}) copy-start(f32[4,2,16,256]{3,2,1,0:T(8,128)} %param.15) | copy-start | bytes 393220
